TPU v7x, 32 devices: a whole 2x2x4 slice. The times are simulated.
32 devices in a mesh: dp: 8 (over z, y), tensor: 4 (over x, core).
Axes of the slice: x: 2, y: 2, z: 4, core: 2. Of those that a mesh axis runs over, the one named last changes fastest.
Arguments:
- tokens: bfloat16 [16, 1024, 1536], P('dp', 'tensor'), may hold values from -6 to 6
- context: bfloat16 [16, 130, 768], P('dp'), may hold values from -6 to 6
- positions: int32 [16, 1024], P('dp'), may hold values from 0 to 4095
- seq_mask: int32 [16], P('dp'), may hold values 0 or 1
- cotangent: bfloat16 [16, 1024, 1536], P('dp', 'tensor'), may hold values from -6 to 6
- norm_gains: float32 [3, 1536], P(None, ('dp', 'tensor')), may hold values from 0.25 to 1.75
- norm_shifts: float32 [3, 1536], P(None, ('dp', 'tensor')), may hold values from -3 to 3
- w_qkv: bfloat16 [3, 1536, 1536], P(None, 'dp', 'tensor'), may hold values from -0.15625 to 0.15625
- w_self_out: bfloat16 [1536, 1536], P('tensor', 'dp'), may hold values from -2.5 to 2.5
- w_cross_q: bfloat16 [1536, 1536], P('dp', 'tensor'), may hold values from -0.15625 to 0.15625
- w_cross_kv: bfloat16 [2, 768, 1536], P(None, 'dp', 'tensor'), may hold values from -0.21875 to 0.21875
- w_cross_out: bfloat16 [1536, 1536], P('tensor', 'dp'), may hold values from -0.875 to 0.875
- w_gate_up: bfloat16 [2, 1536, 6144], P(None, 'dp', 'tensor'), may hold values from -0.15625 to 0.15625
- w_down: bfloat16 [6144, 1536], P('tensor', 'dp'), may hold values from -0.15625 to 0.15625
Outputs:
- out: bfloat16 [16, 1024, 1536], P('dp', 'tensor')
- grad_input: float32 [16, 1024, 1536], P('dp', 'tensor')
- grad_norm_gains: float32 [3, 1536], P(None, ('dp', 'tensor'))
- grad_norm_shifts: float32 [3, 1536], P(None, ('dp', 'tensor'))
- grad_qkv: float32 [3, 1536, 1536], P(None, 'dp', 'tensor')
- grad_self_out: float32 [1536, 1536], P('tensor', 'dp')
- grad_cross_q: float32 [1536, 1536], P('dp', 'tensor')
- grad_cross_kv: float32 [2, 768, 1536], P(None, 'dp', 'tensor')
- grad_cross_out: float32 [1536, 1536], P('tensor', 'dp')
- grad_gate_up: float32 [2, 1536, 6144], P(None, 'dp', 'tensor')
- grad_down: float32 [6144, 1536], P('tensor', 'dp')
Inputs may be any that keep to these rules, and one draw needn't show every extreme that they name: `seq_mask`: 1 marks a sequence slot that holds data, 0 an empty slot.
All inputs are finite; a program needn't handle non-finite values. No bound on the sum of `seq_mask` on one device may be relied on, other than what follows from the above.
Results may differ from a plain program's by a relative error of at most 0.02.
Values may be sent and summed in bfloat16 or wider, within the bound.
No kernel may reach another device: no remote copies, remote signals or barrier semaphores. Data moves between devices by JAX's collectives and lax.ppermute only.
A program may use at most 256 MiB of HBM per device.

v0:
```python
import math

import jax
import jax.numpy as jnp
from jax import lax
from jax.sharding import PartitionSpec as P

HEAD_WIDTH = 64
ROT = 32


EPS = 1e-05


def tables(pos_row):
    half_rot = ROT // 2
    inverse = jnp.exp(jnp.arange(half_rot, dtype=jnp.float32) * (-2.0 * math.log(10000.0) / ROT))
    angles = pos_row.astype(jnp.float32)[:, None] * inverse[None, :]
    return (jnp.cos(angles), jnp.sin(angles))


def rotate(input_values, cosine, sine_table):
    half_rot = cosine.shape[-1]
    first_half = input_values[..., :half_rot]
    second_half = input_values[..., half_rot : 2 * half_rot]
    rest_dims = input_values[..., 2 * half_rot :]
    cos_b = cosine[:, None, :]
    sin_b = sine_table[:, None, :]
    return jnp.concatenate(
        [
            first_half * cos_b - second_half * sin_b,
            second_half * cos_b + first_half * sin_b,
            rest_dims,
        ],
        axis=-1,
    )


def unrotate(grad_out, cosine, sine_table):
    half_rot = cosine.shape[-1]
    first_half = grad_out[..., :half_rot]
    second_half = grad_out[..., half_rot : 2 * half_rot]
    rest_dims = grad_out[..., 2 * half_rot :]
    cos_b = cosine[:, None, :]
    sin_b = sine_table[:, None, :]
    return jnp.concatenate(
        [
            first_half * cos_b + second_half * sin_b,
            second_half * cos_b - first_half * sin_b,
            rest_dims,
        ],
        axis=-1,
    )


def layer_normalize(token_rows, gain_row, shift_row):
    mean_row = jnp.mean(token_rows, axis=-1, keepdims=True)
    centred = token_rows - mean_row
    inv_std = lax.rsqrt(jnp.mean(centred * centred, axis=-1, keepdims=True) + EPS)
    normed = centred * inv_std
    return (normed * gain_row + shift_row, normed, inv_std)


def norm_pullback(grad_out, normed, inv_std, gain_row):
    scaled = grad_out * gain_row
    back_rows = inv_std * (
        scaled
        - jnp.mean(scaled, axis=-1, keepdims=True)
        - normed * jnp.mean(scaled * normed, axis=-1, keepdims=True)
    )
    return (back_rows, jnp.sum(grad_out * normed, axis=0), jnp.sum(grad_out, axis=0))


def attend_forward(queries, input_keys, input_values):
    length, head_count, head_size = queries.shape
    block_rows = min(512, length)
    scaling = head_size ** (-0.5)
    blocks = queries.reshape(length // block_rows, block_rows, head_count, head_size)

    def per_block(query_block):
        attention_logits = (
            jnp.einsum("ioc,soc->ois", query_block, input_keys, preferred_element_type=jnp.float32)
            * scaling
        )
        row_peak = jnp.max(attention_logits, axis=-1, keepdims=True)
        weighed = jnp.exp(attention_logits - row_peak)
        row_total = jnp.sum(weighed, axis=-1, keepdims=True)
        reduced_weights = (weighed / row_total).astype(jnp.bfloat16)
        result = jnp.einsum(
            "roe,erg->org", reduced_weights, input_values, preferred_element_type=jnp.float32
        )
        return (result, (row_peak + jnp.log(row_total))[..., 0])

    results, log_sums = lax.map(per_block, blocks)
    return (results.reshape(length, head_count * head_size), log_sums)


def attend_backward(queries, input_keys, input_values, grad_out, log_sums):
    length, head_count, head_size = queries.shape
    block_rows = min(512, length)
    scaling = head_size ** (-0.5)
    blocks = queries.reshape(length // block_rows, block_rows, head_count, head_size)
    grad_blocks = grad_out.reshape(length // block_rows, block_rows, head_count, head_size)

    def per_block(carry, item_args):
        grad_keys, grad_values = carry
        query_block, gradient_block, lse_block = item_args
        attention_logits = (
            jnp.einsum("ioc,soc->ois", query_block, input_keys, preferred_element_type=jnp.float32)
            * scaling
        )
        attention_weights = jnp.exp(attention_logits - lse_block[..., None])
        grad_values = grad_values + jnp.einsum(
            "lup,ulk->plk",
            attention_weights.astype(jnp.bfloat16),
            gradient_block,
            preferred_element_type=jnp.float32,
        )
        grad_probs = jnp.einsum(
            "ioc,soc->ois", gradient_block, input_values, preferred_element_type=jnp.float32
        )
        row_delta = jnp.sum(attention_weights * grad_probs, axis=-1, keepdims=True)
        gradient_logits = (attention_weights * (grad_probs - row_delta)).astype(jnp.bfloat16)
        grad_q = (
            jnp.einsum(
                "roe,erg->org", gradient_logits, input_keys, preferred_element_type=jnp.float32
            )
            * scaling
        )
        grad_keys = (
            grad_keys
            + jnp.einsum(
                "lup,ulk->plk", gradient_logits, query_block, preferred_element_type=jnp.float32
            )
            * scaling
        )
        return ((grad_keys, grad_values), grad_q)

    start_keys = jnp.zeros(input_keys.shape, jnp.float32)
    start_values = jnp.zeros(input_values.shape, jnp.float32)
    (grad_keys, grad_values), grad_q = lax.scan(
        per_block, (start_keys, start_values), (blocks, grad_blocks, log_sums)
    )
    return (grad_q.reshape(length, head_count, head_size), grad_keys, grad_values)


def body(
    tokens,
    context,
    positions,
    seq_mask,
    cotangent,
    norm_gains,
    norm_shifts,
    w_qkv,
    w_self_out,
    w_cross_q,
    w_cross_kv,
    w_cross_out,
    w_gate_up,
    w_down,
):
    complete_gain, complete_shift = (
        lax.all_gather(norm_gains, ("dp", "tensor"), axis=1, tiled=True),
        lax.all_gather(norm_shifts, ("dp", "tensor"), axis=1, tiled=True),
    )

    def fetch_weights():
        return (
            lax.all_gather(w_qkv, "dp", axis=1, tiled=True),
            lax.all_gather(w_self_out, "dp", axis=1, tiled=True),
            lax.all_gather(w_cross_q, "dp", axis=0, tiled=True),
            lax.all_gather(w_cross_kv, "dp", axis=1, tiled=True),
            lax.all_gather(w_cross_out, "dp", axis=1, tiled=True),
            lax.all_gather(w_gate_up, "dp", axis=1, tiled=True),
            lax.all_gather(w_down, "dp", axis=1, tiled=True),
        )

    def full_rows(part_rows):
        return lax.all_gather(part_rows, "tensor", axis=0, tiled=True)

    def share_rows(term_rows):
        return lax.psum_scatter(term_rows, "tensor", scatter_dimension=0, tiled=True)

    def full_grads(part_rows):
        return lax.all_gather(part_rows, "tensor", axis=0, tiled=True)

    def share_grads(term_rows):
        return lax.psum_scatter(term_rows, "tensor", scatter_dimension=0, tiled=True)

    outputs = []
    grad_inputs = []
    totals = None
    norm_totals = None
    length = positions.shape[1]
    ctx_len = context.shape[1]
    for micro_step in range(tokens.shape[0]):
        gathered = fetch_weights()
        wqkv_full, wso_full, wcq_full, wckv_full, wco_full, wgu_full, wdn_full = gathered
        head_count = wqkv_full.shape[2] // HEAD_WIDTH
        keep_scale = seq_mask[micro_step].astype(jnp.float32)
        token_rows = tokens[micro_step].astype(jnp.float32)
        cond_rows = context[micro_step]
        cosine, sine_table = tables(positions[micro_step])
        first_normalized, first_standardized, first_reciprocal = layer_normalize(
            token_rows, complete_gain[0], complete_shift[0]
        )
        rows_one = full_rows(first_normalized.astype(jnp.bfloat16))
        projected = jnp.einsum(
            "ld,kdh->klh", rows_one, wqkv_full, preferred_element_type=jnp.float32
        )
        queries = rotate(
            projected[0].reshape(length, head_count, HEAD_WIDTH), cosine, sine_table
        ).astype(jnp.bfloat16)
        keys_rot = rotate(
            projected[1].reshape(length, head_count, HEAD_WIDTH), cosine, sine_table
        ).astype(jnp.bfloat16)
        values_low = projected[2].reshape(length, head_count, HEAD_WIDTH).astype(jnp.bfloat16)
        attended, lse_self = attend_forward(queries, keys_rot, values_low)
        attended = attended.astype(jnp.bfloat16)
        leading_sum = token_rows + share_rows(
            jnp.dot(attended, wso_full, preferred_element_type=jnp.float32)
        )
        second_normalized, second_standardized, second_reciprocal = layer_normalize(
            leading_sum, complete_gain[1], complete_shift[1]
        )
        rows_two = full_rows(second_normalized.astype(jnp.bfloat16))
        cross_q = jnp.dot(rows_two, wcq_full, preferred_element_type=jnp.float32).astype(
            jnp.bfloat16
        )
        cross_q = cross_q.reshape(length, head_count, HEAD_WIDTH)
        cross_kv = jnp.einsum(
            "cd,kdh->kch", cond_rows, wckv_full, preferred_element_type=jnp.float32
        ).astype(jnp.bfloat16)
        cross_k = cross_kv[0].reshape(ctx_len, head_count, HEAD_WIDTH)
        cross_v = cross_kv[1].reshape(ctx_len, head_count, HEAD_WIDTH)
        crossed, lse_cross = attend_forward(cross_q, cross_k, cross_v)
        crossed = crossed.astype(jnp.bfloat16)
        trailing_sum = leading_sum + share_rows(
            jnp.dot(crossed, wco_full, preferred_element_type=jnp.float32)
        )
        third_normalized, third_standardized, third_reciprocal = layer_normalize(
            trailing_sum, complete_gain[2], complete_shift[2]
        )
        rows_three = full_rows(third_normalized.astype(jnp.bfloat16))
        gate_up = jnp.einsum(
            "ld,kdf->klf", rows_three, wgu_full, preferred_element_type=jnp.float32
        )
        gate_pre = gate_up[0]
        up_pre = gate_up[1]
        gate_sig = jax.nn.sigmoid(gate_pre)
        gate_act = gate_pre * gate_sig
        hidden = (gate_act * up_pre).astype(jnp.bfloat16)
        third_sum = trailing_sum + share_rows(
            jnp.dot(hidden, wdn_full, preferred_element_type=jnp.float32)
        )
        outputs.append((third_sum * keep_scale).astype(jnp.bfloat16))
        gathered = fetch_weights()
        wqkv_full, wso_full, wcq_full, wckv_full, wco_full, wgu_full, wdn_full = gathered
        grad_third = cotangent[micro_step].astype(jnp.float32) * keep_scale
        grad_full = full_grads(grad_third.astype(jnp.bfloat16))
        grad_dn = jnp.einsum("lf,ld->fd", hidden, grad_full, preferred_element_type=jnp.float32)
        grad_hidden = jnp.einsum(
            "ld,fd->lf", grad_full, wdn_full, preferred_element_type=jnp.float32
        )
        grad_gate = grad_hidden * up_pre * gate_sig * (1.0 + gate_pre * (1.0 - gate_sig))
        grad_up = grad_hidden * gate_act
        grad_gu_rows = jnp.stack([grad_gate, grad_up]).astype(jnp.bfloat16)
        grad_gu = jnp.einsum(
            "ld,klf->kdf", rows_three, grad_gu_rows, preferred_element_type=jnp.float32
        )
        gradient_normalized3 = share_grads(
            jnp.einsum("klf,kdf->ld", grad_gu_rows, wgu_full, preferred_element_type=jnp.float32)
        )
        back_three, gain_three, shift_three = norm_pullback(
            gradient_normalized3, third_standardized, third_reciprocal, complete_gain[2]
        )
        grad_second = grad_third + back_three
        grad_full = full_grads(grad_second.astype(jnp.bfloat16))
        grad_co = jnp.einsum("lh,ld->hd", crossed, grad_full, preferred_element_type=jnp.float32)
        grad_crossed = jnp.einsum(
            "ld,hd->lh", grad_full, wco_full, preferred_element_type=jnp.float32
        ).astype(jnp.bfloat16)
        grad_cq, grad_ck, grad_cv = attend_backward(
            cross_q, cross_k, cross_v, grad_crossed, lse_cross
        )
        grad_cq = grad_cq.reshape(length, -1).astype(jnp.bfloat16)
        grad_ckv_rows = jnp.stack(
            [grad_ck.reshape(ctx_len, -1), grad_cv.reshape(ctx_len, -1)]
        ).astype(jnp.bfloat16)
        grad_cq_weight = jnp.einsum(
            "ld,lh->dh", rows_two, grad_cq, preferred_element_type=jnp.float32
        )
        grad_ckv = jnp.einsum(
            "cd,kch->kdh", cond_rows, grad_ckv_rows, preferred_element_type=jnp.float32
        )
        gradient_normalized2 = share_grads(
            jnp.einsum("lh,dh->ld", grad_cq, wcq_full, preferred_element_type=jnp.float32)
        )
        second_pullback, second_gain, second_offset_shift = norm_pullback(
            gradient_normalized2, second_standardized, second_reciprocal, complete_gain[1]
        )
        grad_first = grad_second + second_pullback
        grad_full = full_grads(grad_first.astype(jnp.bfloat16))
        grad_so = jnp.einsum("lh,ld->hd", attended, grad_full, preferred_element_type=jnp.float32)
        grad_attended = jnp.einsum(
            "ld,hd->lh", grad_full, wso_full, preferred_element_type=jnp.float32
        ).astype(jnp.bfloat16)
        grad_q, grad_k, grad_v = attend_backward(
            queries, keys_rot, values_low, grad_attended, lse_self
        )
        grad_qkv_rows = jnp.stack(
            [
                unrotate(grad_q, cosine, sine_table).reshape(length, -1),
                unrotate(grad_k, cosine, sine_table).reshape(length, -1),
                grad_v.reshape(length, -1),
            ]
        ).astype(jnp.bfloat16)
        grad_qkv = jnp.einsum(
            "ld,klh->kdh", rows_one, grad_qkv_rows, preferred_element_type=jnp.float32
        )
        gradient_normalized1 = share_grads(
            jnp.einsum("klh,kdh->ld", grad_qkv_rows, wqkv_full, preferred_element_type=jnp.float32)
        )
        first_pullback, first_gain, first_offset_shift = norm_pullback(
            gradient_normalized1, first_standardized, first_reciprocal, complete_gain[0]
        )
        grad_inputs.append(grad_first + first_pullback)
        step_grads = (grad_qkv, grad_so, grad_cq_weight, grad_ckv, grad_co, grad_gu, grad_dn)
        step_norms = (
            jnp.stack([first_gain, second_gain, gain_three]),
            jnp.stack([first_offset_shift, second_offset_shift, shift_three]),
        )
        if totals is None:
            totals = step_grads
            norm_totals = step_norms
        else:
            totals = tuple((old_sum + new_term for old_sum, new_term in zip(totals, step_grads)))
            norm_totals = tuple(
                (old_sum + new_term for old_sum, new_term in zip(norm_totals, step_norms))
            )
    qkv_part, so_part, cq_part, ckv_part, co_part, gu_part, dn_part = (
        lax.psum_scatter(
            totals[0].astype(jnp.bfloat16), "dp", scatter_dimension=1, tiled=True
        ).astype(jnp.float32),
        lax.psum_scatter(
            totals[1].astype(jnp.bfloat16), "dp", scatter_dimension=1, tiled=True
        ).astype(jnp.float32),
        lax.psum_scatter(
            totals[2].astype(jnp.bfloat16), "dp", scatter_dimension=0, tiled=True
        ).astype(jnp.float32),
        lax.psum_scatter(
            totals[3].astype(jnp.bfloat16), "dp", scatter_dimension=1, tiled=True
        ).astype(jnp.float32),
        lax.psum_scatter(
            totals[4].astype(jnp.bfloat16), "dp", scatter_dimension=1, tiled=True
        ).astype(jnp.float32),
        lax.psum_scatter(
            totals[5].astype(jnp.bfloat16), "dp", scatter_dimension=1, tiled=True
        ).astype(jnp.float32),
        lax.psum_scatter(
            totals[6].astype(jnp.bfloat16), "dp", scatter_dimension=1, tiled=True
        ).astype(jnp.float32),
    )
    gain_part, shift_part = (
        lax.psum_scatter(norm_totals[0], ("dp", "tensor"), scatter_dimension=1, tiled=True),
        lax.psum_scatter(norm_totals[1], ("dp", "tensor"), scatter_dimension=1, tiled=True),
    )
    return (
        jnp.stack(outputs),
        jnp.stack(grad_inputs),
        gain_part,
        shift_part,
        qkv_part,
        so_part,
        cq_part,
        ckv_part,
        co_part,
        gu_part,
        dn_part,
    )


def solution(mesh):
    in_specs = (
        P("dp", "tensor", None),
        P("dp", None, None),
        P("dp", None),
        P("dp"),
        P("dp", "tensor", None),
        P(None, ("dp", "tensor")),
        P(None, ("dp", "tensor")),
        P(None, "dp", "tensor"),
        P("tensor", "dp"),
        P("dp", "tensor"),
        P(None, "dp", "tensor"),
        P("tensor", "dp"),
        P(None, "dp", "tensor"),
        P("tensor", "dp"),
    )
    out_specs = (
        P("dp", "tensor", None),
        P("dp", "tensor", None),
        P(None, ("dp", "tensor")),
        P(None, ("dp", "tensor")),
        P(None, "dp", "tensor"),
        P("tensor", "dp"),
        P("dp", "tensor"),
        P(None, "dp", "tensor"),
        P("tensor", "dp"),
        P(None, "dp", "tensor"),
        P("tensor", "dp"),
    )
    return jax.shard_map(body, mesh=mesh, in_specs=in_specs, out_specs=out_specs, check_vma=False)
```

profile of v0, /device:TPU:0, one launch (start us, length us, event | category | flops | bytes accessed | tf_op | source)
XLA Modules:
  0.0 2570.3 jit_solution(8005028343715594689)
XLA Ops:
  9.7 43.4 %all-gather = f32[32,48,3]{1,2,0:T(4,128)S(1)} all-gather(f32[1,48,3]{1,2,0:T(4,128)S(1)} %bitcast.747), channel_id=1, replica_groups=mesh['dp'=8,'tensor'=4] {'dp','tensor'}, dimensions={0}, use_global_device_ids=true | all-gather | bytes 19008 | tf_op jit(solution)/shard_map/all_gather | solution.py:164
  53.8 36.8 %all-gather.1 = f32[32,48,3]{1,2,0:T(4,128)S(1)} all-gather(f32[1,48,3]{1,2,0:T(4,128)S(1)} %bitcast.748), channel_id=1, replica_groups=mesh['dp'=8,'tensor'=4] {'dp','tensor'}, dimensions={0}, use_global_device_ids=true | all-gather | bytes 19008 | tf_op jit(solution)/shard_map/all_gather | solution.py:165
  96.1 23.2 all-gather.42.cloned.1.call-done
  119.3 67.4 %all-gather.24.cloned.1.call-done = bf16[3,1536,384]{2,1,0:T(8,128)(2,1)} async-done(((bf16[3,192,384]{2,1,0:T(8,128)(2,1)}), bf16[3,1536,384]{2,1,0:T(8,128)(2,1)}) %all-gather.24.cloned.1.call-update) | async-done | bytes 3538960 | tf_op jit(solution)/shard_map/all_gather | solution.py:170
  234.8 23.1 all-gather.22.cloned.1.call-done
  291.5 27.2 %reduce-scatter.32.cloned.1.call-done = f32[256,1536]{1,0:T(8,128)} async-done(((f32[1024,1536]{1,0:T(8,128)}), f32[256,1536]{1,0:T(8,128)}) %reduce-scatter.32.cloned.1.call-update) | async-done | bytes 1572880 | tf_op jit(solution)/shard_map/reduce_scatter | solution.py:183
  318.7 61.0 %reduce-scatter.26.cloned.1.call-done = f32[256,1536]{1,0:T(8,128)} async-done(((f32[1024,1536]{1,0:T(8,128)}), f32[256,1536]{1,0:T(8,128)}) %reduce-scatter.26.cloned.1.call-update) | async-done | bytes 1572880 | tf_op jit(solution)/shard_map/reduce_scatter | solution.py:183
  387.7 35.3 %all-gather.32.cloned.1.call-done = bf16[2,768,384]{2,1,0:T(8,128)(2,1)} async-done(((bf16[2,96,384]{2,1,0:T(8,128)(2,1)}), bf16[2,768,384]{2,1,0:T(8,128)(2,1)}) %all-gather.32.cloned.1.call-update) | async-done | bytes 1179664 | tf_op jit(solution)/shard_map/all_gather | solution.py:173
  425.6 39.4 %all-gather.30.cloned.1.call-done = bf16[1536,384]{1,0:T(8,128)(2,1)} async-done(((bf16[192,384]{1,0:T(8,128)(2,1)}), bf16[1536,384]{1,0:T(8,128)(2,1)}) %all-gather.30.cloned.1.call-update) | async-done | bytes 1179664 | tf_op jit(solution)/shard_map/all_gather | solution.py:172
  465.1 29.5 %all-gather.44.cloned.1.call-done = bf16[1024,1536]{1,0:T(8,128)(2,1)} async-done(((bf16[256,1536]{1,0:T(8,128)(2,1)}), bf16[1024,1536]{1,0:T(8,128)(2,1)}) %all-gather.44.cloned.1.call-update) | async-done | bytes 3145744 | tf_op jit(solution)/shard_map/all_gather | solution.py:180
  504.9 32.7 %all-gather.34.cloned.1.call-done = bf16[384,1536]{0,1:T(8,128)(2,1)} async-done(((bf16[384,192]{0,1:T(8,128)(2,1)}), bf16[384,1536]{0,1:T(8,128)(2,1)}) %all-gather.34.cloned.1.call-update) | async-done | bytes 1179664 | tf_op jit(solution)/shard_map/all_gather | solution.py:174
  583.7 44.2 %reduce-scatter.34.cloned.1.call-done = f32[256,1536]{1,0:T(8,128)} async-done(((f32[1024,1536]{1,0:T(8,128)}), f32[256,1536]{1,0:T(8,128)}) %reduce-scatter.34.cloned.1.call-update) | async-done | bytes 1572880 | tf_op jit(solution)/shard_map/reduce_scatter | solution.py:183
  631.5 57.5 %reduce-scatter.28.cloned.1.call-done = f32[256,1536]{1,0:T(8,128)} async-done(((f32[1024,1536]{1,0:T(8,128)}), f32[256,1536]{1,0:T(8,128)}) %reduce-scatter.28.cloned.1.call-update) | async-done | bytes 1572880 | tf_op jit(solution)/shard_map/reduce_scatter | solution.py:183
  699.9 129.2 %all-gather.38.cloned.1.call-done = bf16[2,1536,1536]{2,1,0:T(8,128)(2,1)} async-done(((bf16[2,192,1536]{2,1,0:T(8,128)(2,1)}), bf16[2,1536,1536]{2,1,0:T(8,128)(2,1)}) %all-gather.38.cloned.1.call-update) | async-done | bytes 9437200 | tf_op jit(solution)/shard_map/all_gather | solution.py:175
  829.2 28.7 %all-gather.46.cloned.1.call-done = bf16[1024,1536]{1,0:T(8,128)(2,1)} async-done(((bf16[256,1536]{1,0:T(8,128)(2,1)}), bf16[1024,1536]{1,0:T(8,128)(2,1)}) %all-gather.46.cloned.1.call-update) | async-done | bytes 3145744 | tf_op jit(solution)/shard_map/all_gather | solution.py:180
  888.4 82.0 %all-gather.40.cloned.1.call-done = bf16[1536,1536]{0,1:T(8,128)(2,1)} async-done(((bf16[1536,192]{0,1:T(8,128)(2,1)}), bf16[1536,1536]{0,1:T(8,128)(2,1)}) %all-gather.40.cloned.1.call-update) | async-done | bytes 4718608 | tf_op jit(solution)/shard_map/all_gather | solution.py:176
  1090.6 61.1 %reduce-scatter.38.cloned.1.call-done = f32[256,1536]{1,0:T(8,128)} async-done(((f32[1024,1536]{1,0:T(8,128)}), f32[256,1536]{1,0:T(8,128)}) %reduce-scatter.38.cloned.1.call-update) | async-done | bytes 1572880 | tf_op jit(solution)/shard_map/reduce_scatter | solution.py:189
  1155.4 57.2 %reduce-scatter.36.cloned.1.call-done = f32[256,1536]{1,0:T(8,128)} async-done(((f32[1024,1536]{1,0:T(8,128)}), f32[256,1536]{1,0:T(8,128)}) %reduce-scatter.36.cloned.1.call-update) | async-done | bytes 1572880 | tf_op jit(solution)/shard_map/reduce_scatter | solution.py:183
  1212.6 61.1 %reduce-scatter.30.cloned.1.call-done = f32[256,1536]{1,0:T(8,128)} async-done(((f32[1024,1536]{1,0:T(8,128)}), f32[256,1536]{1,0:T(8,128)}) %reduce-scatter.30.cloned.1.call-update) | async-done | bytes 1572880 | tf_op jit(solution)/shard_map/reduce_scatter | solution.py:183
  1280.2 27.9 %all-gather.50.cloned.1.call-done = bf16[1024,1536]{1,0:T(8,128)(2,1)} async-done(((bf16[256,1536]{1,0:T(8,128)(2,1)}), bf16[1024,1536]{1,0:T(8,128)(2,1)}) %all-gather.50.cloned.1.call-update) | async-done | bytes 3145744 | tf_op jit(solution)/shard_map/all_gather | solution.py:186
  1368.0 31.5 %reduce-scatter.40.cloned.1.call-done = f32[256,1536]{1,0:T(8,128)} async-done(((f32[1024,1536]{1,0:T(8,128)}), f32[256,1536]{1,0:T(8,128)}) %reduce-scatter.40.cloned.1.call-update) | async-done | bytes 1572880 | tf_op jit(solution)/shard_map/reduce_scatter | solution.py:189
  1402.2 58.3 %reduce-scatter.46.cloned.1.call-done = f32[256,1536]{1,0:T(8,128)} async-done(((f32[1024,1536]{1,0:T(8,128)}), f32[256,1536]{1,0:T(8,128)}) %reduce-scatter.46.cloned.1.call-update) | async-done | bytes 1572880 | tf_op jit(solution)/shard_map/reduce_scatter | solution.py:189
  1534.4 24.2 copy.178
  1580.4 95.9 %while.113 = (s32[]{:T(128)}, f32[1024,6,64]{0,2,1:T(8,128)S(1)}, f32[1024,6,64]{0,2,1:T(8,128)}, f32[2,512,6,64]{1,0,3,2:T(2,128)}, bf16[2,512,6,64]{1,3,2,0:T(...) while((s32[]{:T(128)}, f32[1024,6,64]{0,2,1:T(8,128)S(1)}, ...), condition=%wide.region_45.46_spmd.clone, body=%wide.region_43.45_spmd.clone.sunk | while | flops 2053174272 | bytes 240740112 | solution.py:141
  1696.0 95.5 %while.115 = (s32[]{:T(128)}, f32[1024,6,64]{0,2,1:T(8,128)S(1)}, f32[1024,6,64]{0,2,1:T(8,128)}, f32[2,512,6,64]{1,0,3,2:T(2,128)}, bf16[2,512,6,64]{1,3,2,0:T(...) while((s32[]{:T(128)}, f32[1024,6,64]{0,2,1:T(8,128)S(1)}, ...), condition=%wide.region_60.61_spmd.clone, body=%wide.region_58.60_spmd.clone.sunk | while | flops 2053174272 | bytes 240740112 | solution.py:141
  1860.1 231.2 %all-reduce.5.cloned.1.call-done = (bf16[2,768,384]{2,0,1:T(2,128)(2,1)}, bf16[2,1536,1536]{2,0,1:T(2,128)(2,1)}) async-done(((bf16[2,768,384]{2,0,1:T(2,128)(2,1)}, bf16[2,1536,1536]{2,0,1:T(2,128)(2,1)}), (bf16[2,768,384]{2,0,1:T(2,128)(2,1)}, bf16[2,1536,1536]{2,0,1:T(2,128)(2,1)})) %all-reduce.5.cloned.1.call-update) | async-done | bytes 10616848
  2097.1 61.2 %reduce-scatter.50.cloned.1.call-done = bf16[384,192]{0,1:T(8,128)(2,1)} async-done(((bf16[384,1536]{0,1:T(8,128)(2,1)}), bf16[384,192]{0,1:T(8,128)(2,1)}) %reduce-scatter.50.cloned.1.call-update) | async-done | bytes 147472 | tf_op jit(solution)/shard_map/reduce_scatter | solution.py:346
  2159.9 80.1 %reduce-scatter.62.cloned.1.call-done = bf16[192,1152]{1,0:T(8,128)(2,1)} async-done(((bf16[1536,1152]{1,0:T(8,128)(2,1)}), bf16[192,1152]{1,0:T(8,128)(2,1)}) %reduce-scatter.62.cloned.1.call-update) | async-done | bytes 442384
  2243.3 57.2 %reduce-scatter.48.cloned.1.call-done = f32[256,1536]{1,0:T(8,128)} async-done(((f32[1024,1536]{1,0:T(8,128)}), f32[256,1536]{1,0:T(8,128)}) %reduce-scatter.48.cloned.1.call-update) | async-done | bytes 1572880 | tf_op jit(solution)/shard_map/reduce_scatter | solution.py:189
  2300.4 61.0 %reduce-scatter.42.cloned.1.call-done = f32[256,1536]{1,0:T(8,128)} async-done(((f32[1024,1536]{1,0:T(8,128)}), f32[256,1536]{1,0:T(8,128)}) %reduce-scatter.42.cloned.1.call-update) | async-done | bytes 1572880 | tf_op jit(solution)/shard_map/reduce_scatter | solution.py:189
  2372.0 90.0 %reduce-scatter.60.cloned.1.call-done = f32[48,3]{1,0:T(8,128)} async-done(((f32[1536,3]{1,0:T(8,128)}), f32[48,3]{1,0:T(8,128)}) %reduce-scatter.60.cloned.1.call-update) | async-done | bytes 592
  2463.4 98.2 %reduce-scatter.58.cloned.1.call-done = f32[48,3]{1,0:T(8,128)} async-done(((f32[1536,3]{1,0:T(8,128)}), f32[48,3]{1,0:T(8,128)}) %reduce-scatter.58.cloned.1.call-update) | async-done | bytes 592
  (735 shorter events, 860.8 us)
Async XLA Ops:
  94.6 163.3 %all-gather.22.cloned.1.call-start = ((), (), s32[]{:S(2)}) async-start(), calls=%async_computation.19 | async-start | bytes 3932160 | tf_op jit(solution)/shard_map/all_gather | solution.py:180
  95.2 223.5 %reduce-scatter.32.cloned.1.call-start = ((), (), s32[]{:S(2)}) async-start(), calls=%async_computation.33 | async-start | bytes 7864320 | tf_op jit(solution)/shard_map/reduce_scatter | solution.py:183
  234.5 145.2 %reduce-scatter.26.cloned.1.call-start = ((), (), s32[]{:S(2)}) async-start(), calls=%async_computation.22 | async-start | bytes 7864320 | tf_op jit(solution)/shard_map/reduce_scatter | solution.py:183
  290.2 174.8 %all-gather.30.cloned.1.call-start = ((), (), s32[]{:S(2)}) async-start(), calls=%async_computation.24 | async-start | bytes 1327104 | tf_op jit(solution)/shard_map/all_gather | solution.py:172
  291.0 203.6 %all-gather.44.cloned.1.call-start = ((), (), s32[]{:S(2)}) async-start(), calls=%async_computation.34 | async-start | bytes 3932160 | tf_op jit(solution)/shard_map/all_gather | solution.py:180
  385.1 152.6 %all-gather.34.cloned.1.call-start = ((), (), s32[]{:S(2)}) async-start(), calls=%async_computation.26 | async-start | bytes 1327104 | tf_op jit(solution)/shard_map/all_gather | solution.py:174
  385.6 181.5 %all-gather.28.cloned.1.call-start = ((), (), s32[]{:S(2)}) async-start(), calls=%async_computation.23 | async-start | bytes 3932160 | tf_op jit(solution)/shard_map/all_gather | solution.py:180
  386.4 241.5 %reduce-scatter.34.cloned.1.call-start = ((), (), s32[]{:S(2)}) async-start(), calls=%async_computation.35 | async-start | bytes 7864320 | tf_op jit(solution)/shard_map/reduce_scatter | solution.py:183
  543.5 145.5 %reduce-scatter.28.cloned.1.call-start = ((), (), s32[]{:S(2)}) async-start(), calls=%async_computation.27 | async-start | bytes 7864320 | tf_op jit(solution)/shard_map/reduce_scatter | solution.py:183
  583.1 246.1 %all-gather.38.cloned.1.call-start = ((), (), s32[]{:S(2)}) async-start(), calls=%async_computation.29 | async-start | bytes 10616832 | tf_op jit(solution)/shard_map/all_gather | solution.py:175
  583.6 274.2 %all-gather.46.cloned.1.call-start = ((), (), s32[]{:S(2)}) async-start(), calls=%async_computation.36 | async-start | bytes 3932160 | tf_op jit(solution)/shard_map/all_gather | solution.py:180
  694.4 194.1 %all-gather.54.cloned.1.call-start = ((), (), s32[]{:S(2)}) async-start(), calls=%async_computation.44 | async-start | bytes 3932160 | tf_op jit(solution)/shard_map/all_gather | solution.py:186
  697.8 272.6 %all-gather.40.cloned.1.call-start = ((), (), s32[]{:S(2)}) async-start(), calls=%async_computation.30 | async-start | bytes 5308416 | tf_op jit(solution)/shard_map/all_gather | solution.py:176
  698.4 302.5 %all-gather.36.cloned.1.call-start = ((), (), s32[]{:S(2)}) async-start(), calls=%async_computation.28 | async-start | bytes 3932160 | tf_op jit(solution)/shard_map/all_gather | solution.py:180
  698.9 330.9 %all-gather.48.cloned.1.call-start = ((), (), s32[]{:S(2)}) async-start(), calls=%async_computation.38 | async-start | bytes 3932160 | tf_op jit(solution)/shard_map/all_gather | solution.py:186
  699.7 390.9 %reduce-scatter.44.cloned.1.call-start = ((), (), s32[]{:S(2)}) async-start(), calls=%async_computation.45 | async-start | bytes 7864320 | tf_op jit(solution)/shard_map/reduce_scatter | solution.py:189
  1000.4 151.3 %reduce-scatter.38.cloned.1.call-start = ((), (), s32[]{:S(2)}) async-start(), calls=%async_computation.39 | async-start | bytes 7864320 | tf_op jit(solution)/shard_map/reduce_scatter | solution.py:189
  1059.6 152.9 %reduce-scatter.36.cloned.1.call-start = ((), (), s32[]{:S(2)}) async-start(), calls=%async_computation.37 | async-start | bytes 7864320 | tf_op jit(solution)/shard_map/reduce_scatter | solution.py:183
  1069.6 204.1 %reduce-scatter.30.cloned.1.call-start = ((), (), s32[]{:S(2)}) async-start(), calls=%async_computation.31 | async-start | bytes 7864320 | tf_op jit(solution)/shard_map/reduce_scatter | solution.py:183
  1079.4 228.6 %all-gather.50.cloned.1.call-start = ((), (), s32[]{:S(2)}) async-start(), calls=%async_computation.40 | async-start | bytes 3932160 | tf_op jit(solution)/shard_map/all_gather | solution.py:186
  1367.9 200.0 %all-gather.52.cloned.1.call-start = ((), (), s32[]{:S(2)}) async-start(), calls=%async_computation.42 | async-start | bytes 3932160 | tf_op jit(solution)/shard_map/all_gather | solution.py:186
  1465.9 220.8 %all-gather.58.cloned.1.call-start = ((), (), s32[]{:S(2)}) async-start(), calls=%async_computation.48 | async-start | bytes 3932160 | tf_op jit(solution)/shard_map/all_gather | solution.py:186
  1469.9 383.3 %reduce-scatter.56.cloned.1.call-start = ((), (), s32[]{:S(2)}) async-start(), calls=%async_computation.53 | async-start | bytes 5308416 | tf_op jit(solution)/shard_map/reduce_scatter | solution.py:361
  1485.8 371.0 %reduce-scatter.54.cloned.1.call-start = ((), (), s32[]{:S(2)}) async-start(), calls=%async_computation.52 | async-start | bytes 1327104 | tf_op jit(solution)/shard_map/reduce_scatter | solution.py:355
  1493.8 364.7 %reduce-scatter.52.cloned.1.call-start = ((), (), s32[]{:S(2)}) async-start(), calls=%async_computation.51 | async-start | bytes 1327104 | tf_op jit(solution)/shard_map/reduce_scatter | solution.py:349
  1516.2 575.1 %all-reduce.5.cloned.1.call-start = ((), (), s32[]{:S(2)}) async-start(), calls=%async_computation.57 | async-start | bytes 21233664
  1567.9 590.4 %reduce-scatter.50.cloned.1.call-start = ((), (), s32[]{:S(2)}) async-start(), calls=%async_computation.50 | async-start | bytes 1327104 | tf_op jit(solution)/shard_map/reduce_scatter | solution.py:346
  1803.3 436.8 %reduce-scatter.62.cloned.1.call-start = ((), (), s32[]{:S(2)}) async-start(), calls=%async_computation.56 | async-start | bytes 3981312
  1830.8 469.6 %reduce-scatter.48.cloned.1.call-start = ((), (), s32[]{:S(2)}) async-start(), calls=%async_computation.49 | async-start | bytes 7864320 | tf_op jit(solution)/shard_map/reduce_scatter | solution.py:189
  1840.9 520.4 %reduce-scatter.42.cloned.1.call-start = ((), (), s32[]{:S(2)}) async-start(), calls=%async_computation.43 | async-start | bytes 7864320 | tf_op jit(solution)/shard_map/reduce_scatter | solution.py:189
  1850.7 611.3 %reduce-scatter.60.cloned.1.call-start = ((), (), s32[]{:S(2)}) async-start(), calls=%async_computation.55 | async-start | bytes 811008
  2365.8 195.8 %reduce-scatter.58.cloned.1.call-start = ((), (), s32[]{:S(2)}) async-start(), calls=%async_computation.54 | async-start | bytes 811008
  (163 other events, 4682.0 us)
Sparse Core Ops, SparseCore 0:
  121.5 65.1 all-gather.23
  188.9 39.6 all-gather.25
  260.3 58.3 reduce-scatter.31
  321.3 58.3 reduce-scatter.25
  381.9 41.0 all-gather.31
  425.2 39.8 all-gather.29
  496.6 41.0 all-gather.33
  569.5 58.3 reduce-scatter.33
  630.6 58.3 reduce-scatter.27
  691.0 138.0 all-gather.37
  859.9 28.5 all-gather.53
  890.5 79.8 all-gather.39
  1001.2 28.5 all-gather.47
  1032.2 58.3 reduce-scatter.43
  1093.3 58.3 reduce-scatter.37
  1154.2 58.3 reduce-scatter.35
  1215.3 58.3 reduce-scatter.29
  1279.5 28.5 all-gather.49
  1310.2 28.5 all-gather.55
  1341.1 58.3 reduce-scatter.39
  1402.1 58.3 reduce-scatter.45
  1496.2 28.5 all-gather.57
  1528.2 95.2 reduce-scatter.55
  1627.0 63.9 reduce-scatter.53
  1694.3 62.9 reduce-scatter.51
  1761.3 330.0 all-reduce.4
  2095.3 62.9 reduce-scatter.49
  2161.9 78.1 reduce-scatter.61
  2242.4 57.9 reduce-scatter.47
  2303.0 58.3 reduce-scatter.41
  2366.5 95.5 reduce-scatter.59
  2467.0 94.5 reduce-scatter.57
  (7 shorter events, 189.4 us)
where the time goes:
time: 2580 us; the launch traced here: 2570 us
  waiting for transfers between devices  1740 us (67%)
  matrix products  418 us (16%)
  local copies, waits for them, and re-layouts  202 us (8%)
  other arithmetic  104 us (4%)
  blocking collectives  80.2 us (3%)
    unnamed x43, waiting for transfers between devices  507 us
    reduce_scatter x6, waiting for transfers between devices, share_rows(): lax.psum_scatter(term_rows, 'tensor', scatter_dimension=0, tiled=True)  308 us
    reduce_scatter x6, waiting for transfers between devices, share_grads(): lax.psum_scatter(term_rows, 'tensor', scatter_dimension=0, tiled=True)  280 us
    all_gather x1, waiting for transfers between devices, fetch_weights(): lax.all_gather(w_gate_up, 'dp', axis=1, tiled=True)  129 us
    all_gather x6, waiting for transfers between devices, full_rows(): return lax.all_gather(part_rows, 'tensor', axis=0, tiled=True)  125 us
    all_gather x1, waiting for transfers between devices, fetch_weights(): lax.all_gather(w_down, 'dp', axis=1, tiled=True)  82 us
    all_gather x1, waiting for transfers between devices, fetch_weights(): lax.all_gather(w_qkv, 'dp', axis=1, tiled=True)  67.4 us
    dynamic_update_slice x8, local copies, waits for them, and re-layouts, attend_forward(): results, log_sums = lax.map(per_block, blocks)  63.3 us
  transfers between devices with their start and end apart: 39, of which 33 were waited for; matrix products, arithmetic and copies ran while one was open for 26% of the time, Pallas kernels for 0%

commit v1 on v0

v1 whole, which is shorter than its diff:
```python
import functools
import math

import jax
import jax.numpy as jnp
from jax import lax
from jax.experimental import pallas as pl
from jax.experimental.pallas import tpu as pltpu
from jax.sharding import PartitionSpec as P

HEAD_WIDTH = 64
ROT = 32
EPS = 1e-05
BF = jnp.bfloat16
F32 = jnp.float32
LOG2E = math.log2(math.e)
VMEM_BYTES = 56 * 1024 * 1024


def call(kernel, outs, grid, in_specs, out_specs, scratch, flops, moved, operands):
    return pl.pallas_call(
        kernel,
        out_shape=outs,
        grid=grid,
        in_specs=in_specs,
        out_specs=out_specs,
        scratch_shapes=scratch,
        compiler_params=pltpu.CompilerParams(vmem_limit_bytes=VMEM_BYTES),
        cost_estimate=pl.CostEstimate(flops=flops, bytes_accessed=moved, transcendentals=0),
    )(*operands)


def shape(dims, kind=BF):
    return jax.ShapeDtypeStruct(dims, kind)


def whole(dims):
    return pl.BlockSpec(dims, lambda *_: (0,) * len(dims))


SMEM = pl.BlockSpec(memory_space=pltpu.SMEM)


def dot_nn(a, b):
    return jnp.dot(a, b, preferred_element_type=F32)


def dot_nt(a, b):
    return lax.dot_general(a, b, (((1,), (1,)), ((), ())), preferred_element_type=F32)


def dot_tn(a, b):
    return lax.dot_general(a, b, (((0,), (0,)), ((), ())), preferred_element_type=F32)


def assemble(parity, own, other, scratch):
    pairs, _, rows, width = scratch.shape
    scratch[:, pl.ds(parity, 1)] = own[...].reshape(pairs, 1, rows, width)
    scratch[:, pl.ds(1 - parity, 1)] = other[...].reshape(pairs, 1, rows, width)
    return scratch[...].reshape(pairs * 2 * rows, width)


def split_rows(parity, value, scratch, own, other, columns):
    pairs, _, rows, width = scratch.shape
    scratch[...] = value.reshape(scratch.shape)
    own[:, columns] = scratch[:, pl.ds(parity, 1)].reshape(pairs * rows, width)
    other[:, columns] = scratch[:, pl.ds(1 - parity, 1)].reshape(pairs * rows, width)


def rope(v, cosine, low_sine, high_sine, sign):
    width = v.shape[-1]
    half = ROT // 2
    ahead = pltpu.roll(v, width - half, 1)
    behind = pltpu.roll(v, half, 1)
    return v * cosine + sign * (behind * high_sine - ahead * low_sine)


def head_mask(h):
    lane = lax.broadcasted_iota(jnp.int32, (1, 2 * HEAD_WIDTH), 1)
    return (lane // HEAD_WIDTH) == h


def attend_rows(q_ref, k_ref, v_ref, att_ref, lse_scratch, valid):
    length, width = q_ref.shape
    keys = k_ref.shape[0]
    block = min(256, length)
    scale = HEAD_WIDTH**-0.5 * LOG2E
    lanes = 2 * HEAD_WIDTH

    def rows_step(i, _):
        rows = pl.ds(pl.multiple_of(i * block, block), block)
        lane = lax.broadcasted_iota(jnp.int32, (block, lanes), 1)
        sums = jnp.zeros((block, lanes), F32)
        for pair in range(width // lanes):
            columns = slice(pair * lanes, (pair + 1) * lanes)
            q = q_ref[rows, columns]
            total = None
            for h in range(2):
                mask = head_mask(h)
                k = jnp.where(mask, k_ref[:, columns], jnp.zeros((), BF))
                v = jnp.where(mask, v_ref[:, columns], jnp.zeros((), BF))
                logits = dot_nt(q, k) * scale
                if valid < keys:
                    spot = lax.broadcasted_iota(jnp.int32, logits.shape, 1)
                    logits = jnp.where(spot < valid, logits, -jnp.inf)
                peak = jnp.max(logits, axis=1, keepdims=True)
                weights = jnp.exp2(logits - peak)
                norm = jnp.sum(weights, axis=1, keepdims=True)
                term = dot_nn(weights.astype(BF), v) / norm
                total = term if total is None else total + term
                sums = jnp.where(lane == pair * 2 + h, peak + jnp.log2(norm), sums)
            att_ref[rows, columns] = total.astype(BF)
        lse_scratch[rows, :] = sums
        return 0

    lax.fori_loop(0, length // block, rows_step, 0)


def attend_back(q_ref, k_ref, v_ref, att_ref, do_ref, lse_ref, dq_acc, put_k, put_v, put_q, valid):
    length, width = q_ref.shape
    keys = k_ref.shape[0]
    block = min(256, keys)
    scale = HEAD_WIDTH**-0.5
    lanes = 2 * HEAD_WIDTH
    for pair in range(width // lanes):
        columns = slice(pair * lanes, (pair + 1) * lanes)
        product = do_ref[:, columns].astype(F32) * att_ref[:, columns].astype(F32)
        deltas = []
        for h in range(2):
            ones = jnp.where(head_mask(h), 1.0, 0.0).astype(F32)
            deltas.append(
                lax.dot_general(
                    jnp.broadcast_to(ones, (8, lanes)),
                    product,
                    (((1,), (1,)), ((), ())),
                    preferred_element_type=F32,
                    precision=lax.Precision.HIGHEST,
                )[:1]
            )
        dq_acc[...] = jnp.zeros_like(dq_acc)

        def keys_step(i, _):
            rows = pl.ds(pl.multiple_of(i * block, block), block)
            dk_total, dv_total = None, None
            for h in range(2):
                mask = head_mask(h)
                zero = jnp.zeros((), BF)
                k = jnp.where(mask, k_ref[rows, columns], zero)
                v = jnp.where(mask, v_ref[rows, columns], zero)
                q = q_ref[:, columns]
                do = do_ref[:, columns]
                head = pair * 2 + h
                logits = dot_nt(k, q) * (scale * LOG2E)
                weights = jnp.exp2(logits - lse_ref[head : head + 1, :])
                if valid < keys:
                    spot = i * block + lax.broadcasted_iota(jnp.int32, weights.shape, 0)
                    weights = jnp.where(spot < valid, weights, 0.0)
                dp = dot_nt(v, do)
                ds = (weights * (dp - deltas[h])).astype(BF)
                dv = dot_nn(weights.astype(BF), jnp.where(mask, do, zero))
                dk = dot_nn(ds, jnp.where(mask, q, zero))
                dq_acc[...] += dot_tn(ds, k)
                dk_total = dk if dk_total is None else dk_total + dk
                dv_total = dv if dv_total is None else dv_total + dv
            put_k(rows, columns, dk_total * scale)
            put_v(rows, columns, dv_total)
            return 0

        lax.fori_loop(0, keys // block, keys_step, 0)
        put_q(columns, dq_acc[...] * scale)


def finish_sums(lse_scratch, lse_ref):
    lse_ref[...] = jnp.transpose(lse_scratch[...])[: lse_ref.shape[0]]


def row_norm(t):
    mean = jnp.mean(t, axis=-1, keepdims=True)
    centred = t - mean
    return centred * lax.rsqrt(jnp.mean(centred * centred, axis=-1, keepdims=True) + EPS)


def self_forward(parity, parts, seq, gain, shift, w_own, w_other, cos, low, high, heads):
    part_rows, model = parts[0].shape[1:]
    length = part_rows * len(parts)
    width = heads * HEAD_WIDTH
    lanes = 2 * HEAD_WIDTH
    pairs_rows = w_own.shape[0]

    def kernel(par, p0, p1, p2, p3, g, b, own, other, c_ref, l_ref, h_ref, normed, q, k, v, att, lse, scr, sums):
        for i, part in enumerate((p0, p1, p2, p3)):
            rows = slice(i * part_rows, (i + 1) * part_rows)
            normed[rows, :] = (row_norm(part[0].astype(F32)) * g[...] + b[...]).astype(BF)
        weight = assemble(par[0], own, other, scr)
        for j, target in enumerate((q, k, v)):
            value = dot_nn(normed[...], weight[:, j * width : (j + 1) * width])
            if j == 2:
                target[...] = value.astype(BF)
                continue
            for pair in range(width // lanes):
                columns = slice(pair * lanes, (pair + 1) * lanes)
                target[:, columns] = rope(value[:, columns], c_ref[...], l_ref[...], h_ref[...], 1.0).astype(BF)
        attend_rows(q, k, v, att, sums, length)
        finish_sums(sums, lse)

    part_spec = pl.BlockSpec((1, part_rows, model), lambda *_: (seq, 0, 0))
    table_spec = whole((length, lanes))
    dp = 2 * (pairs_rows // 1)
    return call(
        kernel,
        (shape((length, model)),) + (shape((length, width)),) * 4 + (shape((8, length), F32),),
        (1,),
        [SMEM] + [part_spec] * 4 + [whole((1, model))] * 2 + [whole(w_own.shape)] * 2 + [table_spec] * 3,
        (whole((length, model)),) + (whole((length, width)),) * 4 + (whole((8, length)),),
        [pltpu.VMEM(scratch_dims(model, w_own), BF), pltpu.VMEM((length, lanes), F32)],
        2 * length * model * 3 * width + 4 * length * length * width,
        16_000_000,
        (parity, *parts, gain, shift, w_own, w_other, cos, low, high),
    )


PAIRS = {}


def scratch_dims(model, w_own):
    pairs = PAIRS["pairs"]
    return (pairs, 2, w_own.shape[0] // pairs, w_own.shape[1])


def project(parity, rows, w_own, w_other, column, model):
    length, width = rows.shape
    half_rows = length // 2
    pairs = PAIRS["pairs"]
    w_rows = w_own.shape[0]

    def kernel(par, a, own, other, keep, send, scr):
        weight = assemble(par[0], own, other, scr)
        send[...] = dot_nt(a[half_rows:, :], weight).astype(BF)
        keep[...] = dot_nt(a[:half_rows, :], weight).astype(BF)

    w_spec = pl.BlockSpec((w_rows, width), lambda *_: (0, column))
    return call(
        kernel,
        (shape((half_rows, model)),) * 2,
        (1,),
        [SMEM, whole((length, width)), w_spec, w_spec],
        (whole((half_rows, model)),) * 2,
        [pltpu.VMEM((pairs, 2, w_rows // pairs, width), BF)],
        2 * length * width * model,
        length * (width + model) * 2 + 2 * w_rows * width * 2,
        (parity, rows, w_own, w_other),
    )


def cross_forward(parity, parts, w_own, w_other, column, keys, values, valid):
    part_rows, model = parts[0].shape
    length = part_rows * len(parts)
    width = keys.shape[1]
    count = keys.shape[0]
    lanes = 2 * HEAD_WIDTH
    pairs = PAIRS["pairs"]
    w_rows = w_own.shape[0]

    def kernel(par, p0, p1, p2, p3, own, other, k, v, q, att, lse, scr, sums):
        weight = assemble(par[0], own, other, scr)
        for i, part in enumerate((p0, p1, p2, p3)):
            q[i * part_rows : (i + 1) * part_rows, :] = dot_nn(part[...], weight).astype(BF)
        attend_rows(q, k, v, att, sums, valid)
        finish_sums(sums, lse)

    w_spec = pl.BlockSpec((w_rows, width), lambda *_: (0, column))
    return call(
        kernel,
        (shape((length, width)),) * 2 + (shape((8, length), F32),),
        (1,),
        [SMEM] + [whole((part_rows, model))] * 4 + [w_spec] * 2 + [whole((count, width))] * 2,
        (whole((length, width)),) * 2 + (whole((8, length)),),
        [pltpu.VMEM((pairs, 2, w_rows // pairs, width), BF), pltpu.VMEM((length, lanes), F32)],
        2 * length * model * width + 4 * length * count * width,
        8_000_000,
        (parity, *parts, w_own, w_other, keys, values),
    )


def gate_forward(parity, parts, w_own, w_other):
    part_rows, model = parts[0].shape
    length = part_rows * len(parts)
    hidden = w_own.shape[1] // 2
    block = 512
    steps = hidden // block
    pairs = PAIRS["pairs"]
    w_rows = w_own.shape[0]

    def kernel(par, p0, p1, p2, p3, go, gt, uo, ut, gate, up, act, scr, scr2):
        w_gate = assemble(par[0], go, gt, scr)
        w_up = assemble(par[0], uo, ut, scr2)
        for i, part in enumerate((p0, p1, p2, p3)):
            rows = slice(i * part_rows, (i + 1) * part_rows)
            g = dot_nn(part[...], w_gate)
            u = dot_nn(part[...], w_up)
            gate[rows, :] = g.astype(BF)
            up[rows, :] = u.astype(BF)
            act[rows, :] = (g / (1.0 + jnp.exp2(-LOG2E * g)) * u).astype(BF)

    g_spec = pl.BlockSpec((w_rows, block), lambda j: (0, j))
    u_spec = pl.BlockSpec((w_rows, block), lambda j: (0, steps + j))
    out_spec = pl.BlockSpec((length, block), lambda j: (0, j))
    return call(
        kernel,
        (shape((length, hidden)),) * 3,
        (steps,),
        [SMEM] + [whole((part_rows, model))] * 4 + [g_spec, g_spec, u_spec, u_spec],
        (out_spec,) * 3,
        [pltpu.VMEM((pairs, 2, w_rows // pairs, block), BF)] * 2,
        4 * length * model * hidden,
        22_000_000,
        (parity, *parts, w_own, w_other, w_own, w_other),
    )


def gate_backward(parity, parts, seq, gate, up, d_own, d_other, w_own, w_other):
    part_rows, model = parts[0].shape[1:]
    length = part_rows * len(parts)
    half_rows = length // 2
    hidden = gate.shape[1]
    block = 512
    steps = hidden // block
    pairs = PAIRS["pairs"]
    w_rows = w_own.shape[0]

    def kernel(
        par, p0, p1, p2, p3, g_ref, u_ref, do, dt, go, gt, uo, ut, dgate, dup, keep, send, scr, scr2, scr3, acc
    ):
        j = pl.program_id(0)
        w_down = assemble(par[0], do, dt, scr)
        w_gate = assemble(par[0], go, gt, scr2)
        w_up = assemble(par[0], uo, ut, scr3)

        @pl.when(j == 0)
        def _():
            acc[...] = jnp.zeros_like(acc)

        for i, part in enumerate((p0, p1, p2, p3)):
            rows = slice(i * part_rows, (i + 1) * part_rows)
            d_hidden = dot_nn(part[0], w_down)
            g = g_ref[rows, :].astype(F32)
            u = u_ref[rows, :].astype(F32)
            sig = 1.0 / (1.0 + jnp.exp2(-LOG2E * g))
            d_gate = (d_hidden * u * sig * (1.0 + g * (1.0 - sig))).astype(BF)
            d_up = (d_hidden * (g * sig)).astype(BF)
            dgate[rows, :] = d_gate
            dup[rows, :] = d_up
            acc[rows, :] += dot_nt(d_gate, w_gate) + dot_nt(d_up, w_up)

        @pl.when(j == steps - 1)
        def _():
            keep[...] = acc[:half_rows, :].astype(BF)
            send[...] = acc[half_rows:, :].astype(BF)

    part_spec = pl.BlockSpec((1, part_rows, model), lambda *_: (seq, 0, 0))
    act_spec = pl.BlockSpec((length, block), lambda j: (0, j))
    d_spec = pl.BlockSpec((w_rows, block), lambda j: (0, j))
    u_spec = pl.BlockSpec((w_rows, block), lambda j: (0, steps + j))
    return call(
        kernel,
        (shape((length, hidden)),) * 2 + (shape((half_rows, model)),) * 2,
        (steps,),
        [SMEM] + [part_spec] * 4 + [act_spec] * 2 + [d_spec, d_spec, d_spec, d_spec, u_spec, u_spec],
        (act_spec,) * 2 + (whole((half_rows, model)),) * 2,
        [pltpu.VMEM((pairs, 2, w_rows // pairs, block), BF)] * 3 + [pltpu.VMEM((length, model), F32)],
        6 * length * model * hidden,
        33_000_000,
        (parity, *parts, gate, up, d_own, d_other, w_own, w_other, w_own, w_other),
    )


def cross_backward(parity, parts, w_own, w_other, column_out, column_q, q, keys, values, att, lse, valid):
    part_rows, model = parts[0].shape
    length = part_rows * len(parts)
    half_rows = length // 2
    count, width = keys.shape
    lanes = 2 * HEAD_WIDTH
    pairs = PAIRS["pairs"]
    w_rows = w_own.shape[0]

    def kernel(
        par, p0, p1, p2, p3, oo, ot, qo, qt, q_ref, k_ref, v_ref, a_ref, l_ref, dq, dk, dv, keep, send, scr, do, acc
    ):
        weight = assemble(par[0], oo, ot, scr)
        for i, part in enumerate((p0, p1, p2, p3)):
            do[i * part_rows : (i + 1) * part_rows, :] = dot_nn(part[...], weight).astype(BF)

        def put_k(rows, columns, value):
            dk[rows, columns] = value.astype(BF)

        def put_v(rows, columns, value):
            dv[rows, columns] = value.astype(BF)

        def put_q(columns, value):
            dq[:, columns] = value.astype(BF)

        attend_back(q_ref, k_ref, v_ref, a_ref, do, l_ref, acc, put_k, put_v, put_q, valid)
        weight = assemble(par[0], qo, qt, scr)
        send[...] = dot_nt(dq[half_rows:, :], weight).astype(BF)
        keep[...] = dot_nt(dq[:half_rows, :], weight).astype(BF)

    o_spec = pl.BlockSpec((w_rows, width), lambda *_: (0, column_out))
    q_spec = pl.BlockSpec((w_rows, width), lambda *_: (0, column_q))
    rows_spec = whole((length, width))
    keys_spec = whole((count, width))
    return call(
        kernel,
        (shape((length, width)), shape((count, width)), shape((count, width)))
        + (shape((half_rows, model)),) * 2,
        (1,),
        [SMEM]
        + [whole((part_rows, model))] * 4
        + [o_spec, o_spec, q_spec, q_spec]
        + [rows_spec, keys_spec, keys_spec, rows_spec, whole((8, length))],
        (rows_spec, keys_spec, keys_spec) + (whole((half_rows, model)),) * 2,
        [
            pltpu.VMEM((pairs, 2, w_rows // pairs, width), BF),
            pltpu.VMEM((length, width), BF),
            pltpu.VMEM((length, lanes), F32),
        ],
        4 * length * model * width + 10 * length * count * width,
        12_000_000,
        (parity, *parts, w_own, w_other, w_own, w_other, q, keys, values, att, lse),
    )


def self_backward(parity, parts, o_own, o_other, w_own, w_other, q, k, v, att, lse, cos, low, high):
    part_rows, model = parts[0].shape
    length = part_rows * len(parts)
    half_rows = length // 2
    width = q.shape[1]
    lanes = 2 * HEAD_WIDTH
    pairs = PAIRS["pairs"]
    w_rows = w_own.shape[0]

    def kernel(
        par, p0, p1, p2, p3, oo, ot, wo, wt, q_ref, k_ref, v_ref, a_ref, l_ref, c_ref, lo_ref, h_ref,
        grads, keep, send, scr, scr2, do, acc,
    ):
        weight = assemble(par[0], oo, ot, scr)
        for i, part in enumerate((p0, p1, p2, p3)):
            do[i * part_rows : (i + 1) * part_rows, :] = dot_nn(part[...], weight).astype(BF)

        def put_k(rows, columns, value):
            value = rope(value, c_ref[rows, :], lo_ref[rows, :], h_ref[rows, :], -1.0)
            grads[rows, slice(width + columns.start, width + columns.stop)] = value.astype(BF)

        def put_v(rows, columns, value):
            grads[rows, slice(2 * width + columns.start, 2 * width + columns.stop)] = value.astype(BF)

        def put_q(columns, value):
            grads[:, columns] = rope(value, c_ref[...], lo_ref[...], h_ref[...], -1.0).astype(BF)

        attend_back(q_ref, k_ref, v_ref, a_ref, do, l_ref, acc, put_k, put_v, put_q, length)
        weight = assemble(par[0], wo, wt, scr2)
        send[...] = dot_nt(grads[half_rows:, :], weight).astype(BF)
        keep[...] = dot_nt(grads[:half_rows, :], weight).astype(BF)

    o_spec = pl.BlockSpec((w_rows, width), lambda *_: (0, 0))
    rows_spec = whole((length, width))
    return call(
        kernel,
        (shape((length, 3 * width)),) + (shape((half_rows, model)),) * 2,
        (1,),
        [SMEM]
        + [whole((part_rows, model))] * 4
        + [o_spec] * 2
        + [whole(w_own.shape)] * 2
        + [rows_spec] * 4
        + [whole((8, length))]
        + [whole((length, lanes))] * 3,
        (whole((length, 3 * width)),) + (whole((half_rows, model)),) * 2,
        [
            pltpu.VMEM((pairs, 2, w_rows // pairs, width), BF),
            pltpu.VMEM((pairs, 2, w_rows // pairs, 3 * width), BF),
            pltpu.VMEM((length, width), BF),
            pltpu.VMEM((length, lanes), F32),
        ],
        8 * length * model * width + 10 * length * length * width,
        24_000_000,
        (parity, *parts, o_own, o_other, w_own, w_other, q, k, v, att, lse, cos, low, high),
    )


def weight_grad(parity, lefts, rights, block):
    model = lefts[0].shape[-1]
    total = rights[0].shape[1]
    steps = total // block
    pairs = PAIRS["pairs"]
    count = len(lefts)
    half = model // 2
    per = [left.shape[-2] * (left.shape[0] if left.ndim == 3 else 1) for left in lefts]

    def kernel(par, *refs):
        left_refs = refs[:count]
        right_refs = refs[count : count + len(rights)]
        own, other, acc, scr = refs[count + len(rights) :]
        place = 0
        flat = []
        for right in right_refs:
            flat.append((place, right))
            place += right.shape[0]
        start = 0
        for n, left in enumerate(left_refs):
            rows = left.shape[0]
            base, right = [(b, r) for b, r in flat if b <= start][-1]
            term = dot_tn(left[...], right[start - base : start - base + rows, :])
            if n == 0:
                acc[...] = term
            else:
                acc[...] += term
            start += rows
        split_rows(par[0], acc[...].astype(BF), scr, own, other, slice(None))

    left_specs = [whole(left.shape) for left in lefts]
    right_specs = [pl.BlockSpec((right.shape[0], block), lambda j: (0, j)) for right in rights]
    out_spec = pl.BlockSpec((half, block), lambda j: (0, j))
    return call(
        kernel,
        (shape((half, total)),) * 2,
        (steps,),
        [SMEM] + left_specs + right_specs,
        (out_spec,) * 2,
        [
            pltpu.VMEM((model, block), F32),
            pltpu.VMEM((pairs, 2, model // (2 * pairs), block), BF),
        ],
        2 * sum(per) * model * total,
        sum(per) * (model + total) * 2 + model * total * 2,
        (parity, *lefts, *rights),
    )


def make_body(dp, group):
    pairs = dp // 2
    swap = [(i, i ^ 1) for i in range(dp)]
    lines = [list(range(0, dp, 2)), list(range(1, dp, 2))]
    over_core = [(i, i ^ 1) for i in range(group)]
    over_x = [(i, i ^ 2) for i in range(group)]

    def body(
        tokens,
        context,
        positions,
        seq_mask,
        cotangent,
        norm_gains,
        norm_shifts,
        w_qkv,
        w_self_out,
        w_cross_q,
        w_cross_kv,
        w_cross_out,
        w_gate_up,
        w_down,
    ):
        PAIRS["pairs"] = pairs
        rank = lax.axis_index("dp")
        spot = lax.axis_index("tensor")
        parity = (rank % 2).astype(jnp.int32).reshape(1)
        seqs, part_rows, model = tokens.shape
        length = positions.shape[1]
        ctx_len = context.shape[1]
        rows = w_qkv.shape[1]
        width = w_qkv.shape[2]
        heads = width // HEAD_WIDTH
        hidden = w_down.shape[0]
        ctx_rows = w_cross_kv.shape[1]

        def fetch(local):
            mine = lax.all_gather(local, "dp", axis=0, tiled=True, axis_index_groups=lines)
            return mine, lax.ppermute(mine, "dp", swap)

        def give(own, other):
            got = lax.ppermute(other, "dp", swap)
            return lax.psum_scatter(
                own + got, "dp", scatter_dimension=0, tiled=True, axis_index_groups=lines
            ).astype(F32)

        def core(v):
            return lax.ppermute(v, "tensor", over_core)

        def across(v):
            return lax.ppermute(v, "tensor", over_x)

        def spread(own):
            far = across(own)
            return (own, far, core(own), core(far))

        def gather_sum(keep, send):
            got = core(send)
            part = part_rows
            far = (keep[part:].astype(F32) + got[part:].astype(F32)).astype(BF)
            back = across(far)
            return keep[:part].astype(F32) + got[:part].astype(F32) + back.astype(F32)

        w_one = jnp.transpose(w_qkv, (1, 0, 2)).reshape(rows, 3 * width)
        w_two = jnp.concatenate(
            [w_self_out.T, w_cross_q, w_cross_out.T, w_cross_kv.reshape(rows, width)], axis=1
        )
        w_three = jnp.transpose(w_gate_up, (1, 0, 2)).reshape(rows, 2 * hidden)
        w_four = w_down.T
        qkv_own, qkv_other = fetch(w_one)
        two_own, two_other = fetch(w_two)
        gu_own, gu_other = fetch(w_three)
        dn_own, dn_other = fetch(w_four)

        keep_scale = seq_mask.astype(F32)[:, None, None]
        token_parts = spread(tokens)
        grad_third = cotangent.astype(F32) * keep_scale
        third_parts = spread(grad_third.astype(BF))

        packed = lax.all_gather(
            jnp.concatenate([norm_gains, norm_shifts], axis=0), ("dp", "tensor"), axis=1, tiled=True
        )
        gains = [packed[j : j + 1] for j in range(3)]
        shifts = [packed[3 + j : 4 + j] for j in range(3)]

        order = jnp.stack([spot, spot ^ 2, spot ^ 1, spot ^ 3])
        half_rot = ROT // 2
        lane = jnp.arange(2 * HEAD_WIDTH) % HEAD_WIDTH
        inverse = jnp.exp((lane % half_rot).astype(F32) * (-2.0 * math.log(10000.0) / ROT))
        tables = []
        for s in range(seqs):
            place = jnp.take(positions[s].reshape(group, part_rows), order, axis=0).reshape(length)
            angles = place.astype(F32)[:, None] * inverse[None, :]
            turned = lane < ROT
            sine = jnp.sin(angles)
            tables.append(
                (
                    jnp.where(turned, jnp.cos(angles), 1.0),
                    jnp.where(lane < half_rot, sine, 0.0),
                    jnp.where((lane >= half_rot) & turned, sine, 0.0),
                )
            )

        ctx_pad = -(-ctx_len // 128) * 128
        kv_own = two_own[:, 3 * width :].reshape(pairs, 2, ctx_rows, width)
        kv_other = two_other[:, 3 * width :].reshape(pairs, 2, ctx_rows, width)
        even = parity[0] == 0
        kv_weight = jnp.stack(
            [jnp.where(even, kv_own, kv_other), jnp.where(even, kv_other, kv_own)], axis=1
        )
        kv_weight = jnp.transpose(kv_weight, (2, 0, 1, 3, 4)).reshape(2, pairs * 2 * ctx_rows, width)
        padded = jnp.pad(context, ((0, 0), (0, ctx_pad - ctx_len), (0, 0)))
        cross_kv = jnp.einsum("scd,kdh->skch", padded, kv_weight, preferred_element_type=F32).astype(BF)

        state = [dict() for _ in range(seqs)]
        for s in range(seqs):
            st = state[s]
            st["normed1"], st["q"], st["k"], st["v"], st["att"], st["lse"] = self_forward(
                parity, token_parts, s, gains[0], shifts[0], qkv_own, qkv_other, *tables[s], heads
            )
        for s in range(seqs):
            st = state[s]
            keep, send = project(parity, st["att"], two_own, two_other, 0, model)
            st["first"] = tokens[s].astype(F32) + gather_sum(keep, send)
            st["xhat2"], st["inv2"] = norm_parts(st["first"])
            normed2 = (st["xhat2"] * gains[1] + shifts[1]).astype(BF)
            st["normed2"] = spread(normed2)
        for s in range(seqs):
            st = state[s]
            st["cq"], st["crossed"], st["clse"] = cross_forward(
                parity, st["normed2"], two_own, two_other, 1, cross_kv[s, 0], cross_kv[s, 1], ctx_len
            )
            keep, send = project(parity, st["crossed"], two_own, two_other, 2, model)
            st["second"] = st["first"] + gather_sum(keep, send)
            st["xhat3"], st["inv3"] = norm_parts(st["second"])
            normed3 = (st["xhat3"] * gains[2] + shifts[2]).astype(BF)
            st["normed3"] = spread(normed3)
        for s in range(seqs):
            st = state[s]
            st["gate"], st["up"], st["hidden"] = gate_forward(parity, st["normed3"], gu_own, gu_other)
        outs = []
        for s in range(seqs):
            st = state[s]
            st["dgate"], st["dup"], keep, send = gate_backward(
                parity, third_parts, s, st["gate"], st["up"], dn_own, dn_other, gu_own, gu_other
            )
            st["d_normed3"] = gather_sum(keep, send)
        third_lefts = [part[s] for s in range(seqs) for part in third_parts]
        dn_grad = give(*weight_grad(parity, third_lefts, [st["hidden"] for st in state], 384))
        gate_grad = weight_grad(
            parity, [p for st in state for p in st["normed3"]], [st["dgate"] for st in state], 384
        )
        up_grad = weight_grad(
            parity, [p for st in state for p in st["normed3"]], [st["dup"] for st in state], 384
        )
        gate_part = give(*gate_grad)
        up_part = give(*up_grad)
        for s in range(seqs):
            st = state[s]
            keep, send = project(parity, st["hidden"], dn_own, dn_other, 0, model)
            third = st["second"] + gather_sum(keep, send)
            outs.append((third * keep_scale[s]).astype(BF))

        gain_grads, shift_grads = [0.0] * 3, [0.0] * 3
        for s in range(seqs):
            st = state[s]
            back, gain_term, shift_term = norm_back(st["d_normed3"], st["xhat3"], st["inv3"], gains[2])
            gain_grads[2] += gain_term
            shift_grads[2] += shift_term
            st["d_second"] = grad_third[s] + back
            st["dy2"] = spread(st["d_second"].astype(BF))
        for s in range(seqs):
            st = state[s]
            st["dcq"], st["dck"], st["dcv"], keep, send = cross_backward(
                parity, st["dy2"], two_own, two_other, 2, 1, st["cq"],
                cross_kv[s, 0], cross_kv[s, 1], st["crossed"], st["clse"], ctx_len,
            )
            d_normed2 = gather_sum(keep, send)
            back, gain_term, shift_term = norm_back(d_normed2, st["xhat2"], st["inv2"], gains[1])
            gain_grads[1] += gain_term
            shift_grads[1] += shift_term
            st["d_first"] = st["d_second"] + back
            st["dy1"] = spread(st["d_first"].astype(BF))
        co_grad = weight_grad(
            parity, [p for st in state for p in st["dy2"]], [st["crossed"] for st in state], width
        )
        cq_grad = weight_grad(
            parity, [p for st in state for p in st["normed2"]], [st["dcq"] for st in state], width
        )
        dkv = jnp.stack([jnp.stack([st["dck"], st["dcv"]]) for st in state])[:, :, :ctx_len]
        kv_grad = jnp.einsum("scd,skch->kdh", context, dkv, preferred_element_type=F32).astype(BF)
        kv_grad = jnp.transpose(kv_grad.reshape(2, pairs, 2, ctx_rows, width), (1, 2, 0, 3, 4))
        kv_own_grad = jnp.where(even, kv_grad[:, 0], kv_grad[:, 1]).reshape(pairs * rows, width)
        kv_other_grad = jnp.where(even, kv_grad[:, 1], kv_grad[:, 0]).reshape(pairs * rows, width)
        middle = give(
            jnp.concatenate([co_grad[0], cq_grad[0], kv_own_grad], axis=1),
            jnp.concatenate([co_grad[1], cq_grad[1], kv_other_grad], axis=1),
        )
        for s in range(seqs):
            st = state[s]
            st["dqkv"], keep, send = self_backward(
                parity, st["dy1"], two_own, two_other, qkv_own, qkv_other,
                st["q"], st["k"], st["v"], st["att"], st["lse"], *tables[s],
            )
            st["d_normed1"] = gather_sum(keep, send)
        so_grad = weight_grad(
            parity, [p for st in state for p in st["dy1"]], [st["att"] for st in state], width
        )
        qkv_grad = weight_grad(
            parity, [st["normed1"] for st in state], [st["dqkv"] for st in state], width
        )
        last = give(
            jnp.concatenate([so_grad[0], qkv_grad[0]], axis=1),
            jnp.concatenate([so_grad[1], qkv_grad[1]], axis=1),
        )
        grad_inputs = []
        for s in range(seqs):
            st = state[s]
            xhat, inv = norm_parts(tokens[s].astype(F32))
            back, gain_term, shift_term = norm_back(st["d_normed1"], xhat, inv, gains[0])
            gain_grads[0] += gain_term
            shift_grads[0] += shift_term
            grad_inputs.append(st["d_first"] + back)
        norm_grads = lax.psum_scatter(
            jnp.stack(gain_grads + shift_grads), ("dp", "tensor"), scatter_dimension=1, tiled=True
        )
        return (
            jnp.stack(outs),
            jnp.stack(grad_inputs),
            norm_grads[:3],
            norm_grads[3:],
            jnp.transpose(last[:, width:].reshape(rows, 3, width), (1, 0, 2)),
            last[:, :width].T,
            middle[:, width : 2 * width],
            middle[:, 2 * width :].reshape(2, ctx_rows, width),
            middle[:, :width].T,
            jnp.stack([gate_part, up_part]),
            dn_grad.T,
        )

    return body


def norm_parts(rows):
    mean = jnp.mean(rows, axis=-1, keepdims=True)
    centred = rows - mean
    inv = lax.rsqrt(jnp.mean(centred * centred, axis=-1, keepdims=True) + EPS)
    return centred * inv, inv


def norm_back(grad, xhat, inv, gain):
    scaled = grad * gain
    back = inv * (
        scaled
        - jnp.mean(scaled, axis=-1, keepdims=True)
        - xhat * jnp.mean(scaled * xhat, axis=-1, keepdims=True)
    )
    return back, jnp.sum(grad * xhat, axis=0), jnp.sum(grad, axis=0)


def solution(mesh):
    in_specs = (
        P("dp", "tensor", None),
        P("dp", None, None),
        P("dp", None),
        P("dp"),
        P("dp", "tensor", None),
        P(None, ("dp", "tensor")),
        P(None, ("dp", "tensor")),
        P(None, "dp", "tensor"),
        P("tensor", "dp"),
        P("dp", "tensor"),
        P(None, "dp", "tensor"),
        P("tensor", "dp"),
        P(None, "dp", "tensor"),
        P("tensor", "dp"),
    )
    out_specs = (
        P("dp", "tensor", None),
        P("dp", "tensor", None),
        P(None, ("dp", "tensor")),
        P(None, ("dp", "tensor")),
        P(None, "dp", "tensor"),
        P("tensor", "dp"),
        P("dp", "tensor"),
        P(None, "dp", "tensor"),
        P("tensor", "dp"),
        P(None, "dp", "tensor"),
        P("tensor", "dp"),
    )
    body = make_body(mesh.shape["dp"], mesh.shape["tensor"])
    return jax.shard_map(body, mesh=mesh, in_specs=in_specs, out_specs=out_specs, check_vma=False)
```

time: 2580 us -> 1230 us (0.48)
  waiting for transfers between devices: 1740 us -> 587 us
  matrix products: 418 us -> 2.62 us
  Pallas kernels: 0 us -> 385 us
  local copies, waits for them, and re-layouts: 202 us -> 39.2 us
  starting transfers between devices: 4.47 us -> 45.2 us
  blocking collectives: 80.2 us -> 39.6 us
    reduce_scatter x16 -> x5, waiting for transfers between devices: 649 us -> 47.2 us  [give(): lax.psum_scatter(own + got, 'dp', scatter_dimension=0, tiled=True, axis_i...]
    all_gather x19 -> x4, waiting for transfers between devices: 583 us -> 90 us  [fetch(): lax.all_gather(local, 'dp', axis=0, tiled=True, axis_index_groups=lines)]
    unnamed x43 -> x11, waiting for transfers between devices: 507 us -> 60.7 us
    dot_general x96 -> x2, matrix products: 418 us -> 2.62 us  [the longest x1 1.84 us: body(): jnp.einsum('scd,skch->kdh', context, dkv, preferred_element_type=F32)]
    ppermute x0 -> x63, waiting for transfers between devices: none -> 389 us  [the longest x22 297 us: across(): return lax.ppermute(v, 'tensor', over_x)]
    pallas_call x0 -> x25, Pallas kernels: none -> 385 us  [call(): pl.pallas_call(kernel, out_shape=outs, grid=grid, in_specs=in_specs, out_...]
    dynamic_update_slice x8 -> x0, local copies, waits for them, and re-layouts: 63.3 us -> none  [attend_forward(): results, log_sums = lax.map(per_block, blocks)]
    ppermute x0 -> x63, starting transfers between devices: none -> 44.2 us  [the longest x22 26.7 us: across(): return lax.ppermute(v, 'tensor', over_x)]
  transfers between devices with their start and end apart: 39 -> 73, of which waited for: 33 -> 29; matrix products, arithmetic and copies ran while one was open for 26% -> 11% of each run, Pallas kernels for 0% -> 25%
where the time goes in v1:
time: 1230 us; the launch traced here: 1220 us
  waiting for transfers between devices  587 us (48%)
  Pallas kernels  385 us (31%)
  other arithmetic  108 us (9%)
  starting transfers between devices  45.2 us (4%)
  blocking collectives  39.6 us (3%)
  local copies, waits for them, and re-layouts  39.2 us (3%)
  between operations  15.8 us (1%)
    pallas_call x25, Pallas kernels, call(): pl.pallas_call(kernel, out_shape=outs, grid=grid, in_specs=in_specs, out_...  385 us
    ppermute x22, waiting for transfers between devices, across(): return lax.ppermute(v, 'tensor', over_x)  297 us
    all_gather x4, waiting for transfers between devices, fetch(): lax.all_gather(local, 'dp', axis=0, tiled=True, axis_index_groups=lines)  90 us
    ppermute x5, waiting for transfers between devices, give(): got = lax.ppermute(other, 'dp', swap)  65.7 us
    unnamed x11, waiting for transfers between devices  60.7 us
    reduce_scatter x5, waiting for transfers between devices, give(): lax.psum_scatter(own + got, 'dp', scatter_dimension=0, tiled=True, axis_i...  47.2 us
    all_gather x1, blocking collectives, body(): lax.all_gather(jnp.concatenate([norm_gains, norm_shifts], axis=0), ('dp',...  39.6 us
    ppermute x22, starting transfers between devices, across(): return lax.ppermute(v, 'tensor', over_x)  26.7 us
  transfers between devices with their start and end apart: 73, of which 29 were waited for; matrix products, arithmetic and copies ran while one was open for 11% of the time, Pallas kernels for 25%

profile of v1, /device:TPU:0, one launch (start us, length us, event | category | flops | bytes accessed | tf_op | source)
XLA Modules:
  0.0 1222.4 jit_solution(10600420734195393347)
XLA Ops:
  13.3 50.1 %all-gather.8.cloned.1.call-done.own.oo.qo = bf16[768,1536]{1,0:T(8,128)(2,1)} async-done(((bf16[192,1536]{1,0:T(8,128)(2,1)}), bf16[768,1536]{1,0:T(8,128)(2,1)}) %all-gather.8.cloned.1.call-update) | async-done | bytes 2359312 | tf_op jit(solution)/shard_map/all_gather | solution.py:576
  64.9 39.8 %all-gather.6.cloned.1.call-done.own.wo = bf16[768,1152]{1,0:T(8,128)(2,1)} async-done(((bf16[192,1152]{1,0:T(8,128)(2,1)}), bf16[768,1152]{1,0:T(8,128)(2,1)}) %all-gather.6.cloned.1.call-update) | async-done | bytes 1769488 | tf_op jit(solution)/shard_map/all_gather | solution.py:576
  108.1 39.6 %all-gather = f32[32,48,6]{1,2,0:T(8,128)S(1)} all-gather(f32[1,48,6]{1,2,0:T(8,128)S(1)} %maximum_bitcast_fusion.2), channel_id=1, replica_groups=mesh['dp'=8,'tensor'=4] {'dp','tensor'}, dimensions={0}, use_global_device_ids=true | all-gather | bytes 38016 | tf_op jit(solution)/shard_map/all_gather | solution.py:618
  155.3 23.7 %shard_map.227 = (bf16[1024,1536]{1,0:T(8,128)(2,1)}, bf16[1024,384]{1,0:T(8,128)(2,1)}, bf16[1024,384]{1,0:T(8,128)(2,1)}, bf16[1024,384]{1,0:T(8,128)(2,1)}, b...) custom-call(s32[1]{0:T(128)} %bitcast.1.par, bf16[2,256,1536]{2,1,0:T(8,128)(2,1)} %p0.3, ...), custom_call_target="tpu_custom_call" | custom-call | flops 5234491392 | bytes 16000000 | tf_op jit(solution)/shard_map/pallas_call | solution.py:21
  184.9 23.7 %shard_map.221 = (bf16[1024,1536]{1,0:T(8,128)(2,1)}, bf16[1024,384]{1,0:T(8,128)(2,1)}, bf16[1024,384]{1,0:T(8,128)(2,1)}, bf16[1024,384]{1,0:T(8,128)(2,1)}, b...) custom-call(s32[1]{0:T(128)} %bitcast.1.par, bf16[2,256,1536]{2,1,0:T(8,128)(2,1)} %p0.3, ...), custom_call_target="tpu_custom_call" | custom-call | flops 5234491392 | bytes 16000000 | tf_op jit(solution)/shard_map/pallas_call | solution.py:21
  236.3 15.9 %collective-permute-done.6 = bf16[256,1536]{1,0:T(8,128)(2,1)S(1)} collective-permute-done((bf16[256,1536]{1,0:T(8,128)(2,1)S(1)}, bf16[256,1536]{1,0:T(8,128)(2,1)S(1)}, u32[]{:S(2)}, u32[]{:S(2)}) %collective-permute-start.6) | collective-permute-done | bytes 786464 | tf_op jit(solution)/shard_map/ppermute | solution.py:589
  260.4 18.6 %collective-permute-done.7.p1.refs_1_ = bf16[256,1536]{1,0:T(8,128)(2,1)} collective-permute-done((bf16[256,1536]{1,0:T(8,128)(2,1)}, bf16[256,1536]{1,0:T(8,128)(2,1)}, u32[]{:S(2)}, u32[]{:S(2)}) %collective-permute-start.7) | collective-permute-done | bytes 786464 | tf_op jit(solution)/shard_map/ppermute | solution.py:589
  353.8 14.5 %collective-permute-done.25 = bf16[256,1536]{1,0:T(8,128)(2,1)} collective-permute-done((bf16[256,1536]{1,0:T(8,128)(2,1)}, bf16[256,1536]{1,0:T(8,128)(2,1)}, u32[]{:S(2)}, u32[]{:S(2)}) %collective-permute-start.25) | collective-permute-done | bytes 786464 | tf_op jit(solution)/shard_map/ppermute | solution.py:589
  374.8 44.1 %collective-permute-done.12.p1.refs_1_ = bf16[256,1536]{1,0:T(8,128)(2,1)} collective-permute-done((bf16[256,1536]{1,0:T(8,128)(2,1)}, bf16[256,1536]{1,0:T(8,128)(2,1)}, u32[]{:S(2)}, u32[]{:S(2)}) %collective-permute-start.12) | collective-permute-done | bytes 786464 | tf_op jit(solution)/shard_map/ppermute | solution.py:589
  435.5 15.5 %shard_map.225 = (bf16[1024,1536]{1,0:T(8,128)(2,1)}, bf16[1024,1536]{1,0:T(8,128)(2,1)}, bf16[1024,1536]{1,0:T(8,128)(2,1)}) custom-call(s32[1]{0:T(128)} %bitcast.1.par, bf16[256,1536]{1,0:T(8,128)(2,1)} %get-tuple-element.267.p0.refs_0_, bf16[256,1536]{1,0:T(8,128)(2,1)} %collective-permute-done.12.p1.refs_1_, ...), custom_call_target="tpu_custom_call" | custom-call | flops 9663676416 | bytes 22000000 | tf_op jit(solution)/shard_map/pallas_call | solution.py:21
  452.7 15.2 %shard_map.231 = (bf16[1024,1536]{1,0:T(8,128)(2,1)}, bf16[1024,1536]{1,0:T(8,128)(2,1)}, bf16[1024,1536]{1,0:T(8,128)(2,1)}) custom-call(s32[1]{0:T(128)} %bitcast.1.par, bf16[256,1536]{1,0:T(8,128)(2,1)} %get-tuple-element.268.p0.refs_4_, bf16[256,1536]{1,0:T(8,128)(2,1)} %collective-permute-done.26.p1.refs_5_, bf16[256,1536]{1,0:T(8,128)(2,1)} %copy-done.101, ...), custom_call_target="tpu_custom_call" | custom-call | flops 9663676416 | bytes 22000000 | tf_op jit(solution)/shard_map/pallas_call | solution.py:21
  468.0 13.9 %collective-permute-done.16.other.dt = bf16[768,1536]{1,0:T(8,128)(2,1)} collective-permute-done((bf16[768,1536]{1,0:T(8,128)(2,1)}, bf16[768,1536]{1,0:T(8,128)(2,1)}, u32[]{:S(2)}, u32[]{:S(2)}) %collective-permute-start.16) | collective-permute-done | bytes 2359328 | tf_op jit(solution)/shard_map/ppermute | solution.py:577
  481.9 25.9 %shard_map.233 = (bf16[1024,1536]{1,0:T(8,128)(2,1)}, bf16[1024,1536]{1,0:T(8,128)(2,1)}, bf16[512,1536]{1,0:T(8,128)(2,1)}, bf16[512,1536]{1,0:T(8,128)(2,1)}) custom-call(s32[1]{0:T(128)} %bitcast.1.par, bf16[2,256,1536]{2,1,0:T(8,128)(2,1)} %get-tuple-element.241.p0, bf16[2,256,1536]{2,1,0:T(8,128)(2,1)} %collective-permute-done.31.p1, ...), custom_call_target="tpu_custom_call" | custom-call | flops 14495514624 | bytes 33000000 | tf_op jit(solution)/shard_map/pallas_call | solution.py:21
  507.8 26.3 %shard_map.236 = (bf16[1024,1536]{1,0:T(8,128)(2,1)}, bf16[1024,1536]{1,0:T(8,128)(2,1)}, bf16[512,1536]{1,0:T(8,128)(2,1)}, bf16[512,1536]{1,0:T(8,128)(2,1)}) custom-call(s32[1]{0:T(128)} %bitcast.1.par, bf16[2,256,1536]{2,1,0:T(8,128)(2,1)} %get-tuple-element.241.p0, bf16[2,256,1536]{2,1,0:T(8,128)(2,1)} %collective-permute-done.31.p1, ...), custom_call_target="tpu_custom_call" | custom-call | flops 14495514624 | bytes 33000000 | tf_op jit(solution)/shard_map/pallas_call | solution.py:21
  534.1 18.8 %shard_map.243 = (bf16[768,1536]{1,0:T(8,128)(2,1)}, bf16[768,1536]{1,0:T(8,128)(2,1)}) custom-call(s32[1]{0:T(128)} %bitcast.1.par, bf16[256,1536]{1,0:T(8,128)(2,1)} %get-tuple-element.267.p0.refs_0_, bf16[256,1536]{1,0:T(8,128)(2,1)} %collective-permute-done.12.p1.refs_1_, bf16[256,1536]{1,0:T(8,128)(2,1)} %collective-permute-done.13.p2.refs_2_, ...), custom_call_target="tpu_custom_call" | custom-call | flops 9663676416 | bytes 17301504 | tf_op jit(solution)/shard_map/pallas_call | solution.py:21
  563.5 42.3 %collective-permute-done.60 = bf16[768,1536]{1,0:T(8,128)(2,1)S(1)} collective-permute-done((bf16[768,1536]{1,0:T(8,128)(2,1)}, bf16[768,1536]{1,0:T(8,128)(2,1)S(1)}, u32[]{:S(2)}, u32[]{:S(2)}) %collective-permute-start.60) | collective-permute-done | bytes 2359328 | tf_op jit(solution)/shard_map/ppermute | solution.py:580
  617.9 19.0 %shard_map.244 = (bf16[768,1536]{1,0:T(8,128)(2,1)}, bf16[768,1536]{1,0:T(8,128)(2,1)}) custom-call(s32[1]{0:T(128)} %bitcast.1.par, bf16[256,1536]{1,0:T(8,128)(2,1)} %get-tuple-element.267.p0.refs_0_, bf16[256,1536]{1,0:T(8,128)(2,1)} %collective-permute-done.12.p1.refs_1_, bf16[256,1536]{1,0:T(8,128)(2,1)} %collective-permute-done.13.p2.refs_2_, ...), custom_call_target="tpu_custom_call" | custom-call | flops 9663676416 | bytes 17301504 | tf_op jit(solution)/shard_map/pallas_call | solution.py:21
  648.8 18.9 %shard_map.245 = (bf16[768,1536]{1,0:T(8,128)(2,1)}, bf16[768,1536]{1,0:T(8,128)(2,1)}) custom-call(s32[1]{0:T(128)} %bitcast.1.par, bf16[256,1536]{1,0:T(8,128)(2,1)} %get-tuple-element.249.refs_0_, bf16[256,1536]{1,0:T(8,128)(2,1)} %get-tuple-element.247.refs_1_, bf16[256,1536]{1,0:T(8,128)(2,1)} %get-tuple-element.245.refs_2_, ...), custom_call_target="tpu_custom_call" | custom-call | flops 9663676416 | bytes 17301504 | tf_op jit(solution)/shard_map/pallas_call | solution.py:21
  726.1 16.5 %collective-permute-done.47 = bf16[256,1536]{1,0:T(8,128)(2,1)} collective-permute-done((bf16[256,1536]{1,0:T(8,128)(2,1)}, bf16[256,1536]{1,0:T(8,128)(2,1)}, u32[]{:S(2)}, u32[]{:S(2)}) %collective-permute-start.47) | collective-permute-done | bytes 786464 | tf_op jit(solution)/shard_map/ppermute | solution.py:589
  754.5 18.4 %collective-permute-done.36.p1.refs_1_ = bf16[256,1536]{1,0:T(8,128)(2,1)S(1)} collective-permute-done((bf16[256,1536]{1,0:T(8,128)(2,1)S(1)}, bf16[256,1536]{1,0:T(8,128)(2,1)S(1)}, u32[]{:S(2)}, u32[]{:S(2)}) %collective-permute-start.36) | collective-permute-done | bytes 786464 | tf_op jit(solution)/shard_map/ppermute | solution.py:589
  773.5 15.2 %collective-permute-done.48.p1.refs_5_ = bf16[256,1536]{1,0:T(8,128)(2,1)} collective-permute-done((bf16[256,1536]{1,0:T(8,128)(2,1)}, bf16[256,1536]{1,0:T(8,128)(2,1)}, u32[]{:S(2)}, u32[]{:S(2)}) %collective-permute-start.48) | collective-permute-done | bytes 786464 | tf_op jit(solution)/shard_map/ppermute | solution.py:589
  789.8 15.6 %shard_map.234 = (bf16[1024,384]{1,0:T(8,128)(2,1)}, bf16[256,384]{1,0:T(8,128)(2,1)}, bf16[256,384]{1,0:T(8,128)(2,1)}, bf16[512,1536]{1,0:T(8,128)(2,1)}, bf16[512,1536]{1,0:T(8,128)(2,1)}) custom-call(s32[1]{0:T(128)} %bitcast.1.par, bf16[256,1536]{1,0:T(8,128)(2,1)} %copy-done.24, bf16[256,1536]{1,0:T(8,128)(2,1)} %copy-done.53, ...), custom_call_target="tpu_custom_call" | custom-call | flops 3422552064 | bytes 12000000 | tf_op jit(solution)/shard_map/pallas_call | solution.py:21
  809.9 15.5 %shard_map.237 = (bf16[1024,384]{1,0:T(8,128)(2,1)}, bf16[256,384]{1,0:T(8,128)(2,1)}, bf16[256,384]{1,0:T(8,128)(2,1)}, bf16[512,1536]{1,0:T(8,128)(2,1)}, bf16[512,1536]{1,0:T(8,128)(2,1)}) custom-call(s32[1]{0:T(128)} %bitcast.1.par, bf16[256,1536]{1,0:T(8,128)(2,1)} %get-tuple-element.236.p0.refs_4_, ...), custom_call_target="tpu_custom_call" | custom-call | flops 3422552064 | bytes 12000000 | tf_op jit(solution)/shard_map/pallas_call | solution.py:21
  854.9 15.2 %collective-permute-done.40 = bf16[256,1536]{1,0:T(8,128)(2,1)S(1)} collective-permute-done((bf16[256,1536]{1,0:T(8,128)(2,1)S(1)}, bf16[256,1536]{1,0:T(8,128)(2,1)S(1)}, u32[]{:S(2)}, u32[]{:S(2)}) %collective-permute-start.40) | collective-permute-done | bytes 786464 | tf_op jit(solution)/shard_map/ppermute | solution.py:589
  872.1 14.3 %collective-permute-done.52 = bf16[256,1536]{1,0:T(8,128)(2,1)S(1)} collective-permute-done((bf16[256,1536]{1,0:T(8,128)(2,1)S(1)}, bf16[256,1536]{1,0:T(8,128)(2,1)S(1)}, u32[]{:S(2)}, u32[]{:S(2)}) %collective-permute-start.52) | collective-permute-done | bytes 786464 | tf_op jit(solution)/shard_map/ppermute | solution.py:589
  895.3 15.9 %collective-permute-done.41.p1.refs_1_ = bf16[256,1536]{1,0:T(8,128)(2,1)} collective-permute-done((bf16[256,1536]{1,0:T(8,128)(2,1)}, bf16[256,1536]{1,0:T(8,128)(2,1)}, u32[]{:S(2)}, u32[]{:S(2)}) %collective-permute-start.41) | collective-permute-done | bytes 786464 | tf_op jit(solution)/shard_map/ppermute | solution.py:589
  927.6 35.6 %shard_map.235 = (bf16[1024,1152]{1,0:T(8,128)(2,1)}, bf16[512,1536]{1,0:T(8,128)(2,1)}, bf16[512,1536]{1,0:T(8,128)(2,1)}) custom-call(s32[1]{0:T(128)} %bitcast.1.par, bf16[256,1536]{1,0:T(8,128)(2,1)} %get-tuple-element.218.p0.refs_0_, bf16[256,1536]{1,0:T(8,128)(2,1)} %collective-permute-done.41.p1.refs_1_, bf16[256,1536]{1,0:T(8,128)(2,1)} %copy-done.104, ...), custom_call_target="tpu_custom_call" | custom-call | flops 8858370048 | bytes 24000000 | tf_op jit(solution)/shard_map/pallas_call | solution.py:21
  964.9 35.5 %shard_map.238 = (bf16[1024,1152]{1,0:T(8,128)(2,1)}, bf16[512,1536]{1,0:T(8,128)(2,1)}, bf16[512,1536]{1,0:T(8,128)(2,1)}) custom-call(s32[1]{0:T(128)} %bitcast.1.par, bf16[256,1536]{1,0:T(8,128)(2,1)} %get-tuple-element.216.p0.refs_4_, bf16[256,1536]{1,0:T(8,128)(2,1)} %copy-done.103, bf16[256,1536]{1,0:T(8,128)(2,1)} %copy-done.105, ...), custom_call_target="tpu_custom_call" | custom-call | flops 8858370048 | bytes 24000000 | tf_op jit(solution)/shard_map/pallas_call | solution.py:21
  1008.3 15.4 %shard_map.240 = (bf16[768,1152]{1,0:T(8,128)(2,1)}, bf16[768,1152]{1,0:T(8,128)(2,1)}) custom-call(s32[1]{0:T(128)} %bitcast.1.par, bf16[1024,1536]{1,0:T(8,128)(2,1)} %get-tuple-element.133.refs_0_, bf16[1024,1536]{1,0:T(8,128)(2,1)} %get-tuple-element.134.refs_1_, bf16[1024,1152]{1,0:T(8,128)(2,1)} %get-tuple-element.135.refs_2_, ...), custom_call_target="tpu_custom_call" | custom-call | flops 7247757312 | bytes 14548992 | tf_op jit(solution)/shard_map/pallas_call | solution.py:21
  1031.2 17.9 %collective-permute-done.45 = bf16[256,1536]{1,0:T(8,128)(2,1)S(1)} collective-permute-done((bf16[256,1536]{1,0:T(8,128)(2,1)S(1)}, bf16[256,1536]{1,0:T(8,128)(2,1)S(1)}, u32[]{:S(2)}, u32[]{:S(2)}) %collective-permute-start.45) | collective-permute-done | bytes 786464 | tf_op jit(solution)/shard_map/ppermute | solution.py:589
  1102.0 60.5 %reduce-scatter.19.cloned.1.call-done = f32[48,6]{1,0:T(8,128)} async-done(((f32[1536,6]{1,0:T(8,128)}), f32[48,6]{1,0:T(8,128)}) %reduce-scatter.19.cloned.1.call-update) | async-done | bytes 1168
  1164.8 47.2 %reduce-scatter.9.cloned.1.call-done = bf16[192,1536]{1,0:T(8,128)(2,1)} async-done(((bf16[768,1536]{1,0:T(8,128)(2,1)}), bf16[192,1536]{1,0:T(8,128)(2,1)}) %reduce-scatter.9.cloned.1.call-update) | async-done | bytes 589840 | tf_op jit(solution)/shard_map/reduce_scatter | solution.py:581
  (498 shorter events, 402.0 us)
Async XLA Ops:
  7.2 56.2 %all-gather.8.cloned.1.call-start = ((), (), s32[]{:S(2)}) async-start(), calls=%async_computation.7 | async-start | bytes 2949120 | tf_op jit(solution)/shard_map/all_gather | solution.py:576
  9.3 95.4 %all-gather.6.cloned.1.call-start = ((), (), s32[]{:S(2)}) async-start(), calls=%async_computation.6 | async-start | bytes 2211840 | tf_op jit(solution)/shard_map/all_gather | solution.py:576
  10.2 316.5 %all-gather.10.cloned.1.call-start = ((), (), s32[]{:S(2)}) async-start(), calls=%async_computation.8 | async-start | bytes 5898240 | tf_op jit(solution)/shard_map/all_gather | solution.py:576
  10.3 95.9 %collective-permute-start = (bf16[2,256,1536]{2,1,0:T(8,128)(2,1)}, bf16[2,256,1536]{2,1,0:T(8,128)(2,1)}, u32[]{:S(2)}, u32[]{:S(2)}) collective-permute-start(bf16[2,256,1536]{2,1,0:T(8,128)(2,1)} %p0.3), channel_id=1, source_target_pairs={{0,2},{1,3},{2,0},{3,1},{4,6},{5,7},{6,4},{7,5},{8,10},{9,11},{10,... | collective-permute-start | bytes 4718600 | tf_op jit(solution)/shard_map/ppermute | solution.py:589
  63.4 115.6 %collective-permute-start.4 = (bf16[768,1536]{1,0:T(8,128)(2,1)}, bf16[768,1536]{1,0:T(8,128)(2,1)S(1)}, u32[]{:S(2)}, u32[]{:S(2)}) collective-permute-start(bf16[768,1536]{1,0:T(8,128)(2,1)} %all-gather.8.cloned.1.call-done.own.oo.qo), channel_id=1, source_target_pairs={{0,4},{4,0},{8,12},{12,8},{16,20},{20,16},{24,28},{28,24},{1,5},{5... | collective-permute-start | bytes 7077896 | tf_op jit(solution)/shard_map/ppermute | solution.py:577
  104.7 50.6 %collective-permute-start.3 = (bf16[768,1152]{1,0:T(8,128)(2,1)}, bf16[768,1152]{1,0:T(8,128)(2,1)}, u32[]{:S(2)}, u32[]{:S(2)}) collective-permute-start(bf16[768,1152]{1,0:T(8,128)(2,1)} %all-gather.6.cloned.1.call-done.own.wo), channel_id=1, source_target_pairs={{0,4},{4,0},{8,12},{12,8},{16,20},{20,16},{24,28},{28,24},{1,5},{5... | collective-permute-start | bytes 5308424 | tf_op jit(solution)/shard_map/ppermute | solution.py:577
  106.2 48.7 %collective-permute-start.1 = (bf16[2,256,1536]{2,1,0:T(8,128)(2,1)}, bf16[2,256,1536]{2,1,0:T(8,128)(2,1)}, u32[]{:S(2)}, u32[]{:S(2)}) collective-permute-start(bf16[2,256,1536]{2,1,0:T(8,128)(2,1)} %p0.3), channel_id=1, source_target_pairs={{0,1},{1,0},{2,3},{3,2},{4,5},{5,4},{6,7},{7,6},{8,9},{9,8},{10,11... | collective-permute-start | bytes 4718600 | tf_op jit(solution)/shard_map/ppermute | solution.py:586
  106.2 48.7 %collective-permute-start.2 = (bf16[2,256,1536]{2,1,0:T(8,128)(2,1)}, bf16[2,256,1536]{2,1,0:T(8,128)(2,1)}, u32[]{:S(2)}, u32[]{:S(2)}) collective-permute-start(bf16[2,256,1536]{2,1,0:T(8,128)(2,1)} %collective-permute-done.p1), channel_id=1, source_target_pairs={{0,1},{1,0},{2,3},{3,2},{4,5},{5,4},{6,7},{7,6},{8,9},{9,8},{10,11... | collective-permute-start | bytes 4718600 | tf_op jit(solution)/shard_map/ppermute | solution.py:586
  215.0 203.9 %all-gather.12.cloned.1.call-start = ((), (), s32[]{:S(2)}) async-start(), calls=%async_computation.9 | async-start | bytes 2949120 | tf_op jit(solution)/shard_map/all_gather | solution.py:576
  326.8 105.0 %collective-permute-start.15 = (bf16[768,3072]{1,0:T(8,128)(2,1)}, bf16[768,3072]{1,0:T(8,128)(2,1)}, u32[]{:S(2)}, u32[]{:S(2)}) collective-permute-start(bf16[768,3072]{1,0:T(8,128)(2,1)} %all-gather.10.cloned.1.call-done.go.uo), channel_id=1, source_target_pairs={{0,4},{4,0},{8,12},{12,8},{16,20},{20,16},{24,28},{28,24},{1,5},{5... | collective-permute-start | bytes 14155784 | tf_op jit(solution)/shard_map/ppermute | solution.py:577
  337.7 81.2 %collective-permute-start.31 = (bf16[2,256,1536]{2,1,0:T(8,128)(2,1)}, bf16[2,256,1536]{2,1,0:T(8,128)(2,1)}, u32[]{:S(2)}, u32[]{:S(2)}) collective-permute-start(bf16[2,256,1536]{2,1,0:T(8,128)(2,1)} %get-tuple-element.241.p0), channel_id=1, source_target_pairs={{0,2},{1,3},{2,0},{3,1},{4,6},{5,7},{6,4},{7,5},{8,10},{9,11},{10,... | collective-permute-start | bytes 4718600 | tf_op jit(solution)/shard_map/ppermute | solution.py:589
  339.1 748.7 %reduce-scatter.13.cloned.1.call-start = ((), (), s32[]{:S(2)}) async-start(), calls=%async_computation.12 | async-start | bytes 2949120 | tf_op jit(solution)/shard_map/reduce_scatter | solution.py:581
  372.7 46.2 %collective-permute-start.12 = (bf16[256,1536]{1,0:T(8,128)(2,1)}, bf16[256,1536]{1,0:T(8,128)(2,1)}, u32[]{:S(2)}, u32[]{:S(2)}) collective-permute-start(bf16[256,1536]{1,0:T(8,128)(2,1)} %get-tuple-element.267.p0.refs_0_), channel_id=1, source_target_pairs={{0,2},{1,3},{2,0},{3,1},{4,6},{5,7},{6,4},{7,5},{8,10},{9,11},{10,... | collective-permute-start | bytes 2359304 | tf_op jit(solution)/shard_map/ppermute | solution.py:589
  374.1 57.6 %collective-permute-start.13 = (bf16[256,1536]{1,0:T(8,128)(2,1)}, bf16[256,1536]{1,0:T(8,128)(2,1)}, u32[]{:S(2)}, u32[]{:S(2)}) collective-permute-start(bf16[256,1536]{1,0:T(8,128)(2,1)} %get-tuple-element.267.p0.refs_0_), channel_id=1, source_target_pairs={{0,1},{1,0},{2,3},{3,2},{4,5},{5,4},{6,7},{7,6},{8,9},{9,8},{10,11... | collective-permute-start | bytes 2359304 | tf_op jit(solution)/shard_map/ppermute | solution.py:586
  374.1 60.9 %collective-permute-start.26 = (bf16[256,1536]{1,0:T(8,128)(2,1)}, bf16[256,1536]{1,0:T(8,128)(2,1)}, u32[]{:S(2)}, u32[]{:S(2)}) collective-permute-start(bf16[256,1536]{1,0:T(8,128)(2,1)} %get-tuple-element.268.p0.refs_4_), channel_id=1, source_target_pairs={{0,2},{1,3},{2,0},{3,1},{4,6},{5,7},{6,4},{7,5},{8,10},{9,11},{10,... | collective-permute-start | bytes 2359304 | tf_op jit(solution)/shard_map/ppermute | solution.py:589
  418.9 63.0 %collective-permute-start.16 = (bf16[768,1536]{1,0:T(8,128)(2,1)}, bf16[768,1536]{1,0:T(8,128)(2,1)}, u32[]{:S(2)}, u32[]{:S(2)}) collective-permute-start(bf16[768,1536]{1,0:T(8,128)(2,1)} %all-gather.12.cloned.1.call-done.own.do), channel_id=1, source_target_pairs={{0,4},{4,0},{8,12},{12,8},{16,20},{20,16},{24,28},{28,24},{1,5},{5... | collective-permute-start | bytes 7077896 | tf_op jit(solution)/shard_map/ppermute | solution.py:577
  552.8 53.1 %collective-permute-start.60 = (bf16[768,1536]{1,0:T(8,128)(2,1)}, bf16[768,1536]{1,0:T(8,128)(2,1)S(1)}, u32[]{:S(2)}, u32[]{:S(2)}) collective-permute-start(bf16[768,1536]{1,0:T(8,128)(2,1)} %get-tuple-element.153), channel_id=1, source_target_pairs={{0,4},{4,0},{8,12},{12,8},{16,20},{20,16},{24,28},{28,24},{1,5},{5... | collective-permute-start | bytes 7077896 | tf_op jit(solution)/shard_map/ppermute | solution.py:580
  607.9 479.9 %reduce-scatter.15.cloned.1.call-start = ((), (), s32[]{:S(2)}) async-start(), calls=%async_computation.13 | async-start | bytes 2949120 | tf_op jit(solution)/shard_map/reduce_scatter | solution.py:581
  617.9 50.5 %collective-permute-start.17 = (bf16[512,1536]{1,0:T(8,128)(2,1)}, bf16[512,1536]{1,0:T(8,128)(2,1)S(1)}, u32[]{:S(2)}, u32[]{:S(2)}) collective-permute-start(bf16[512,1536]{1,0:T(8,128)(2,1)} %get-tuple-element.94), channel_id=1, source_target_pairs={{0,1},{1,0},{2,3},{3,2},{4,5},{5,4},{6,7},{7,6},{8,9},{9,8},{10,11... | collective-permute-start | bytes 4718600 | tf_op jit(solution)/shard_map/ppermute | solution.py:586
  636.8 54.4 %collective-permute-start.61 = (bf16[768,1536]{1,0:T(8,128)(2,1)}, bf16[768,1536]{1,0:T(8,128)(2,1)}, u32[]{:S(2)}, u32[]{:S(2)}) collective-permute-start(bf16[768,1536]{1,0:T(8,128)(2,1)} %get-tuple-element.157), channel_id=1, source_target_pairs={{0,4},{4,0},{8,12},{12,8},{16,20},{20,16},{24,28},{28,24},{1,5},{5... | collective-permute-start | bytes 7077896 | tf_op jit(solution)/shard_map/ppermute | solution.py:580
  667.7 138.2 %collective-permute-start.62 = (bf16[768,1536]{1,0:T(8,128)(2,1)}, bf16[768,1536]{1,0:T(8,128)(2,1)}, u32[]{:S(2)}, u32[]{:S(2)}) collective-permute-start(bf16[768,1536]{1,0:T(8,128)(2,1)} %get-tuple-element.159), channel_id=1, source_target_pairs={{0,4},{4,0},{8,12},{12,8},{16,20},{20,16},{24,28},{28,24},{1,5},{5... | collective-permute-start | bytes 7077896 | tf_op jit(solution)/shard_map/ppermute | solution.py:580
  677.1 49.0 %collective-permute-start.30 = (bf16[256,1536]{1,0:T(8,128)(2,1)}, bf16[256,1536]{1,0:T(8,128)(2,1)}, u32[]{:S(2)}, u32[]{:S(2)}) collective-permute-start(bf16[256,1536]{1,0:T(8,128)(2,1)} %add_convert_fusion.6), channel_id=1, source_target_pairs={{0,2},{1,3},{2,0},{3,1},{4,6},{5,7},{6,4},{7,5},{8,10},{9,11},{10,... | collective-permute-start | bytes 2359304 | tf_op jit(solution)/shard_map/ppermute | solution.py:589
  691.2 51.4 %collective-permute-start.47 = (bf16[256,1536]{1,0:T(8,128)(2,1)}, bf16[256,1536]{1,0:T(8,128)(2,1)}, u32[]{:S(2)}, u32[]{:S(2)}) collective-permute-start(bf16[256,1536]{1,0:T(8,128)(2,1)} %add_convert_fusion.2), channel_id=1, source_target_pairs={{0,2},{1,3},{2,0},{3,1},{4,6},{5,7},{6,4},{7,5},{8,10},{9,11},{10,... | collective-permute-start | bytes 2359304 | tf_op jit(solution)/shard_map/ppermute | solution.py:589
  696.3 394.3 %reduce-scatter.17.cloned.1.call-start = ((), (), s32[]{:S(2)}) async-start(), calls=%async_computation.14 | async-start | bytes 2949120 | tf_op jit(solution)/shard_map/reduce_scatter | solution.py:581
  805.4 42.8 %collective-permute-start.39 = (bf16[512,1536]{1,0:T(8,128)(2,1)}, bf16[512,1536]{1,0:T(8,128)(2,1)}, u32[]{:S(2)}, u32[]{:S(2)}) collective-permute-start(bf16[512,1536]{1,0:T(8,128)(2,1)} %get-tuple-element.111), channel_id=1, source_target_pairs={{0,1},{1,0},{2,3},{3,2},{4,5},{5,4},{6,7},{7,6},{8,9},{9,8},{10,11... | collective-permute-start | bytes 4718600 | tf_op jit(solution)/shard_map/ppermute | solution.py:586
  809.7 283.2 %reduce-scatter.11.cloned.1.call-start = ((), (), s32[]{:S(2)}) async-start(), calls=%async_computation.11 | async-start | bytes 2211840 | tf_op jit(solution)/shard_map/reduce_scatter | solution.py:581
  851.3 60.0 %collective-permute-start.59 = (bf16[768,1152]{1,0:T(8,128)(2,1)S(1)}, bf16[768,1152]{1,0:T(8,128)(2,1)S(1)}, u32[]{:S(2)}, u32[]{:S(2)}) collective-permute-start(bf16[768,1152]{1,0:T(8,128)(2,1)S(1)} %pad_maximum_fusion.2), channel_id=1, source_target_pairs={{0,4},{4,0},{8,12},{12,8},{16,20},{20,16},{24,28},{28,24},{1,5},{5... | collective-permute-start | bytes 5308424 | tf_op jit(solution)/shard_map/ppermute | solution.py:580
  913.0 249.6 %reduce-scatter.19.cloned.1.call-start = ((), (), s32[]{:S(2)}) async-start(), calls=%async_computation.15 | async-start | bytes 811008
  913.1 50.7 %collective-permute-start.54 = (bf16[256,1536]{1,0:T(8,128)(2,1)}, bf16[256,1536]{1,0:T(8,128)(2,1)S(1)}, u32[]{:S(2)}, u32[]{:S(2)}) collective-permute-start(bf16[256,1536]{1,0:T(8,128)(2,1)} %get-tuple-element.216.p0.refs_4_), channel_id=1, source_target_pairs={{0,1},{1,0},{2,3},{3,2},{4,5},{5,4},{6,7},{7,6},{8,9},{9,8},{10,11... | collective-permute-start | bytes 2359304 | tf_op jit(solution)/shard_map/ppermute | solution.py:586
  963.2 65.2 %collective-permute-start.44 = (bf16[512,1536]{1,0:T(8,128)(2,1)}, bf16[512,1536]{1,0:T(8,128)(2,1)S(1)}, u32[]{:S(2)}, u32[]{:S(2)}) collective-permute-start(bf16[512,1536]{1,0:T(8,128)(2,1)} %get-tuple-element.117), channel_id=1, source_target_pairs={{0,1},{1,0},{2,3},{3,2},{4,5},{5,4},{6,7},{7,6},{8,9},{9,8},{10,11... | collective-permute-start | bytes 4718600 | tf_op jit(solution)/shard_map/ppermute | solution.py:586
  1026.9 54.0 %collective-permute-start.58 = (bf16[768,1536]{1,0:T(8,128)(2,1)}, bf16[768,1536]{1,0:T(8,128)(2,1)}, u32[]{:S(2)}, u32[]{:S(2)}) collective-permute-start(bf16[768,1536]{1,0:T(8,128)(2,1)} %pad_maximum_fusion.1), channel_id=1, source_target_pairs={{0,4},{4,0},{8,12},{12,8},{16,20},{20,16},{24,28},{28,24},{1,5},{5... | collective-permute-start | bytes 7077896 | tf_op jit(solution)/shard_map/ppermute | solution.py:580
  1069.0 143.0 %reduce-scatter.9.cloned.1.call-start = ((), (), s32[]{:S(2)}) async-start(), calls=%async_computation.10 | async-start | bytes 2949120 | tf_op jit(solution)/shard_map/reduce_scatter | solution.py:581
  (149 other events, 2562.4 us)
Sparse Core Ops, SparseCore 0:
  10.2 53.1 all-gather.7
  65.5 39.1 all-gather.5
  215.1 88.2 all-gather.9
  339.2 47.7 all-gather.11
  608.0 46.9 reduce-scatter.12
  696.4 46.1 reduce-scatter.14
  809.8 46.9 reduce-scatter.16
  913.1 37.3 reduce-scatter.10
  1069.1 93.4 reduce-scatter.18
  1164.8 47.1 reduce-scatter.8

commit v2 on v1

v2 whole, which is shorter than its diff:
```python
import functools
import math

import jax
import jax.numpy as jnp
from jax import lax
from jax.experimental import pallas as pl
from jax.experimental.pallas import tpu as pltpu
from jax.sharding import PartitionSpec as P

HEAD_WIDTH = 64
ROT = 32
EPS = 1e-05
BF = jnp.bfloat16
F32 = jnp.float32
LOG2E = math.log2(math.e)
VMEM_BYTES = 56 * 1024 * 1024


def call(kernel, outs, grid, in_specs, out_specs, scratch, flops, moved, operands):
    return pl.pallas_call(
        kernel,
        out_shape=outs,
        grid=grid,
        in_specs=in_specs,
        out_specs=out_specs,
        scratch_shapes=scratch,
        compiler_params=pltpu.CompilerParams(vmem_limit_bytes=VMEM_BYTES),
        cost_estimate=pl.CostEstimate(flops=flops * 3, bytes_accessed=moved, transcendentals=0),
    )(*operands)


def after(value, *others):
    return lax.optimization_barrier((value, *others))[0]


def shape(dims, kind=BF):
    return jax.ShapeDtypeStruct(dims, kind)


def whole(dims):
    return pl.BlockSpec(dims, lambda *_: (0,) * len(dims))


SMEM = pl.BlockSpec(memory_space=pltpu.SMEM)


def dot_nn(a, b):
    return jnp.dot(a, b, preferred_element_type=F32)


def dot_nt(a, b):
    return lax.dot_general(a, b, (((1,), (1,)), ((), ())), preferred_element_type=F32)


def dot_tn(a, b):
    return lax.dot_general(a, b, (((0,), (0,)), ((), ())), preferred_element_type=F32)


def assemble(parity, own, other, scratch):
    pairs, _, rows, width = scratch.shape
    scratch[:, pl.ds(parity, 1)] = own[...].reshape(pairs, 1, rows, width)
    scratch[:, pl.ds(1 - parity, 1)] = other[...].reshape(pairs, 1, rows, width)
    return scratch[...].reshape(pairs * 2 * rows, width)


def split_rows(parity, value, scratch, own, other, columns):
    pairs, _, rows, width = scratch.shape
    scratch[...] = value.reshape(scratch.shape)
    own[:, columns] = scratch[:, pl.ds(parity, 1)].reshape(pairs * rows, width)
    other[:, columns] = scratch[:, pl.ds(1 - parity, 1)].reshape(pairs * rows, width)


def rope(v, cosine, low_sine, high_sine, sign):
    width = v.shape[-1]
    half = ROT // 2
    ahead = pltpu.roll(v, width - half, 1)
    behind = pltpu.roll(v, half, 1)
    return v * cosine + sign * (behind * high_sine - ahead * low_sine)


def head_mask(h):
    lane = lax.broadcasted_iota(jnp.int32, (1, 2 * HEAD_WIDTH), 1)
    return (lane // HEAD_WIDTH) == h


def attend_rows(q_ref, k_ref, v_ref, att_ref, lse_scratch, valid, base=0):
    length, width = q_ref.shape
    keys = k_ref.shape[0]
    block = min(256, length)
    scale = HEAD_WIDTH**-0.5 * LOG2E
    lanes = 2 * HEAD_WIDTH

    def rows_step(i, _):
        rows = pl.ds(pl.multiple_of(i * block, block), block)
        lane = lax.broadcasted_iota(jnp.int32, (block, lanes), 1)
        sums = lse_scratch[rows, :]
        for pair in range(width // lanes):
            columns = slice(pair * lanes, (pair + 1) * lanes)
            q = q_ref[rows, columns]
            total = None
            for h in range(2):
                mask = head_mask(h)
                k = jnp.where(mask, k_ref[:, columns], jnp.zeros((), BF))
                v = jnp.where(mask, v_ref[:, columns], jnp.zeros((), BF))
                logits = dot_nt(q, k) * scale
                if valid < keys:
                    spot = lax.broadcasted_iota(jnp.int32, logits.shape, 1)
                    logits = jnp.where(spot < valid, logits, -jnp.inf)
                peak = jnp.max(logits, axis=1, keepdims=True)
                weights = jnp.exp2(logits - peak)
                norm = jnp.sum(weights, axis=1, keepdims=True)
                term = dot_nn(weights.astype(BF), v) / norm
                total = term if total is None else total + term
                sums = jnp.where(lane == base + pair * 2 + h, peak + jnp.log2(norm), sums)
            att_ref[rows, columns] = total.astype(BF)
        lse_scratch[rows, :] = sums
        return 0

    lax.fori_loop(0, length // block, rows_step, 0)


def attend_back(q_ref, k_ref, v_ref, att_ref, do_ref, lse_ref, dq_acc, put_k, put_v, put_q, valid, base=0):
    length, width = q_ref.shape
    keys = k_ref.shape[0]
    block = min(256, keys)
    scale = HEAD_WIDTH**-0.5
    lanes = 2 * HEAD_WIDTH
    for pair in range(width // lanes):
        columns = slice(pair * lanes, (pair + 1) * lanes)
        product = do_ref[:, columns].astype(F32) * att_ref[:, columns].astype(F32)
        deltas = []
        for h in range(2):
            ones = jnp.where(head_mask(h), 1.0, 0.0).astype(F32)
            deltas.append(
                lax.dot_general(
                    jnp.broadcast_to(ones, (8, lanes)),
                    product,
                    (((1,), (1,)), ((), ())),
                    preferred_element_type=F32,
                    precision=lax.Precision.HIGHEST,
                )[:1]
            )
        dq_acc[...] = jnp.zeros_like(dq_acc)

        def keys_step(i, _):
            rows = pl.ds(pl.multiple_of(i * block, block), block)
            dk_total, dv_total = None, None
            for h in range(2):
                mask = head_mask(h)
                zero = jnp.zeros((), BF)
                k = jnp.where(mask, k_ref[rows, columns], zero)
                v = jnp.where(mask, v_ref[rows, columns], zero)
                q = q_ref[:, columns]
                do = do_ref[:, columns]
                head = base + pair * 2 + h
                logits = dot_nt(k, q) * (scale * LOG2E)
                weights = jnp.exp2(logits - lse_ref[head : head + 1, :])
                if valid < keys:
                    spot = i * block + lax.broadcasted_iota(jnp.int32, weights.shape, 0)
                    weights = jnp.where(spot < valid, weights, 0.0)
                dp = dot_nt(v, do)
                ds = (weights * (dp - deltas[h])).astype(BF)
                dv = dot_nn(weights.astype(BF), jnp.where(mask, do, zero))
                dk = dot_nn(ds, jnp.where(mask, q, zero))
                dq_acc[...] += dot_tn(ds, k)
                dk_total = dk if dk_total is None else dk_total + dk
                dv_total = dv if dv_total is None else dv_total + dv
            put_k(rows, columns, dk_total * scale)
            put_v(rows, columns, dv_total)
            return 0

        lax.fori_loop(0, keys // block, keys_step, 0)
        put_q(columns, dq_acc[...] * scale)


def finish_sums(lse_scratch, lse_ref):
    lse_ref[...] = jnp.transpose(lse_scratch[...])[: lse_ref.shape[0]]


def row_norm(t):
    mean = jnp.mean(t, axis=-1, keepdims=True)
    centred = t - mean
    return centred * lax.rsqrt(jnp.mean(centred * centred, axis=-1, keepdims=True) + EPS)


def self_forward(parts, seq, gain, shift, w_full, cos, low, high, heads):
    part_rows, model = parts[0].shape[1:]
    length = part_rows * len(parts)
    width = heads * HEAD_WIDTH
    lanes = 2 * HEAD_WIDTH

    def kernel(p0, p1, p2, p3, g, b, weight, c_ref, l_ref, h_ref, normed, q, k, v, att, lse, sums):
        for i, part in enumerate((p0, p1, p2, p3)):
            rows = slice(i * part_rows, (i + 1) * part_rows)
            normed[rows, :] = (row_norm(part[0].astype(F32)) * g[...] + b[...]).astype(BF)
        for j, target in enumerate((q, k, v)):
            value = dot_nn(normed[...], weight[:, j * width : (j + 1) * width])
            if j == 2:
                target[...] = value.astype(BF)
                continue
            for pair in range(width // lanes):
                columns = slice(pair * lanes, (pair + 1) * lanes)
                target[:, columns] = rope(value[:, columns], c_ref[...], l_ref[...], h_ref[...], 1.0).astype(BF)
        sums[...] = jnp.zeros_like(sums)
        attend_rows(q, k, v, att, sums, length)
        finish_sums(sums, lse)

    part_spec = pl.BlockSpec((1, part_rows, model), lambda *_: (seq, 0, 0))
    table_spec = whole((length, lanes))
    return call(
        kernel,
        (shape((length, model)),) + (shape((length, width)),) * 4 + (shape((8, length), F32),),
        (1,),
        [part_spec] * 4 + [whole((1, model))] * 2 + [whole(w_full.shape)] + [table_spec] * 3,
        (whole((length, model)),) + (whole((length, width)),) * 4 + (whole((8, length)),),
        [pltpu.VMEM((length, lanes), F32)],
        2 * length * model * 3 * width + 4 * length * length * width,
        16_000_000,
        (*parts, gain, shift, w_full, cos, low, high),
    )


PAIRS = {}


def project(rows, w_full, column=0):
    length, width = rows.shape
    half_rows = length // 2
    model = w_full.shape[0]

    def kernel(a, weight, keep, send):
        send[...] = dot_nt(a[half_rows:, :], weight[...]).astype(BF)
        keep[...] = dot_nt(a[:half_rows, :], weight[...]).astype(BF)

    return call(
        kernel,
        (shape((half_rows, model)),) * 2,
        (1,),
        [whole((length, width)), pl.BlockSpec((model, width), lambda *_: (0, column))],
        (whole((half_rows, model)),) * 2,
        [],
        2 * length * width * model,
        length * (width + model) * 2 + model * width * 2,
        (rows, w_full),
    )


def norm_terms(t):
    mean = jnp.mean(t, axis=-1, keepdims=True)
    centred = t - mean
    inv = lax.rsqrt(jnp.mean(centred * centred, axis=-1, keepdims=True) + EPS)
    return centred * inv, inv


def add_terms(refs):
    total = refs[0][...].astype(F32)
    for ref in refs[1:]:
        total = total + ref[...].astype(F32)
    return total


def cross_forward(tokens, seq, terms, norms, weights, kv, valid):
    rows, model = terms[2].shape
    parts = len(weights)
    width = weights[0].shape[1] // 2
    count = kv.shape[3]
    lanes = 2 * HEAD_WIDTH
    heads = width // HEAD_WIDTH
    lse_rows = -(-parts * heads // 8) * 8

    def kernel(t, a, b, c, n_ref, w0, w1, w2, w3, kv_ref, first, second, normed2, normed3, q, att, lse, sums):
        value = t[0].astype(F32) + add_terms((a, b, c))
        first[...] = value
        normed2[...] = (norm_terms(value)[0] * n_ref[1:2, :] + n_ref[4:5, :]).astype(BF)
        sums[...] = jnp.zeros_like(sums)
        total = value
        for p, w in enumerate((w0, w1, w2, w3)):
            columns = pl.ds(p * width, width)
            q[:, columns] = dot_nn(normed2[...], w[:, :width]).astype(BF)
            attend_rows(
                q.at[:, columns], kv_ref.at[p, 0, 0], kv_ref.at[p, 0, 1], att.at[:, columns], sums, valid, p * heads
            )
            total = total + dot_nt(att[:, columns], w[:, width:])
        second[...] = total
        normed3[...] = (norm_terms(total)[0] * n_ref[2:3, :] + n_ref[5:6, :]).astype(BF)
        finish_sums(sums, lse)

    rows_spec = whole((rows, model))
    return call(
        kernel,
        (shape((rows, model), F32),) * 2 + (shape((rows, model)),) * 4 + (shape((lse_rows, rows), F32),),
        (1,),
        [pl.BlockSpec((1, rows, model), lambda *_: (seq, 0, 0))]
        + [rows_spec] * 3
        + [whole(norms.shape)]
        + [whole(weights[0].shape)] * 4
        + [pl.BlockSpec((parts, 1, 2, count, width), lambda *_: (0, seq, 0, 0, 0))],
        (rows_spec,) * 6 + (whole((lse_rows, rows)),),
        [pltpu.VMEM((rows, lanes), F32)],
        4 * rows * model * parts * width + 4 * rows * count * parts * width,
        18_000_000,
        (tokens, *terms, norms, *weights, kv),
    )


def norm_pull(grad, t, gain):
    xhat, inv = norm_terms(t)
    scaled = grad * gain
    back = inv * (
        scaled
        - jnp.mean(scaled, axis=-1, keepdims=True)
        - xhat * jnp.mean(scaled * xhat, axis=-1, keepdims=True)
    )
    return back, jnp.sum(grad * xhat, axis=0, keepdims=True), jnp.sum(grad, axis=0, keepdims=True)


def cross_backward(third, seq, terms, second, first, norms, weights, kv, q, att, lse, valid):
    rows, model = terms[2].shape
    parts = len(weights)
    width = weights[0].shape[1] // 2
    count = kv.shape[3]
    lanes = 2 * HEAD_WIDTH
    heads = width // HEAD_WIDTH

    def kernel(
        t, a, b, c, s_ref, f_ref, n_ref, w0, w1, w2, w3, kv_ref, q_ref, a_ref, l_ref,
        d_first, dy2, dy1, dq, dkv, stats, do, acc,
    ):
        back, gain3, shift3 = norm_pull(add_terms((a, b, c)), s_ref[...], n_ref[2:3, :])
        d_second = t[0].astype(F32) + back
        dy2[...] = d_second.astype(BF)
        d_normed2 = None
        for p, w in enumerate((w0, w1, w2, w3)):
            columns = pl.ds(p * width, width)
            do[...] = dot_nn(dy2[...], w[:, width:]).astype(BF)

            def put_k(rows_at, at, value, p=p):
                dkv[p, 0, rows_at, at] = value.astype(BF)

            def put_v(rows_at, at, value, p=p):
                dkv[p, 1, rows_at, at] = value.astype(BF)

            def put_q(at, value, p=p):
                dq[:, slice(p * width + at.start, p * width + at.stop)] = value.astype(BF)

            attend_back(
                q_ref.at[:, columns], kv_ref.at[p, 0, 0], kv_ref.at[p, 0, 1], a_ref.at[:, columns], do, l_ref, acc,
                put_k, put_v, put_q, valid, p * heads,
            )
            term = dot_nt(dq[:, columns], w[:, :width])
            d_normed2 = term if d_normed2 is None else d_normed2 + term
        back, gain2, shift2 = norm_pull(d_normed2, f_ref[...], n_ref[1:2, :])
        value = d_second + back
        d_first[...] = value
        dy1[...] = value.astype(BF)
        stats[...] = jnp.concatenate([gain2, gain3, shift2, shift3, jnp.zeros((4, model), F32)], axis=0)

    rows_spec = whole((rows, model))
    return call(
        kernel,
        (shape((rows, model), F32),)
        + (shape((rows, model)),) * 3
        + (shape((parts, 2, count, width)), shape((8, model), F32)),
        (1,),
        [pl.BlockSpec((1, rows, model), lambda *_: (seq, 0, 0))]
        + [rows_spec] * 5
        + [whole(norms.shape)]
        + [whole(weights[0].shape)] * 4
        + [pl.BlockSpec((parts, 1, 2, count, width), lambda *_: (0, seq, 0, 0, 0))]
        + [rows_spec] * 2
        + [whole(lse.shape)],
        (rows_spec,) * 4 + (whole((parts, 2, count, width)), whole((8, model))),
        [pltpu.VMEM((rows, width), BF), pltpu.VMEM((rows, lanes), F32)],
        4 * rows * model * parts * width + 10 * rows * count * parts * width,
        24_000_000,
        (third, *terms, second, first, norms, *weights, kv, q, att, lse),
    )


def cross_weight_grad(parity, normed, dys, dqs, atts, parts):
    seqs = len(dys)
    rows, model = dys[0].shape
    width = model // parts
    pairs = PAIRS["pairs"]
    half = model // 2

    def kernel(par, *refs):
        n_refs, y_refs, q_refs, a_refs = (refs[i * seqs : (i + 1) * seqs] for i in range(4))
        outs = refs[4 * seqs : 4 * seqs + parts]
        scr = refs[-1]
        for p in range(parts):
            at = slice(p * width, (p + 1) * width)
            for j, (lefts, rights) in enumerate(((n_refs, q_refs), (y_refs, a_refs))):
                value = None
                for left, right in zip(lefts, rights):
                    term = dot_tn(left[...], right[:, at])
                    value = term if value is None else value + term
                scr[...] = value.astype(BF).reshape(scr.shape)
                columns = slice(j * width, (j + 1) * width)
                outs[p][0, :, columns] = scr[:, pl.ds(par[0], 1)].reshape(half, width)
                outs[p][1, :, columns] = scr[:, pl.ds(1 - par[0], 1)].reshape(half, width)

    return call(
        kernel,
        (shape((2, half, 2 * width)),) * parts,
        (1,),
        [SMEM] + [whole((rows, model))] * (4 * seqs),
        (whole((2, half, 2 * width)),) * parts,
        [pltpu.VMEM((pairs, 2, half // pairs, width), BF)],
        4 * seqs * rows * model * model,
        16_000_000,
        (parity, *normed, *dys, *dqs, *atts),
    )


def gate_forward(parts, weights):
    part_rows, model = parts[0].shape
    length = part_rows * len(parts)
    hidden = weights.shape[2]
    block = 512
    steps = hidden // block

    def kernel(p0, p1, p2, p3, wg, wu, gate, up, act):
        for i, part in enumerate((p0, p1, p2, p3)):
            rows = slice(i * part_rows, (i + 1) * part_rows)
            g = dot_nn(part[...], wg[0])
            u = dot_nn(part[...], wu[0])
            gate[rows, :] = g.astype(BF)
            up[rows, :] = u.astype(BF)
            act[rows, :] = (g / (1.0 + jnp.exp2(-LOG2E * g)) * u).astype(BF)

    g_spec = pl.BlockSpec((1, model, block), lambda j: (0, 0, j))
    u_spec = pl.BlockSpec((1, model, block), lambda j: (1, 0, j))
    out_spec = pl.BlockSpec((length, block), lambda j: (0, j))
    return call(
        kernel,
        (shape((length, hidden)),) * 3,
        (steps,),
        [whole((part_rows, model))] * 4 + [g_spec, u_spec],
        (out_spec,) * 3,
        [],
        4 * length * model * hidden,
        22_000_000,
        (*parts, weights, weights),
    )


def gate_backward(parts, seq, gate, up, w_down, weights):
    part_rows, model = parts[0].shape[1:]
    length = part_rows * len(parts)
    half_rows = length // 2
    hidden = gate.shape[1]
    block = 512
    steps = hidden // block

    def kernel(p0, p1, p2, p3, g_ref, u_ref, wd, wg, wu, dgate, dup, keep, send, acc):
        j = pl.program_id(0)

        @pl.when(j == 0)
        def _():
            acc[...] = jnp.zeros_like(acc)

        for i, part in enumerate((p0, p1, p2, p3)):
            rows = slice(i * part_rows, (i + 1) * part_rows)
            d_hidden = dot_nn(part[0], wd[...])
            g = g_ref[rows, :].astype(F32)
            u = u_ref[rows, :].astype(F32)
            sig = 1.0 / (1.0 + jnp.exp2(-LOG2E * g))
            d_gate = (d_hidden * u * sig * (1.0 + g * (1.0 - sig))).astype(BF)
            d_up = (d_hidden * (g * sig)).astype(BF)
            dgate[rows, :] = d_gate
            dup[rows, :] = d_up
            acc[rows, :] += dot_nt(d_gate, wg[0]) + dot_nt(d_up, wu[0])

        @pl.when(j == steps - 1)
        def _():
            keep[...] = acc[:half_rows, :].astype(BF)
            send[...] = acc[half_rows:, :].astype(BF)

    part_spec = pl.BlockSpec((1, part_rows, model), lambda *_: (seq, 0, 0))
    act_spec = pl.BlockSpec((length, block), lambda j: (0, j))
    w_spec = pl.BlockSpec((model, block), lambda j: (0, j))
    g_spec = pl.BlockSpec((1, model, block), lambda j: (0, 0, j))
    u_spec = pl.BlockSpec((1, model, block), lambda j: (1, 0, j))
    return call(
        kernel,
        (shape((length, hidden)),) * 2 + (shape((half_rows, model)),) * 2,
        (steps,),
        [part_spec] * 4 + [act_spec] * 2 + [w_spec, g_spec, u_spec],
        (act_spec,) * 2 + (whole((half_rows, model)),) * 2,
        [pltpu.VMEM((length, model), F32)],
        6 * length * model * hidden,
        33_000_000,
        (*parts, gate, up, w_down, weights, weights),
    )


def self_backward(parts, o_full, w_full, q, k, v, att, lse, cos, low, high):
    part_rows, model = parts[0].shape
    length = part_rows * len(parts)
    half_rows = length // 2
    width = q.shape[1]
    lanes = 2 * HEAD_WIDTH

    def kernel(
        p0, p1, p2, p3, o_ref, w_ref, q_ref, k_ref, v_ref, a_ref, l_ref, c_ref, lo_ref, h_ref,
        grads, keep, send, do, acc,
    ):
        for i, part in enumerate((p0, p1, p2, p3)):
            do[i * part_rows : (i + 1) * part_rows, :] = dot_nn(part[...], o_ref[...]).astype(BF)

        def put_k(rows, columns, value):
            value = rope(value, c_ref[rows, :], lo_ref[rows, :], h_ref[rows, :], -1.0)
            grads[rows, slice(width + columns.start, width + columns.stop)] = value.astype(BF)

        def put_v(rows, columns, value):
            grads[rows, slice(2 * width + columns.start, 2 * width + columns.stop)] = value.astype(BF)

        def put_q(columns, value):
            grads[:, columns] = rope(value, c_ref[...], lo_ref[...], h_ref[...], -1.0).astype(BF)

        attend_back(q_ref, k_ref, v_ref, a_ref, do, l_ref, acc, put_k, put_v, put_q, length)
        send[...] = dot_nt(grads[half_rows:, :], w_ref[...]).astype(BF)
        keep[...] = dot_nt(grads[:half_rows, :], w_ref[...]).astype(BF)

    o_spec = pl.BlockSpec((model, width), lambda *_: (0, 2))
    rows_spec = whole((length, width))
    return call(
        kernel,
        (shape((length, 3 * width)),) + (shape((half_rows, model)),) * 2,
        (1,),
        [whole((part_rows, model))] * 4
        + [o_spec]
        + [whole(w_full.shape)]
        + [rows_spec] * 4
        + [whole((8, length))]
        + [whole((length, lanes))] * 3,
        (whole((length, 3 * width)),) + (whole((half_rows, model)),) * 2,
        [
            pltpu.VMEM((length, width), BF),
            pltpu.VMEM((length, lanes), F32),
        ],
        8 * length * model * width + 10 * length * length * width,
        24_000_000,
        (*parts, o_full, w_full, q, k, v, att, lse, cos, low, high),
    )


def weight_grad(parity, lefts, rights, block, first=0, steps=None):
    model = lefts[0].shape[-1]
    steps = steps or rights[0].shape[1] // block
    total = steps * block
    pairs = PAIRS["pairs"]
    count = len(lefts)
    half = model // 2
    length = sum(left.shape[0] for left in lefts)

    def kernel(par, *refs):
        left_refs = refs[:count]
        right_refs = refs[count : count + len(rights)]
        own, other, rows_scr, scr = refs[count + len(rights) :]

        @pl.when(pl.program_id(0) == 0)
        def _():
            start = 0
            for left in left_refs:
                rows_scr[start : start + left.shape[0], :] = left[...]
                start += left.shape[0]

        start = 0
        value = None
        for right in right_refs:
            term = dot_tn(rows_scr[start : start + right.shape[0], :], right[...])
            value = term if value is None else value + term
            start += right.shape[0]
        split_rows(par[0], value.astype(BF), scr, own, other, slice(None))

    left_specs = [whole(left.shape) for left in lefts]
    right_specs = [pl.BlockSpec((right.shape[0], block), lambda j: (0, first + j)) for right in rights]
    return call(
        kernel,
        (shape((half, total)),) * 2,
        (steps,),
        [SMEM] + left_specs + right_specs,
        (pl.BlockSpec((half, block), lambda j: (0, j)),) * 2,
        [pltpu.VMEM((length, model), BF), pltpu.VMEM((pairs, 2, model // (2 * pairs), block), BF)],
        2 * length * model * total,
        length * (model + total) * 2 + model * total * 2,
        (parity, *lefts, *rights),
    )


def make_body(dp, group):
    pairs = dp // 2
    swap = [(i, i ^ 1) for i in range(dp)]
    lines = [list(range(0, dp, 2)), list(range(1, dp, 2))]
    over_core = [(i, i ^ 1) for i in range(group)]
    over_x = [(i, i ^ 2) for i in range(group)]

    def body(
        tokens,
        context,
        positions,
        seq_mask,
        cotangent,
        norm_gains,
        norm_shifts,
        w_qkv,
        w_self_out,
        w_cross_q,
        w_cross_kv,
        w_cross_out,
        w_gate_up,
        w_down,
    ):
        PAIRS["pairs"] = pairs
        rank = lax.axis_index("dp")
        spot = lax.axis_index("tensor")
        parity = (rank % 2).astype(jnp.int32).reshape(1)
        seqs, part_rows, model = tokens.shape
        length = positions.shape[1]
        ctx_len = context.shape[1]
        rows = w_qkv.shape[1]
        width = w_qkv.shape[2]
        heads = width // HEAD_WIDTH
        hidden = w_down.shape[0]
        ctx_rows = w_cross_kv.shape[1]

        turns = {}

        def in_turn(axis, v, pairs_of, name):
            if axis in turns:
                v = after(v, turns[axis])
            turns[axis] = lax.ppermute(v, name, pairs_of)
            return turns[axis]

        def fetch_all(local):
            return lax.all_gather(local, "dp", axis=0, tiled=True)

        def pair_sum(own, other, *ready):
            got = in_turn("y", other, swap, "dp")
            return own + after(got, *ready)

        def line_sum(v):
            return lax.psum_scatter(v, "dp", scatter_dimension=0, tiled=True, axis_index_groups=lines).astype(F32)

        def core(v):
            return lax.ppermute(v, "tensor", over_core)

        def across(v):
            return in_turn("x", v, over_x, "tensor")

        def spread(own):
            far = across(own)
            return (own, far, core(own), core(far))

        def reduce_rows(keep, send):
            got = core(send)
            far = (keep[part_rows:].astype(F32) + got[part_rows:].astype(F32)).astype(BF)
            return keep, got, across(far)

        def gather_sum(keep, got, back):
            return keep[:part_rows].astype(F32) + got[:part_rows].astype(F32) + back.astype(F32)

        def reduce_parts(own, far, near, both):
            own = (own.astype(F32) + core(near).astype(F32)).astype(BF)
            far = (far.astype(F32) + core(both).astype(F32)).astype(BF)
            return own, across(far)

        def total_of(v):
            for bit in range((group - 1).bit_length()):
                v = v + lax.ppermute(v, "tensor", [(i, i ^ (1 << bit)) for i in range(group)])
            for bit in range((dp - 1).bit_length()):
                v = v + lax.ppermute(v, "dp", [(i, i ^ (1 << bit)) for i in range(dp)])
            return v

        place = rank * group + spot
        mine = jnp.concatenate([norm_gains, norm_shifts], axis=0)
        share = mine.shape[1]
        norms = total_of(lax.dynamic_update_slice(jnp.zeros((6, model), F32), mine, (0, place * share)))
        gains = [norms[j : j + 1] for j in range(3)]
        shifts = [norms[3 + j : 4 + j] for j in range(3)]
        keep_scale = seq_mask.astype(F32)[:, None, None]
        grad_third = cotangent.astype(F32) * keep_scale
        token_parts = spread(after(tokens, norms))
        third_parts = spread(after(grad_third.astype(BF), token_parts[1]))

        w_one = jnp.transpose(w_qkv, (1, 0, 2)).reshape(rows, 3 * width)
        qkv_full = fetch_all(w_one)
        w_two = jnp.concatenate(
            [w_cross_q, w_cross_out.T, w_self_out.T, w_cross_kv.reshape(rows, width)], axis=1
        )
        two_full = fetch_all(after(w_two, qkv_full, token_parts[1]))

        order = jnp.stack([spot, spot ^ 2, spot ^ 1, spot ^ 3])
        half_rot = ROT // 2
        lane = jnp.arange(2 * HEAD_WIDTH) % HEAD_WIDTH
        inverse = jnp.exp((lane % half_rot).astype(F32) * (-2.0 * math.log(10000.0) / ROT))
        tables = []
        for s in range(seqs):
            spots = jnp.take(positions[s].reshape(group, part_rows), order, axis=0).reshape(length)
            angles = spots.astype(F32)[:, None] * inverse[None, :]
            turned = lane < ROT
            sine = jnp.sin(angles)
            tables.append(
                (
                    jnp.where(turned, jnp.cos(angles), 1.0),
                    jnp.where(lane < half_rot, sine, 0.0),
                    jnp.where((lane >= half_rot) & turned, sine, 0.0),
                )
            )

        state = [dict() for _ in range(seqs)]
        for s in range(seqs):
            st = state[s]
            gain = gains[0]
            if s > 0:
                gain = after(gain, state[0]["att"], third_parts[1])
            st["normed1"], st["q"], st["k"], st["v"], st["att"], st["lse"] = self_forward(
                token_parts, s, gain, shifts[0], qkv_full, *tables[s], heads
            )
        last = state[seqs - 1]["att"]
        two_full = after(two_full, last)
        gu_full = lax.all_gather(after(w_gate_up, two_full), "dp", axis=1, tiled=True)
        cross_full = two_full[:, : 2 * width]

        ctx_pad = -(-ctx_len // 128) * 128
        kv_weight = jnp.transpose(two_full[:, 3 * width :].reshape(dp, 2, ctx_rows, width), (1, 0, 2, 3))
        kv_weight = kv_weight.reshape(2, dp * ctx_rows, width)
        cross_kv = jnp.einsum("scd,kdh->skch", context, kv_weight, preferred_element_type=F32).astype(BF)
        cross_kv = jnp.stack(spread(cross_kv))
        cross_kv = jnp.pad(cross_kv, ((0, 0), (0, 0), (0, 0), (0, ctx_pad - ctx_len), (0, 0)))

        for s in range(seqs):
            st = state[s]
            st["terms"] = reduce_rows(*project(after(st["att"], last), two_full, 2))
            last = st["terms"][0]
        cross_parts = spread(cross_full)
        for s in range(seqs):
            st = state[s]
            terms = st["terms"]
            if s > 0:
                terms = (after(terms[0], gu_full), *terms[1:])
            st["first"], st["second"], st["normed2"], normed3, st["cq"], st["crossed"], st["clse"] = cross_forward(
                tokens, s, terms, norms, cross_parts, cross_kv, ctx_len
            )
            st["normed3"] = spread(normed3)
        dn_full = fetch_all(after(w_down.T, gu_full))
        for s in range(seqs):
            st = state[s]
            st["gate"], st["up"], st["hidden"] = gate_forward(st["normed3"], gu_full)
        third_lefts = [part[s] for s in range(seqs) for part in third_parts]
        dn_pair = weight_grad(parity, third_lefts, [st["hidden"] for st in state], 384)
        last = dn_pair[1]
        for s in range(seqs):
            st = state[s]
            st["dgate"], st["dup"], keep, send = gate_backward(
                third_parts, s, after(st["gate"], last), st["up"], dn_full, gu_full
            )
            last = keep
            st["d_normed3"] = reduce_rows(keep, send)
        dn_sum = pair_sum(*dn_pair, last)
        dn_grad = line_sum(dn_sum)
        normed3 = [p for st in state for p in st["normed3"]]
        gate_pair = weight_grad(parity, normed3, [after(st["dgate"], dn_sum) for st in state], 384)
        up_pair = weight_grad(parity, normed3, [after(st["dup"], gate_pair[1]) for st in state], 384)

        gain_grads, shift_grads = [0.0] * 3, [0.0] * 3
        last = up_pair[1]
        for s in range(seqs):
            st = state[s]
            st["d_first"], st["dy2"], dy1, st["dcq"], st["dkv"], stats = cross_backward(
                third_parts[0], s, st["d_normed3"], st["second"], after(st["first"], last), norms, cross_parts,
                cross_kv, st["cq"], st["crossed"], st["clse"], ctx_len,
            )
            last = dy1
            for j in range(1, 3):
                gain_grads[j] += stats[j - 1]
                shift_grads[j] += stats[j + 1]
            st["dy1"] = spread(dy1)
        gate_sum = pair_sum(*gate_pair, last)
        gate_part = line_sum(after(gate_sum, dn_grad))
        cross_terms = cross_weight_grad(
            parity,
            [after(st["normed2"], last, state[0]["dy1"][1]) for st in state],
            [st["dy2"] for st in state],
            [st["dcq"] for st in state],
            [st["crossed"] for st in state],
            group,
        )
        last = cross_terms[0]
        for s in range(seqs):
            st = state[s]
            st["out_terms"] = project(after(st["hidden"], last), dn_full)
            last = st["out_terms"][0]
        dkv_own, dkv_far = reduce_parts(*(jnp.stack([st["dkv"][p] for st in state]) for p in range(group)))
        cross_mine, cross_far = reduce_parts(*cross_terms)
        last = (last, dn_grad, gate_sum, *(p for st in state for p in st["dy1"]))
        for s in range(seqs):
            st = state[s]
            st["dqkv"], keep, send = self_backward(
                st["dy1"], two_full, qkv_full,
                after(st["q"], *last), st["k"], st["v"], st["att"], st["lse"], *tables[s],
            )
            last = keep
            st["d_normed1"] = (keep, send)
            if s > 0:
                continue
            up_sum = pair_sum(*up_pair, last)
            up_part = line_sum(after(up_sum, gate_part))
            so_pair = weight_grad(
                parity,
                [p for st in state for p in st["dy1"]],
                [after(st["att"], last, gate_part) for st in state],
                width,
            )
            dkv = (dkv_own.astype(F32) + after(dkv_far, last).astype(F32)).astype(BF)[:, :, :ctx_len]
            kv_grad = jnp.einsum("scd,skch->kdh", context, dkv, preferred_element_type=F32).astype(BF)
            kv_grad = jnp.transpose(kv_grad.reshape(2, pairs, 2, ctx_rows, width), (1, 2, 0, 3, 4))
            even = parity[0] == 0
            kv_mine = jnp.where(even, kv_grad[:, 0], kv_grad[:, 1]).reshape(pairs * rows, width)
            kv_other = jnp.where(even, kv_grad[:, 1], kv_grad[:, 0]).reshape(pairs * rows, width)
            cross_sum = cross_mine + after(cross_far, so_pair)
            middle_pair = [
                jnp.concatenate(v, axis=1)
                for v in ((cross_sum[0], kv_mine, so_pair[0]), (cross_sum[1], kv_other, so_pair[1]))
            ]
            last = (up_sum, *middle_pair)
        middle_sum = pair_sum(*middle_pair, keep)
        normed1 = [st["normed1"] for st in state]
        qkv_pairs = []
        for first, steps in ((0, 1), (1, 2)):
            ready = qkv_pairs[0][1] if first else up_part
            dqkv = [after(st["dqkv"], ready) for st in state]
            qkv_pairs.append(weight_grad(parity, normed1, dqkv, width, first, steps))
        middle = line_sum(after(middle_sum, up_part))
        for st in state:
            st["out_terms"] = reduce_rows(*st["out_terms"])
        for st in state:
            st["d_normed1"] = reduce_rows(*st["d_normed1"])
        q_part = line_sum(after(pair_sum(*qkv_pairs[0], qkv_pairs[1][0]), middle))
        kv_part = line_sum(after(pair_sum(*qkv_pairs[1], *(st["d_normed1"][2] for st in state)), q_part))
        qkv_part = jnp.concatenate([q_part, kv_part], axis=1)
        outs = []
        for s in range(seqs):
            st = state[s]
            third = st["second"] + gather_sum(*st["out_terms"])
            outs.append((third * keep_scale[s]).astype(BF))
        grad_inputs = []
        for s in range(seqs):
            st = state[s]
            xhat, inv = norm_parts(tokens[s].astype(F32))
            back, gain_term, shift_term = norm_back(
                gather_sum(*(after(v, qkv_pairs[1][1]) for v in st["d_normed1"])), xhat, inv, gains[0]
            )
            gain_grads[0] += gain_term
            shift_grads[0] += shift_term
            grad_inputs.append(st["d_first"] + back)
        norm_grads = lax.dynamic_slice(
            total_of(jnp.stack(gain_grads + shift_grads)), (0, place * share), (6, share)
        )
        return (
            jnp.stack(outs),
            jnp.stack(grad_inputs),
            norm_grads[:3],
            norm_grads[3:],
            jnp.transpose(qkv_part.reshape(rows, 3, width), (1, 0, 2)),
            middle[:, 3 * width :].T,
            middle[:, :width],
            middle[:, 2 * width : 3 * width].reshape(2, ctx_rows, width),
            middle[:, width : 2 * width].T,
            jnp.stack([gate_part, up_part]),
            dn_grad.T,
        )

    return body


def norm_parts(rows):
    mean = jnp.mean(rows, axis=-1, keepdims=True)
    centred = rows - mean
    inv = lax.rsqrt(jnp.mean(centred * centred, axis=-1, keepdims=True) + EPS)
    return centred * inv, inv


def norm_back(grad, xhat, inv, gain):
    scaled = grad * gain
    back = inv * (
        scaled
        - jnp.mean(scaled, axis=-1, keepdims=True)
        - xhat * jnp.mean(scaled * xhat, axis=-1, keepdims=True)
    )
    return back, jnp.sum(grad * xhat, axis=0), jnp.sum(grad, axis=0)


def solution(mesh):
    in_specs = (
        P("dp", "tensor", None),
        P("dp", None, None),
        P("dp", None),
        P("dp"),
        P("dp", "tensor", None),
        P(None, ("dp", "tensor")),
        P(None, ("dp", "tensor")),
        P(None, "dp", "tensor"),
        P("tensor", "dp"),
        P("dp", "tensor"),
        P(None, "dp", "tensor"),
        P("tensor", "dp"),
        P(None, "dp", "tensor"),
        P("tensor", "dp"),
    )
    out_specs = (
        P("dp", "tensor", None),
        P("dp", "tensor", None),
        P(None, ("dp", "tensor")),
        P(None, ("dp", "tensor")),
        P(None, "dp", "tensor"),
        P("tensor", "dp"),
        P("dp", "tensor"),
        P(None, "dp", "tensor"),
        P("tensor", "dp"),
        P(None, "dp", "tensor"),
        P("tensor", "dp"),
    )
    body = make_body(mesh.shape["dp"], mesh.shape["tensor"])
    return jax.shard_map(body, mesh=mesh, in_specs=in_specs, out_specs=out_specs, check_vma=False)
```

time: 1230 us -> 889 us (0.72)
  waiting for transfers between devices: 587 us -> 291 us
  blocking collectives: 39.6 us -> 0 us
  other arithmetic: 108 us -> 83.7 us
  Pallas kernels: 385 us -> 400 us
    ppermute x31 -> x34, waiting for transfers between devices: 389 us -> 249 us  [the longest x24 220 us: in_turn(): turns[axis] = lax.ppermute(v, name, pairs_of)]
    unnamed x11 -> x10, waiting for transfers between devices: 60.7 us -> 0.16 us
    all_gather x4, waiting for transfers between devices: 90 us -> 36.2 us  [the longest x3 36.2 us: fetch_all(): return lax.all_gather(local, 'dp', axis=0, tiled=True)]
    reduce_scatter x5 -> x6, waiting for transfers between devices: 47.2 us -> 1.66 us  [line_sum(): lax.psum_scatter(v, 'dp', scatter_dimension=0, tiled=True, axis_index_gro...]
    all_gather x1 -> x0, blocking collectives: 39.6 us -> none  [body(): lax.all_gather(jnp.concatenate([norm_gains, norm_shifts], axis=0), ('dp',...]
    reduce_sum x5 -> x2, other arithmetic: 19.6 us -> 4.87 us  [norm_back(): return (back, jnp.sum(grad * xhat, axis=0), jnp.sum(grad, axis=0))]
    pallas_call x25 -> x23, Pallas kernels: 385 us -> 400 us  [call(): pl.pallas_call(kernel, out_shape=outs, grid=grid, in_specs=in_specs, out_...]
    convert_element_type x19 -> x14, other arithmetic: 31.7 us -> 19.5 us  [the longest x8 8.31 us: reduce_rows(): (keep[part_rows:].astype(F32) + got[part_rows:].astype(F32)).astype(BF)]
  transfers between devices with their start and end apart: 73 -> 72, of which waited for: 29 -> 29; matrix products, arithmetic and copies ran while one was open for 11% -> 12% of each run, Pallas kernels for 25% -> 45%
where the time goes in v2:
time: 889 us; the launch traced here: 879 us
  Pallas kernels  400 us (45%)
  waiting for transfers between devices  291 us (33%)
  other arithmetic  83.7 us (9%)
  starting transfers between devices  46.6 us (5%)
  local copies, waits for them, and re-layouts  40.2 us (5%)
  between operations  15.4 us (2%)
    pallas_call x23, Pallas kernels, call(): pl.pallas_call(kernel, out_shape=outs, grid=grid, in_specs=in_specs, out_...  400 us
    ppermute x24, waiting for transfers between devices, in_turn(): turns[axis] = lax.ppermute(v, name, pairs_of)  220 us
    all_gather x3, waiting for transfers between devices, fetch_all(): return lax.all_gather(local, 'dp', axis=0, tiled=True)  36.2 us
    ppermute x24, starting transfers between devices, in_turn(): turns[axis] = lax.ppermute(v, name, pairs_of)  28.7 us
    ppermute x6, waiting for transfers between devices, total_of(): v = v + lax.ppermute(v, 'dp', [(i, i ^ 1 << bit) for i in range(dp)])  27 us
  transfers between devices with their start and end apart: 72, of which 29 were waited for; matrix products, arithmetic and copies ran while one was open for 12% of the time, Pallas kernels for 45%

profile of v2, /device:TPU:0, one launch (start us, length us, event | category | flops | bytes accessed | tf_op | source)
XLA Modules:
  0.0 879.3 jit_solution(6839369663414401880)
XLA Ops:
  40.6 25.5 %collective-permute-done.5.p1 = bf16[2,256,1536]{2,1,0:T(8,128)(2,1)} collective-permute-done((bf16[2,256,1536]{2,1,0:T(8,128)(2,1)S(1)}, bf16[2,256,1536]{2,1,0:T(8,128)(2,1)}, u32[]{:S(2)}, u32[]{:S(2)}) %collective-permute-start.5) | collective-permute-done | bytes 1572896 | tf_op jit(solution)/shard_map/ppermute | solution.py:635
  66.0 14.7 %all-gather.5.cloned.1.call-done.weight.w_ref = bf16[1536,1152]{1,0:T(8,128)(2,1)} async-done(((bf16[192,1152]{1,0:T(8,128)(2,1)}), bf16[1536,1152]{1,0:T(8,128)(2,1)}) %all-gather.5.cloned.1.call-update) | async-done | bytes 3538960 | tf_op jit(solution)/shard_map/all_gather | solution.py:639
  93.6 23.6 %shard_map.221 = (bf16[1024,1536]{1,0:T(8,128)(2,1)}, bf16[1024,384]{1,0:T(8,128)(2,1)}, bf16[1024,384]{1,0:T(8,128)(2,1)}, bf16[1024,384]{1,0:T(8,128)(2,1)}, b...) custom-call(bf16[2,256,1536]{2,1,0:T(8,128)(2,1)} %t.3, bf16[2,256,1536]{2,1,0:T(8,128)(2,1)} %collective-permute-done.5.p1, ...), custom_call_target="tpu_custom_call" | custom-call | flops 15703474176 | bytes 16000000 | tf_op jit(solution)/shard_map/pallas_call | solution.py:21
  126.8 23.4 %shard_map.222 = (bf16[1024,1536]{1,0:T(8,128)(2,1)}, bf16[1024,384]{1,0:T(8,128)(2,1)}, bf16[1024,384]{1,0:T(8,128)(2,1)}, bf16[1024,384]{1,0:T(8,128)(2,1)}, b...) custom-call(bf16[2,256,1536]{2,1,0:T(8,128)(2,1)} %t.3, bf16[2,256,1536]{2,1,0:T(8,128)(2,1)} %collective-permute-done.5.p1, ...), custom_call_target="tpu_custom_call" | custom-call | flops 15703474176 | bytes 16000000 | tf_op jit(solution)/shard_map/pallas_call | solution.py:21
  150.2 11.7 %all-gather.7.cloned.1.call-done.weight.o_ref = bf16[1536,1536]{1,0:T(8,128)(2,1)} async-done(((bf16[192,1536]{1,0:T(8,128)(2,1)}), bf16[1536,1536]{1,0:T(8,128)(2,1)}) %all-gather.7.cloned.1.call-update) | async-done | bytes 4718608 | tf_op jit(solution)/shard_map/all_gather | solution.py:639
  175.2 10.4 %collective-permute-done.10 = bf16[2,2,130,384]{3,2,1,0:T(8,128)(2,1)S(1)} collective-permute-done((bf16[2,2,130,384]{3,2,1,0:T(8,128)(2,1)S(1)}, bf16[2,2,130,384]{3,2,1,0:T(8,128)(2,1)S(1)}, u32[]{:S(2)}, u32[]{:S(2)}) %collective-permute-start.10) | collective-permute-done | bytes 399392 | tf_op jit(solution)/shard_map/ppermute | solution.py:635
  187.3 17.6 %collective-permute-done.11.c = bf16[256,1536]{1,0:T(8,128)(2,1)S(1)} collective-permute-done((bf16[256,1536]{1,0:T(8,128)(2,1)S(1)}, bf16[256,1536]{1,0:T(8,128)(2,1)S(1)}, u32[]{:S(2)}, u32[]{:S(2)}) %collective-permute-start.11) | collective-permute-done | bytes 786464 | tf_op jit(solution)/shard_map/ppermute | solution.py:635
  208.9 15.5 %collective-permute-done.13.c = bf16[256,1536]{1,0:T(8,128)(2,1)S(1)} collective-permute-done((bf16[256,1536]{1,0:T(8,128)(2,1)S(1)}, bf16[256,1536]{1,0:T(8,128)(2,1)S(1)}, u32[]{:S(2)}, u32[]{:S(2)}) %collective-permute-start.13) | collective-permute-done | bytes 786464 | tf_op jit(solution)/shard_map/ppermute | solution.py:635
  226.7 50.2 %collective-permute-done.14.w1 = bf16[1536,768]{1,0:T(8,128)(2,1)} collective-permute-done((bf16[1536,768]{1,0:T(8,128)(2,1)}, bf16[1536,768]{1,0:T(8,128)(2,1)}, u32[]{:S(2)}, u32[]{:S(2)}) %collective-permute-start.14) | collective-permute-done | bytes 2359328 | tf_op jit(solution)/shard_map/ppermute | solution.py:635
  286.2 14.6 %shard_map.225 = (f32[256,1536]{1,0:T(8,128)}, f32[256,1536]{1,0:T(8,128)}, bf16[256,1536]{1,0:T(8,128)(2,1)}, bf16[256,1536]{1,0:T(8,128)(2,1)}, bf16[256,1536]...) custom-call(bf16[2,256,1536]{2,1,0:T(8,128)(2,1)} %t.3, bf16[512,1536]{1,0:T(8,128)(2,1)} %get-tuple-element.174.a, ...), custom_call_target="tpu_custom_call" | custom-call | flops 8455716864 | bytes 18000000 | tf_op jit(solution)/shard_map/pallas_call | solution.py:21
  305.4 15.4 %collective-permute-done.19.p1.refs_1_ = bf16[256,1536]{1,0:T(8,128)(2,1)} collective-permute-done((bf16[256,1536]{1,0:T(8,128)(2,1)}, bf16[256,1536]{1,0:T(8,128)(2,1)}, u32[]{:S(2)}, u32[]{:S(2)}) %collective-permute-start.19) | collective-permute-done | bytes 786464 | tf_op jit(solution)/shard_map/ppermute | solution.py:635
  320.8 14.7 %shard_map.227 = (f32[256,1536]{1,0:T(8,128)}, f32[256,1536]{1,0:T(8,128)}, bf16[256,1536]{1,0:T(8,128)(2,1)}, bf16[256,1536]{1,0:T(8,128)(2,1)}, bf16[256,1536]...) custom-call(bf16[2,256,1536]{2,1,0:T(8,128)(2,1)} %t.3, bf16[512,1536]{1,0:T(8,128)(2,1)} %get-tuple-element.189.a, ...), custom_call_target="tpu_custom_call" | custom-call | flops 8455716864 | bytes 18000000 | tf_op jit(solution)/shard_map/pallas_call | solution.py:21
  342.7 13.1 %collective-permute-done.24.p1.refs_5_ = bf16[256,1536]{1,0:T(8,128)(2,1)} collective-permute-done((bf16[256,1536]{1,0:T(8,128)(2,1)}, bf16[256,1536]{1,0:T(8,128)(2,1)}, u32[]{:S(2)}, u32[]{:S(2)}) %collective-permute-start.24) | collective-permute-done | bytes 786464 | tf_op jit(solution)/shard_map/ppermute | solution.py:635
  355.7 14.7 %shard_map.226 = (bf16[1024,1536]{1,0:T(8,128)(2,1)}, bf16[1024,1536]{1,0:T(8,128)(2,1)}, bf16[1024,1536]{1,0:T(8,128)(2,1)}) custom-call(bf16[256,1536]{1,0:T(8,128)(2,1)} %get-tuple-element.185.p0.refs_0_, bf16[256,1536]{1,0:T(8,128)(2,1)} %collective-permute-done.19.p1.refs_1_, bf16[256,1536]{1,0:T(8,128)(2,1)} %collective-permute-done.20.p2.refs_2_, ...), custom_call_target="tpu_custom_call" | custom-call | flops 28991029248 | bytes 22000000 | tf_op jit(solution)/shard_map/pallas_call | solution.py:21
  372.2 15.2 %shard_map.228 = (bf16[1024,1536]{1,0:T(8,128)(2,1)}, bf16[1024,1536]{1,0:T(8,128)(2,1)}, bf16[1024,1536]{1,0:T(8,128)(2,1)}) custom-call(bf16[256,1536]{1,0:T(8,128)(2,1)} %get-tuple-element.191.p0.refs_4_, bf16[256,1536]{1,0:T(8,128)(2,1)} %collective-permute-done.24.p1.refs_5_, bf16[256,1536]{1,0:T(8,128)(2,1)} %copy-done.60, ...), custom_call_target="tpu_custom_call" | custom-call | flops 28991029248 | bytes 22000000 | tf_op jit(solution)/shard_map/pallas_call | solution.py:21
  387.4 19.2 %shard_map.229 = (bf16[768,1536]{1,0:T(8,128)(2,1)}, bf16[768,1536]{1,0:T(8,128)(2,1)}) custom-call(s32[1]{0:T(128)} %bitcast.19.par, bf16[256,1536]{1,0:T(8,128)(2,1)} %get-tuple-element.374.refs_0_, bf16[256,1536]{1,0:T(8,128)(2,1)} %get-tuple-element.372.refs_1_, bf16[256,1536]{1,0:T(8,128)(2,1)} %get-tuple-element.370.refs_2_, ...), custom_call_target="tpu_custom_call" | custom-call | flops 28991029248 | bytes 17301504 | tf_op jit(solution)/shard_map/pallas_call | solution.py:21
  407.4 9.8 %all-gather.11.cloned.1.call-done.wd.weight = bf16[1536,1536]{1,0:T(8,128)(2,1)} async-done(((bf16[192,1536]{1,0:T(8,128)(2,1)}), bf16[1536,1536]{1,0:T(8,128)(2,1)}) %all-gather.11.cloned.1.call-update) | async-done | bytes 4718608 | tf_op jit(solution)/shard_map/all_gather | solution.py:639
  417.2 25.0 %shard_map.230 = (bf16[1024,1536]{1,0:T(8,128)(2,1)}, bf16[1024,1536]{1,0:T(8,128)(2,1)}, bf16[512,1536]{1,0:T(8,128)(2,1)}, bf16[512,1536]{1,0:T(8,128)(2,1)}) custom-call(bf16[2,256,1536]{2,1,0:T(8,128)(2,1)} %copy-done.3, bf16[2,256,1536]{2,1,0:T(8,128)(2,1)} %copy-done.21, bf16[2,256,1536]{2,1,0:T(8,128)(2,1)} %collective-permute-done.22.p2, ...), custom_call_target="tpu_custom_call" | custom-call | flops 43486543872 | bytes 33000000 | tf_op jit(solution)/shard_map/pallas_call | solution.py:21
  442.1 24.9 %shard_map.231 = (bf16[1024,1536]{1,0:T(8,128)(2,1)}, bf16[1024,1536]{1,0:T(8,128)(2,1)}, bf16[512,1536]{1,0:T(8,128)(2,1)}, bf16[512,1536]{1,0:T(8,128)(2,1)}) custom-call(bf16[2,256,1536]{2,1,0:T(8,128)(2,1)} %copy-done.3, bf16[2,256,1536]{2,1,0:T(8,128)(2,1)} %copy-done.21, bf16[2,256,1536]{2,1,0:T(8,128)(2,1)} %collective-permute-done.22.p2, ...), custom_call_target="tpu_custom_call" | custom-call | flops 43486543872 | bytes 33000000 | tf_op jit(solution)/shard_map/pallas_call | solution.py:21
  469.3 19.5 %shard_map.232 = (bf16[768,1536]{1,0:T(8,128)(2,1)}, bf16[768,1536]{1,0:T(8,128)(2,1)}) custom-call(s32[1]{0:T(128)} %bitcast.19.par, bf16[256,1536]{1,0:T(8,128)(2,1)} %get-tuple-element.185.p0.refs_0_, bf16[256,1536]{1,0:T(8,128)(2,1)} %collective-permute-done.19.p1.refs_1_, bf16[256,1536]{1,0:T(8,128)(2,1)} %collective-permute-done.20.p2.refs_2_, ...), custom_call_target="tpu_custom_call" | custom-call | flops 28991029248 | bytes 17301504 | tf_op jit(solution)/shard_map/pallas_call | solution.py:21
  492.5 19.4 %shard_map.233 = (bf16[768,1536]{1,0:T(8,128)(2,1)}, bf16[768,1536]{1,0:T(8,128)(2,1)}) custom-call(s32[1]{0:T(128)} %bitcast.19.par, bf16[256,1536]{1,0:T(8,128)(2,1)} %get-tuple-element.185.p0.refs_0_, bf16[256,1536]{1,0:T(8,128)(2,1)} %collective-permute-done.19.p1.refs_1_, bf16[256,1536]{1,0:T(8,128)(2,1)} %collective-permute-done.20.p2.refs_2_, ...), custom_call_target="tpu_custom_call" | custom-call | flops 28991029248 | bytes 17301504 | tf_op jit(solution)/shard_map/pallas_call | solution.py:21
  514.1 24.0 %shard_map.234 = (f32[256,1536]{1,0:T(8,128)}, bf16[256,1536]{1,0:T(8,128)(2,1)}, bf16[256,1536]{1,0:T(8,128)(2,1)}, bf16[256,1536]{1,0:T(8,128)(2,1)}, bf16[4,2...) custom-call(bf16[2,256,1536]{2,1,0:T(8,128)(2,1)} %copy-done.3, bf16[512,1536]{1,0:T(8,128)(2,1)} %get-tuple-element.199.a, ...), custom_call_target="tpu_custom_call" | custom-call | flops 10267656192 | bytes 24000000 | tf_op jit(solution)/shard_map/pallas_call | solution.py:21
  545.8 24.4 %shard_map.235 = (f32[256,1536]{1,0:T(8,128)}, bf16[256,1536]{1,0:T(8,128)(2,1)}, bf16[256,1536]{1,0:T(8,128)(2,1)}, bf16[256,1536]{1,0:T(8,128)(2,1)}, bf16[4,2...) custom-call(bf16[2,256,1536]{2,1,0:T(8,128)(2,1)} %copy-done.3, bf16[512,1536]{1,0:T(8,128)(2,1)} %get-tuple-element.202.a, ...), custom_call_target="tpu_custom_call" | custom-call | flops 10267656192 | bytes 24000000 | tf_op jit(solution)/shard_map/pallas_call | solution.py:21
  578.0 11.1 %shard_map.236 = (bf16[2,768,768]{2,1,0:T(8,128)(2,1)}, bf16[2,768,768]{2,1,0:T(8,128)(2,1)}, bf16[2,768,768]{2,1,0:T(8,128)(2,1)}, bf16[2,768,768]{2,1,0:T(8,128)(2,1)}) custom-call(s32[1]{0:T(128)} %bitcast.19.par, bf16[256,1536]{1,0:T(8,128)(2,1)} %get-tuple-element.233.refs_0_, bf16[256,1536]{1,0:T(8,128)(2,1)} %get-tuple-element.235.refs_1_, ...), custom_call_target="tpu_custom_call" | custom-call | flops 14495514624 | bytes 16000000 | tf_op jit(solution)/shard_map/pallas_call | solution.py:21
  589.1 9.7 %shard_map.237 = (bf16[512,1536]{1,0:T(8,128)(2,1)}, bf16[512,1536]{1,0:T(8,128)(2,1)}) custom-call(bf16[1024,1536]{1,0:T(8,128)(2,1)} %get-tuple-element.241.refs_8_.a, bf16[1536,1536]{1,0:T(8,128)(2,1)} %all-gather.11.cloned.1.call-done.wd.weight), custom_call_target="tpu_custom_call" | custom-call | flops 14495514624 | bytes 11010048 | tf_op jit(solution)/shard_map/pallas_call | solution.py:21
  619.4 11.9 %collective-permute-done.37 = bf16[2,2,256,384]{3,2,1,0:T(8,128)(2,1)S(1)} collective-permute-done((bf16[2,2,256,384]{3,2,1,0:T(8,128)(2,1)}, bf16[2,2,256,384]{3,2,1,0:T(8,128)(2,1)S(1)}, u32[]{:S(2)}, u32[]{:S(2)}) %collective-permute-start.37) | collective-permute-done | bytes 786464 | tf_op jit(solution)/shard_map/ppermute | solution.py:635
  632.5 35.1 %shard_map.239 = (bf16[1024,1152]{1,0:T(8,128)(2,1)}, bf16[512,1536]{1,0:T(8,128)(2,1)}, bf16[512,1536]{1,0:T(8,128)(2,1)}) custom-call(bf16[256,1536]{1,0:T(8,128)(2,1)} %get-tuple-element.232.p0.refs_0_, bf16[256,1536]{1,0:T(8,128)(2,1)} %collective-permute-done.32.p1.refs_1_, bf16[256,1536]{1,0:T(8,128)(2,1)} %collective-permute-done.42.p2.refs_2_, ...), custom_call_target="tpu_custom_call" | custom-call | flops 26575110144 | bytes 24000000 | tf_op jit(solution)/shard_map/pallas_call | solution.py:21
  700.4 35.1 %shard_map.241 = (bf16[1024,1152]{1,0:T(8,128)(2,1)}, bf16[512,1536]{1,0:T(8,128)(2,1)}, bf16[512,1536]{1,0:T(8,128)(2,1)}) custom-call(bf16[256,1536]{1,0:T(8,128)(2,1)} %get-tuple-element.248.refs_4_.p0, bf16[256,1536]{1,0:T(8,128)(2,1)} %collective-permute-done.36.refs_5_.p1, bf16[256,1536]{1,0:T(8,128)(2,1)} %collective-permute-done.45.refs_6_.p2, ...), custom_call_target="tpu_custom_call" | custom-call | flops 26575110144 | bytes 24000000 | tf_op jit(solution)/shard_map/pallas_call | solution.py:21
  736.3 15.7 %collective-permute-done.59 = bf16[768,1536]{1,0:T(8,128)(2,1)S(1)} collective-permute-done((bf16[768,1536]{1,0:T(8,128)(2,1)}, bf16[768,1536]{1,0:T(8,128)(2,1)S(1)}, u32[]{:S(2)}, u32[]{:S(2)}) %collective-permute-start.59) | collective-permute-done | bytes 2359328 | tf_op jit(solution)/shard_map/ppermute | solution.py:635
  764.8 11.7 %collective-permute-done.51 = bf16[256,1536]{1,0:T(8,128)(2,1)S(1)} collective-permute-done((bf16[256,1536]{1,0:T(8,128)(2,1)S(1)}, bf16[256,1536]{1,0:T(8,128)(2,1)S(1)}, u32[]{:S(2)}, u32[]{:S(2)}) %collective-permute-start.51) | collective-permute-done | bytes 786464 | tf_op jit(solution)/shard_map/ppermute | solution.py:635
  786.0 12.1 %shard_map.243 = (bf16[768,768]{1,0:T(8,128)(2,1)}, bf16[768,768]{1,0:T(8,128)(2,1)}) custom-call(s32[1]{0:T(128)} %bitcast.19.par, bf16[1024,1536]{1,0:T(8,128)(2,1)} %get-tuple-element.266.refs_0_, bf16[1024,1536]{1,0:T(8,128)(2,1)} %get-tuple-element.267.refs_1_, bf16[1024,1152]{1,0:T(8,128)(2,1)} %get-tuple-element.290.refs_2_, ...), custom_call_target="tpu_custom_call" | custom-call | flops 14495514624 | bytes 11796480 | tf_op jit(solution)/shard_map/pallas_call | solution.py:21
  801.1 10.6 %collective-permute-done.60 = bf16[768,384]{1,0:T(8,128)(2,1)S(1)} collective-permute-done((bf16[768,384]{1,0:T(8,128)(2,1)}, bf16[768,384]{1,0:T(8,128)(2,1)S(1)}, u32[]{:S(2)}, u32[]{:S(2)}) %collective-permute-start.60) | collective-permute-done | bytes 589856 | tf_op jit(solution)/shard_map/ppermute | solution.py:635
  (395 shorter events, 264.5 us)
Async XLA Ops:
  7.2 73.5 %all-gather.5.cloned.1.call-start = ((), (), s32[]{:S(2)}) async-start(), calls=%async_computation.6 | async-start | bytes 3981312 | tf_op jit(solution)/shard_map/all_gather | solution.py:639
  9.2 152.7 %all-gather.7.cloned.1.call-start = ((), (), s32[]{:S(2)}) async-start(), calls=%async_computation.7 | async-start | bytes 5308416 | tf_op jit(solution)/shard_map/all_gather | solution.py:639
  36.1 30.0 %collective-permute-start.5 = (bf16[2,256,1536]{2,1,0:T(8,128)(2,1)S(1)}, bf16[2,256,1536]{2,1,0:T(8,128)(2,1)}, u32[]{:S(2)}, u32[]{:S(2)}) collective-permute-start(bf16[2,256,1536]{2,1,0:T(8,128)(2,1)S(1)} %copy-done), channel_id=1, source_target_pairs={{0,2},{1,3},{2,0},{3,1},{4,6},{5,7},{6,4},{7,5},{8,10},{9,11},{10,... | collective-permute-start | bytes 4718600 | tf_op jit(solution)/shard_map/ppermute | solution.py:635
  80.8 240.0 %all-gather.9.cloned.1.call-start = ((), (), s32[]{:S(2)}) async-start(), calls=%async_computation.8 | async-start | bytes 10616832 | tf_op jit(solution)/shard_map/all_gather | solution.py:725
  89.2 36.4 %collective-permute-start.8 = (bf16[2,256,1536]{2,1,0:T(8,128)(2,1)S(1)}, bf16[2,256,1536]{2,1,0:T(8,128)(2,1)S(1)}, u32[]{:S(2)}, u32[]{:S(2)}) collective-permute-start(bf16[2,256,1536]{2,1,0:T(8,128)(2,1)S(1)} %multiply_convert_fusion.p0.t), channel_id=1, source_target_pairs={{0,2},{1,3},{2,0},{3,1},{4,6},{5,7},{6,4},{7,5},{8,10},{9,11},{10,... | collective-permute-start | bytes 4718600 | tf_op jit(solution)/shard_map/ppermute | solution.py:635
  161.9 255.2 %all-gather.11.cloned.1.call-start = ((), (), s32[]{:S(2)}) async-start(), calls=%async_computation.9 | async-start | bytes 5308416 | tf_op jit(solution)/shard_map/all_gather | solution.py:639
  225.3 51.7 %collective-permute-start.14 = (bf16[1536,768]{1,0:T(8,128)(2,1)}, bf16[1536,768]{1,0:T(8,128)(2,1)}, u32[]{:S(2)}, u32[]{:S(2)}) collective-permute-start(bf16[1536,768]{1,0:T(8,128)(2,1)} %slice.218.w0), channel_id=1, source_target_pairs={{0,2},{1,3},{2,0},{3,1},{4,6},{5,7},{6,4},{7,5},{8,10},{9,11},{10,... | collective-permute-start | bytes 7077896 | tf_op jit(solution)/shard_map/ppermute | solution.py:635
  226.7 59.5 %collective-permute-start.15 = (bf16[1536,768]{1,0:T(8,128)(2,1)}, bf16[1536,768]{1,0:T(8,128)(2,1)}, u32[]{:S(2)}, u32[]{:S(2)}) collective-permute-start(bf16[1536,768]{1,0:T(8,128)(2,1)} %slice.218.w0), channel_id=1, source_target_pairs={{0,1},{1,0},{2,3},{3,2},{4,5},{5,4},{6,7},{7,6},{8,9},{9,8},{10,11... | collective-permute-start | bytes 7077896 | tf_op jit(solution)/shard_map/ppermute | solution.py:649
  280.0 57.0 %collective-permute-start.22 = (bf16[2,256,1536]{2,1,0:T(8,128)(2,1)S(1)}, bf16[2,256,1536]{2,1,0:T(8,128)(2,1)}, u32[]{:S(2)}, u32[]{:S(2)}) collective-permute-start(bf16[2,256,1536]{2,1,0:T(8,128)(2,1)S(1)} %multiply_convert_fusion.p0.t), channel_id=1, source_target_pairs={{0,1},{1,0},{2,3},{3,2},{4,5},{5,4},{6,7},{7,6},{8,9},{9,8},{10,11... | collective-permute-start | bytes 4718600 | tf_op jit(solution)/shard_map/ppermute | solution.py:649
  303.6 36.1 %collective-permute-start.23 = (bf16[2,256,1536]{2,1,0:T(8,128)(2,1)S(1)}, bf16[2,256,1536]{2,1,0:T(8,128)(2,1)}, u32[]{:S(2)}, u32[]{:S(2)}) collective-permute-start(bf16[2,256,1536]{2,1,0:T(8,128)(2,1)S(1)} %copy-done.22), channel_id=1, source_target_pairs={{0,1},{1,0},{2,3},{3,2},{4,5},{5,4},{6,7},{7,6},{8,9},{9,8},{10,11... | collective-permute-start | bytes 4718600 | tf_op jit(solution)/shard_map/ppermute | solution.py:649
  304.9 50.9 %collective-permute-start.20 = (bf16[256,1536]{1,0:T(8,128)(2,1)}, bf16[256,1536]{1,0:T(8,128)(2,1)}, u32[]{:S(2)}, u32[]{:S(2)}) collective-permute-start(bf16[256,1536]{1,0:T(8,128)(2,1)} %get-tuple-element.185.p0.refs_0_), channel_id=1, source_target_pairs={{0,1},{1,0},{2,3},{3,2},{4,5},{5,4},{6,7},{7,6},{8,9},{9,8},{10,11... | collective-permute-start | bytes 2359304 | tf_op jit(solution)/shard_map/ppermute | solution.py:649
  320.8 35.0 %collective-permute-start.21 = (bf16[256,1536]{1,0:T(8,128)(2,1)}, bf16[256,1536]{1,0:T(8,128)(2,1)}, u32[]{:S(2)}, u32[]{:S(2)}) collective-permute-start(bf16[256,1536]{1,0:T(8,128)(2,1)} %collective-permute-done.19.p1.refs_1_), channel_id=1, source_target_pairs={{0,1},{1,0},{2,3},{3,2},{4,5},{5,4},{6,7},{7,6},{8,9},{9,8},{10,11... | collective-permute-start | bytes 2359304 | tf_op jit(solution)/shard_map/ppermute | solution.py:649
  339.7 271.4 %reduce-scatter.7.cloned.1.call-start = ((), (), s32[]{:S(2)}) async-start(), calls=%async_computation.10 | async-start | bytes 2949120 | tf_op jit(solution)/shard_map/reduce_scatter | solution.py:646
  406.7 60.4 %collective-permute-start.31 = (bf16[768,1536]{1,0:T(8,128)(2,1)}, bf16[768,1536]{1,0:T(8,128)(2,1)S(1)}, u32[]{:S(2)}, u32[]{:S(2)}) collective-permute-start(bf16[768,1536]{1,0:T(8,128)(2,1)} %get-tuple-element.195), channel_id=1, source_target_pairs={{0,4},{4,0},{8,12},{12,8},{16,20},{20,16},{24,28},{28,24},{1,5},{5... | collective-permute-start | bytes 7077896 | tf_op jit(solution)/shard_map/ppermute | solution.py:635
  469.2 216.6 %reduce-scatter.9.cloned.1.call-start = ((), (), s32[]{:S(2)}) async-start(), calls=%async_computation.11 | async-start | bytes 2949120 | tf_op jit(solution)/shard_map/reduce_scatter | solution.py:646
  488.9 53.8 %collective-permute-start.44 = (bf16[768,1536]{1,0:T(8,128)(2,1)}, bf16[768,1536]{1,0:T(8,128)(2,1)S(1)}, u32[]{:S(2)}, u32[]{:S(2)}) collective-permute-start(bf16[768,1536]{1,0:T(8,128)(2,1)} %get-tuple-element.259), channel_id=1, source_target_pairs={{0,4},{4,0},{8,12},{12,8},{16,20},{20,16},{24,28},{28,24},{1,5},{5... | collective-permute-start | bytes 7077896 | tf_op jit(solution)/shard_map/ppermute | solution.py:635
  513.3 31.0 %collective-permute-start.30 = (bf16[256,1536]{1,0:T(8,128)(2,1)S(1)}, bf16[256,1536]{1,0:T(8,128)(2,1)S(1)}, u32[]{:S(2)}, u32[]{:S(2)}) collective-permute-start(bf16[256,1536]{1,0:T(8,128)(2,1)S(1)} %add_convert_fusion.8), channel_id=1, source_target_pairs={{0,2},{1,3},{2,0},{3,1},{4,6},{5,7},{6,4},{7,5},{8,10},{9,11},{10,... | collective-permute-start | bytes 2359304 | tf_op jit(solution)/shard_map/ppermute | solution.py:635
  538.2 72.9 %collective-permute-start.42 = (bf16[256,1536]{1,0:T(8,128)(2,1)}, bf16[256,1536]{1,0:T(8,128)(2,1)}, u32[]{:S(2)}, u32[]{:S(2)}) collective-permute-start(bf16[256,1536]{1,0:T(8,128)(2,1)} %get-tuple-element.232.p0.refs_0_), channel_id=1, source_target_pairs={{0,1},{1,0},{2,3},{3,2},{4,5},{5,4},{6,7},{7,6},{8,9},{9,8},{10,11... | collective-permute-start | bytes 2359304 | tf_op jit(solution)/shard_map/ppermute | solution.py:649
  544.3 32.9 %collective-permute-start.32 = (bf16[256,1536]{1,0:T(8,128)(2,1)}, bf16[256,1536]{1,0:T(8,128)(2,1)}, u32[]{:S(2)}, u32[]{:S(2)}) collective-permute-start(bf16[256,1536]{1,0:T(8,128)(2,1)} %get-tuple-element.232.p0.refs_0_), channel_id=1, source_target_pairs={{0,2},{1,3},{2,0},{3,1},{4,6},{5,7},{6,4},{7,5},{8,10},{9,11},{10,... | collective-permute-start | bytes 2359304 | tf_op jit(solution)/shard_map/ppermute | solution.py:635
  570.1 44.5 %collective-permute-start.45 = (bf16[256,1536]{1,0:T(8,128)(2,1)}, bf16[256,1536]{1,0:T(8,128)(2,1)}, u32[]{:S(2)}, u32[]{:S(2)}) collective-permute-start(bf16[256,1536]{1,0:T(8,128)(2,1)} %get-tuple-element.248.refs_4_.p0), channel_id=1, source_target_pairs={{0,1},{1,0},{2,3},{3,2},{4,5},{5,4},{6,7},{7,6},{8,9},{9,8},{10,11... | collective-permute-start | bytes 2359304 | tf_op jit(solution)/shard_map/ppermute | solution.py:649
  611.1 143.0 %reduce-scatter.11.cloned.1.call-start = ((), (), s32[]{:S(2)}) async-start(), calls=%async_computation.12 | async-start | bytes 2949120 | tf_op jit(solution)/shard_map/reduce_scatter | solution.py:646
  614.6 57.2 %collective-permute-start.47 = (bf16[768,1536]{1,0:T(8,128)(2,1)}, bf16[768,1536]{1,0:T(8,128)(2,1)}, u32[]{:S(2)}, u32[]{:S(2)}) collective-permute-start(bf16[768,1536]{1,0:T(8,128)(2,1)} %get-tuple-element.270), channel_id=1, source_target_pairs={{0,4},{4,0},{8,12},{12,8},{16,20},{20,16},{24,28},{28,24},{1,5},{5... | collective-permute-start | bytes 7077896 | tf_op jit(solution)/shard_map/ppermute | solution.py:635
  615.2 52.5 %collective-permute-start.49 = (bf16[2,2,256,384]{3,2,1,0:T(8,128)(2,1)S(1)}, bf16[2,2,256,384]{3,2,1,0:T(8,128)(2,1)S(1)}, u32[]{:S(2)}, u32[]{:S(2)}) collective-permute-start(bf16[2,2,256,384]{3,2,1,0:T(8,128)(2,1)S(1)} %pad_maximum_fusion.7), channel_id=1, source_target_pairs={{0,1},{1,0},{2,3},{3,2},{4,5},{5,4},{6,7},{7,6},{8,9},{9,8},{10,11... | collective-permute-start | bytes 2359304 | tf_op jit(solution)/shard_map/ppermute | solution.py:649
  615.2 62.6 %collective-permute-start.33 = (bf16[512,1536]{1,0:T(8,128)(2,1)}, bf16[512,1536]{1,0:T(8,128)(2,1)}, u32[]{:S(2)}, u32[]{:S(2)}) collective-permute-start(bf16[512,1536]{1,0:T(8,128)(2,1)} %get-tuple-element.243), channel_id=1, source_target_pairs={{0,1},{1,0},{2,3},{3,2},{4,5},{5,4},{6,7},{7,6},{8,9},{9,8},{10,11... | collective-permute-start | bytes 4718600 | tf_op jit(solution)/shard_map/ppermute | solution.py:649
  615.8 64.8 %collective-permute-start.40 = (bf16[512,1536]{1,0:T(8,128)(2,1)}, bf16[512,1536]{1,0:T(8,128)(2,1)}, u32[]{:S(2)}, u32[]{:S(2)}) collective-permute-start(bf16[512,1536]{1,0:T(8,128)(2,1)} %get-tuple-element.254), channel_id=1, source_target_pairs={{0,1},{1,0},{2,3},{3,2},{4,5},{5,4},{6,7},{7,6},{8,9},{9,8},{10,11... | collective-permute-start | bytes 4718600 | tf_op jit(solution)/shard_map/ppermute | solution.py:649
  631.3 53.2 %collective-permute-start.38 = (bf16[2,768,768]{2,1,0:T(8,128)(2,1)}, bf16[2,768,768]{2,1,0:T(8,128)(2,1)}, u32[]{:S(2)}, u32[]{:S(2)}) collective-permute-start(bf16[2,768,768]{2,1,0:T(8,128)(2,1)} %add_convert_fusion.1), channel_id=1, source_target_pairs={{0,2},{1,3},{2,0},{3,1},{4,6},{5,7},{6,4},{7,5},{8,10},{9,11},{10,... | collective-permute-start | bytes 7077896 | tf_op jit(solution)/shard_map/ppermute | solution.py:635
  684.5 50.9 %collective-permute-start.39 = (bf16[256,1536]{1,0:T(8,128)(2,1)}, bf16[256,1536]{1,0:T(8,128)(2,1)}, u32[]{:S(2)}, u32[]{:S(2)}) collective-permute-start(bf16[256,1536]{1,0:T(8,128)(2,1)} %add_convert_fusion.6), channel_id=1, source_target_pairs={{0,2},{1,3},{2,0},{3,1},{4,6},{5,7},{6,4},{7,5},{8,10},{9,11},{10,... | collective-permute-start | bytes 2359304 | tf_op jit(solution)/shard_map/ppermute | solution.py:635
  685.8 127.4 %reduce-scatter.13.cloned.1.call-start = ((), (), s32[]{:S(2)}) async-start(), calls=%async_computation.13 | async-start | bytes 2949120 | tf_op jit(solution)/shard_map/reduce_scatter | solution.py:646
  699.8 52.3 %collective-permute-start.59 = (bf16[768,1536]{1,0:T(8,128)(2,1)}, bf16[768,1536]{1,0:T(8,128)(2,1)S(1)}, u32[]{:S(2)}, u32[]{:S(2)}) collective-permute-start(bf16[768,1536]{1,0:T(8,128)(2,1)} %pad_maximum_fusion.2), channel_id=1, source_target_pairs={{0,4},{4,0},{8,12},{12,8},{16,20},{20,16},{24,28},{28,24},{1,5},{5... | collective-permute-start | bytes 7077896 | tf_op jit(solution)/shard_map/ppermute | solution.py:635
  735.4 28.4 %collective-permute-start.52 = (bf16[512,1536]{1,0:T(8,128)(2,1)}, bf16[512,1536]{1,0:T(8,128)(2,1)S(1)}, u32[]{:S(2)}, u32[]{:S(2)}) collective-permute-start(bf16[512,1536]{1,0:T(8,128)(2,1)} %get-tuple-element.301), channel_id=1, source_target_pairs={{0,1},{1,0},{2,3},{3,2},{4,5},{5,4},{6,7},{7,6},{8,9},{9,8},{10,11... | collective-permute-start | bytes 4718600 | tf_op jit(solution)/shard_map/ppermute | solution.py:649
  754.1 85.3 %reduce-scatter.15.cloned.1.call-start = ((), (), s32[]{:S(2)}) async-start(), calls=%async_computation.14 | async-start | bytes 737280 | tf_op jit(solution)/shard_map/reduce_scatter | solution.py:646
  815.4 54.3 %reduce-scatter.17.cloned.1.call-start = ((), (), s32[]{:S(2)}) async-start(), calls=%async_computation.15 | async-start | bytes 1474560 | tf_op jit(solution)/shard_map/reduce_scatter | solution.py:646
  (111 other events, 1797.8 us)
Sparse Core Ops, SparseCore 0:
  10.8 69.8 all-gather.4
  83.5 78.3 all-gather.6
  164.1 136.1 all-gather.8
  339.8 77.3 all-gather.10
  469.3 46.1 reduce-scatter.6
  611.2 46.0 reduce-scatter.8
  685.9 45.5 reduce-scatter.10
  754.2 46.0 reduce-scatter.12
  815.6 20.0 reduce-scatter.14
  841.2 28.4 reduce-scatter.16

commit v3 on v2

--- a/solution.py
+++ b/solution.py
@@ -669,29 +669,10 @@
             return own, across(far)
 
         def total_of(v):
-            for bit in range((group - 1).bit_length()):
-                v = v + lax.ppermute(v, "tensor", [(i, i ^ (1 << bit)) for i in range(group)])
+            v = v + lax.ppermute(v, "tensor", over_core)
             for bit in range((dp - 1).bit_length()):
                 v = v + lax.ppermute(v, "dp", [(i, i ^ (1 << bit)) for i in range(dp)])
-            return v
-
-        place = rank * group + spot
-        mine = jnp.concatenate([norm_gains, norm_shifts], axis=0)
-        share = mine.shape[1]
-        norms = total_of(lax.dynamic_update_slice(jnp.zeros((6, model), F32), mine, (0, place * share)))
-        gains = [norms[j : j + 1] for j in range(3)]
-        shifts = [norms[3 + j : 4 + j] for j in range(3)]
-        keep_scale = seq_mask.astype(F32)[:, None, None]
-        grad_third = cotangent.astype(F32) * keep_scale
-        token_parts = spread(after(tokens, norms))
-        third_parts = spread(after(grad_third.astype(BF), token_parts[1]))
-
-        w_one = jnp.transpose(w_qkv, (1, 0, 2)).reshape(rows, 3 * width)
-        qkv_full = fetch_all(w_one)
-        w_two = jnp.concatenate(
-            [w_cross_q, w_cross_out.T, w_self_out.T, w_cross_kv.reshape(rows, width)], axis=1
-        )
-        two_full = fetch_all(after(w_two, qkv_full, token_parts[1]))
+            return v + across(v)
 
         order = jnp.stack([spot, spot ^ 2, spot ^ 1, spot ^ 3])
         half_rot = ROT // 2
@@ -711,6 +692,24 @@
                 )
             )
 
+        place = rank * group + spot
+        mine = jnp.concatenate([norm_gains, norm_shifts], axis=0)
+        share = mine.shape[1]
+        token_parts = spread(tokens)
+        norms = total_of(lax.dynamic_update_slice(jnp.zeros((6, model), F32), mine, (0, place * share)))
+        gains = [norms[j : j + 1] for j in range(3)]
+        shifts = [norms[3 + j : 4 + j] for j in range(3)]
+        keep_scale = seq_mask.astype(F32)[:, None, None]
+        grad_third = cotangent.astype(F32) * keep_scale
+        third_parts = spread(grad_third.astype(BF))
+
+        w_one = jnp.transpose(w_qkv, (1, 0, 2)).reshape(rows, 3 * width)
+        qkv_full = fetch_all(w_one)
+        w_two = jnp.concatenate(
+            [w_cross_q, w_cross_out.T, w_self_out.T, w_cross_kv.reshape(rows, width)], axis=1
+        )
+        two_full = fetch_all(after(w_two, qkv_full, token_parts[1], tables[0][0], norms))
+
         state = [dict() for _ in range(seqs)]
         for s in range(seqs):
             st = state[s]
@@ -723,7 +722,7 @@
         last = state[seqs - 1]["att"]
         two_full = after(two_full, last)
         gu_full = lax.all_gather(after(w_gate_up, two_full), "dp", axis=1, tiled=True)
-        cross_full = two_full[:, : 2 * width]
+        cross_parts = spread(two_full[:, : 2 * width])
 
         ctx_pad = -(-ctx_len // 128) * 128
         kv_weight = jnp.transpose(two_full[:, 3 * width :].reshape(dp, 2, ctx_rows, width), (1, 0, 2, 3))
@@ -736,17 +735,16 @@
             st = state[s]
             st["terms"] = reduce_rows(*project(after(st["att"], last), two_full, 2))
             last = st["terms"][0]
-        cross_parts = spread(cross_full)
         for s in range(seqs):
             st = state[s]
             terms = st["terms"]
             if s > 0:
-                terms = (after(terms[0], gu_full), *terms[1:])
+                terms = (after(terms[0], state[s - 1]["second"]), *terms[1:])
             st["first"], st["second"], st["normed2"], normed3, st["cq"], st["crossed"], st["clse"] = cross_forward(
                 tokens, s, terms, norms, cross_parts, cross_kv, ctx_len
             )
             st["normed3"] = spread(normed3)
-        dn_full = fetch_all(after(w_down.T, gu_full))
+        dn_full = fetch_all(after(w_down.T, gu_full, *(st["normed3"][0] for st in state)))
         for s in range(seqs):
             st = state[s]
             st["gate"], st["up"], st["hidden"] = gate_forward(st["normed3"], gu_full)
@@ -789,6 +787,7 @@
             [st["crossed"] for st in state],
             group,
         )
+        up_other = after(up_pair[1], last)
         last = cross_terms[0]
         for s in range(seqs):
             st = state[s]
@@ -807,7 +806,7 @@
             st["d_normed1"] = (keep, send)
             if s > 0:
                 continue
-            up_sum = pair_sum(*up_pair, last)
+            up_sum = pair_sum(up_pair[0], up_other, last)
             up_part = line_sum(after(up_sum, gate_part))
             so_pair = weight_grad(
                 parity,
@@ -829,19 +828,15 @@
             last = (up_sum, *middle_pair)
         middle_sum = pair_sum(*middle_pair, keep)
         normed1 = [st["normed1"] for st in state]
-        qkv_pairs = []
-        for first, steps in ((0, 1), (1, 2)):
-            ready = qkv_pairs[0][1] if first else up_part
-            dqkv = [after(st["dqkv"], ready) for st in state]
-            qkv_pairs.append(weight_grad(parity, normed1, dqkv, width, first, steps))
+        qkv_pair = weight_grad(
+            parity, normed1, [after(st["dqkv"], up_part) for st in state], width
+        )
         middle = line_sum(after(middle_sum, up_part))
         for st in state:
             st["out_terms"] = reduce_rows(*st["out_terms"])
         for st in state:
             st["d_normed1"] = reduce_rows(*st["d_normed1"])
-        q_part = line_sum(after(pair_sum(*qkv_pairs[0], qkv_pairs[1][0]), middle))
-        kv_part = line_sum(after(pair_sum(*qkv_pairs[1], *(st["d_normed1"][2] for st in state)), q_part))
-        qkv_part = jnp.concatenate([q_part, kv_part], axis=1)
+        qkv_part = line_sum(after(pair_sum(*qkv_pair, state[0]["d_normed1"][2]), middle))
         outs = []
         for s in range(seqs):
             st = state[s]
@@ -852,7 +847,7 @@
             st = state[s]
             xhat, inv = norm_parts(tokens[s].astype(F32))
             back, gain_term, shift_term = norm_back(
-                gather_sum(*(after(v, qkv_pairs[1][1]) for v in st["d_normed1"])), xhat, inv, gains[0]
+                gather_sum(*(after(v, qkv_pair[1]) for v in st["d_normed1"])), xhat, inv, gains[0]
             )
             gain_grads[0] += gain_term
             shift_grads[0] += shift_term

time: 889 us -> 842 us (0.947)
  waiting for transfers between devices: 291 us -> 251 us
    ppermute x24 -> x25, waiting for transfers between devices: 220 us -> 147 us  [in_turn(): turns[axis] = lax.ppermute(v, name, pairs_of)]
    all_gather x3, waiting for transfers between devices: 36.2 us -> 70.1 us  [fetch_all(): return lax.all_gather(local, 'dp', axis=0, tiled=True)]
    ppermute x6, waiting for transfers between devices: 27 us -> 14.3 us  [total_of(): v = v + lax.ppermute(v, 'dp', [(i, i ^ 1 << bit) for i in range(dp)])]
    ppermute x24 -> x25, starting transfers between devices: 28.7 us -> 32.8 us  [in_turn(): turns[axis] = lax.ppermute(v, name, pairs_of)]
    pallas_call x23 -> x22, Pallas kernels: 400 us -> 397 us  [call(): pl.pallas_call(kernel, out_shape=outs, grid=grid, in_specs=in_specs, out_...]
  transfers between devices with their start and end apart: 72 -> 70, of which waited for: 29 -> 27; matrix products, arithmetic and copies ran while one was open for 12% -> 12% of each run, Pallas kernels for 45% -> 48%
where the time goes in v3:
time: 842 us; the launch traced here: 835 us
  Pallas kernels  397 us (47%)
  waiting for transfers between devices  251 us (30%)
  other arithmetic  76.7 us (9%)
  starting transfers between devices  50.1 us (6%)
  local copies, waits for them, and re-layouts  43 us (5%)
  between operations  14.9 us (2%)
    pallas_call x22, Pallas kernels, call(): pl.pallas_call(kernel, out_shape=outs, grid=grid, in_specs=in_specs, out_...  397 us
    ppermute x25, waiting for transfers between devices, in_turn(): turns[axis] = lax.ppermute(v, name, pairs_of)  147 us
    all_gather x3, waiting for transfers between devices, fetch_all(): return lax.all_gather(local, 'dp', axis=0, tiled=True)  70.1 us
    ppermute x25, starting transfers between devices, in_turn(): turns[axis] = lax.ppermute(v, name, pairs_of)  32.8 us
  transfers between devices with their start and end apart: 70, of which 27 were waited for; matrix products, arithmetic and copies ran while one was open for 12% of the time, Pallas kernels for 48%

profile of v3, /device:TPU:0, one launch (start us, length us, event | category | flops | bytes accessed | tf_op | source)
XLA Modules:
  0.0 834.7 jit_solution(8262862289215653523)
XLA Ops:
  33.2 13.6 %collective-permute-done.p1 = bf16[2,256,1536]{2,1,0:T(8,128)(2,1)} collective-permute-done((bf16[2,256,1536]{2,1,0:T(8,128)(2,1)}, bf16[2,256,1536]{2,1,0:T(8,128)(2,1)}, u32[]{:S(2)}, u32[]{:S(2)}) %collective-permute-start) | collective-permute-done | bytes 1572896 | tf_op jit(solution)/shard_map/ppermute | solution.py:635
  51.0 29.5 %all-gather.5.cloned.1.call-done.weight.w_ref = bf16[1536,1152]{1,0:T(8,128)(2,1)} async-done(((bf16[192,1152]{1,0:T(8,128)(2,1)}), bf16[1536,1152]{1,0:T(8,128)(2,1)}) %all-gather.5.cloned.1.call-update) | async-done | bytes 3538960 | tf_op jit(solution)/shard_map/all_gather | solution.py:639
  87.6 24.4 %shard_map.221 = (bf16[1024,1536]{1,0:T(8,128)(2,1)}, bf16[1024,384]{1,0:T(8,128)(2,1)}, bf16[1024,384]{1,0:T(8,128)(2,1)}, bf16[1024,384]{1,0:T(8,128)(2,1)}, b...) custom-call(bf16[2,256,1536]{2,1,0:T(8,128)(2,1)} %t.3, bf16[2,256,1536]{2,1,0:T(8,128)(2,1)} %collective-permute-done.p1, ...), custom_call_target="tpu_custom_call" | custom-call | flops 15703474176 | bytes 16000000 | tf_op jit(solution)/shard_map/pallas_call | solution.py:21
  120.6 23.4 %shard_map.222 = (bf16[1024,1536]{1,0:T(8,128)(2,1)}, bf16[1024,384]{1,0:T(8,128)(2,1)}, bf16[1024,384]{1,0:T(8,128)(2,1)}, bf16[1024,384]{1,0:T(8,128)(2,1)}, b...) custom-call(bf16[2,256,1536]{2,1,0:T(8,128)(2,1)} %t.3, bf16[2,256,1536]{2,1,0:T(8,128)(2,1)} %collective-permute-done.p1, ...), custom_call_target="tpu_custom_call" | custom-call | flops 15703474176 | bytes 16000000 | tf_op jit(solution)/shard_map/pallas_call | solution.py:21
  144.0 17.6 %all-gather.7.cloned.1.call-done.weight.o_ref = bf16[1536,1536]{1,0:T(8,128)(2,1)} async-done(((bf16[192,1536]{1,0:T(8,128)(2,1)}), bf16[1536,1536]{1,0:T(8,128)(2,1)}) %all-gather.7.cloned.1.call-update) | async-done | bytes 4718608 | tf_op jit(solution)/shard_map/all_gather | solution.py:639
  180.6 36.9 %collective-permute-done.10.w1 = bf16[1536,768]{1,0:T(8,128)(2,1)} collective-permute-done((bf16[1536,768]{1,0:T(8,128)(2,1)}, bf16[1536,768]{1,0:T(8,128)(2,1)}, u32[]{:S(2)}, u32[]{:S(2)}) %collective-permute-start.10) | collective-permute-done | bytes 2359328 | tf_op jit(solution)/shard_map/ppermute | solution.py:635
  226.4 8.8 %collective-permute-done.11 = bf16[2,2,130,384]{3,2,1,0:T(8,128)(2,1)S(1)} collective-permute-done((bf16[2,2,130,384]{3,2,1,0:T(8,128)(2,1)S(1)}, bf16[2,2,130,384]{3,2,1,0:T(8,128)(2,1)S(1)}, u32[]{:S(2)}, u32[]{:S(2)}) %collective-permute-start.11) | collective-permute-done | bytes 399392 | tf_op jit(solution)/shard_map/ppermute | solution.py:635
  240.2 13.7 %collective-permute-done.12.c = bf16[256,1536]{1,0:T(8,128)(2,1)S(1)} collective-permute-done((bf16[256,1536]{1,0:T(8,128)(2,1)S(1)}, bf16[256,1536]{1,0:T(8,128)(2,1)S(1)}, u32[]{:S(2)}, u32[]{:S(2)}) %collective-permute-start.12) | collective-permute-done | bytes 786464 | tf_op jit(solution)/shard_map/ppermute | solution.py:635
  255.4 14.6 %shard_map.224 = (f32[256,1536]{1,0:T(8,128)}, f32[256,1536]{1,0:T(8,128)}, bf16[256,1536]{1,0:T(8,128)(2,1)}, bf16[256,1536]{1,0:T(8,128)(2,1)}, bf16[256,1536]...) custom-call(bf16[2,256,1536]{2,1,0:T(8,128)(2,1)} %t.3, bf16[512,1536]{1,0:T(8,128)(2,1)} %get-tuple-element.167.a, ...), custom_call_target="tpu_custom_call" | custom-call | flops 8455716864 | bytes 18000000 | tf_op jit(solution)/shard_map/pallas_call | solution.py:21
  273.4 14.9 %shard_map.227 = (f32[256,1536]{1,0:T(8,128)}, f32[256,1536]{1,0:T(8,128)}, bf16[256,1536]{1,0:T(8,128)(2,1)}, bf16[256,1536]{1,0:T(8,128)(2,1)}, bf16[256,1536]...) custom-call(bf16[2,256,1536]{2,1,0:T(8,128)(2,1)} %t.3, bf16[512,1536]{1,0:T(8,128)(2,1)} %get-tuple-element.182.a, ...), custom_call_target="tpu_custom_call" | custom-call | flops 8455716864 | bytes 18000000 | tf_op jit(solution)/shard_map/pallas_call | solution.py:21
  292.5 7.6 all-gather.9.cloned.1.call-done.wg.wu
  307.8 14.9 %shard_map.226 = (bf16[1024,1536]{1,0:T(8,128)(2,1)}, bf16[1024,1536]{1,0:T(8,128)(2,1)}, bf16[1024,1536]{1,0:T(8,128)(2,1)}) custom-call(bf16[256,1536]{1,0:T(8,128)(2,1)} %get-tuple-element.178.p0.refs_0_, bf16[256,1536]{1,0:T(8,128)(2,1)} %collective-permute-done.19.p1.refs_1_, bf16[256,1536]{1,0:T(8,128)(2,1)} %collective-permute-done.20.p2.refs_2_, ...), custom_call_target="tpu_custom_call" | custom-call | flops 28991029248 | bytes 22000000 | tf_op jit(solution)/shard_map/pallas_call | solution.py:21
  324.6 14.7 %shard_map.228 = (bf16[1024,1536]{1,0:T(8,128)(2,1)}, bf16[1024,1536]{1,0:T(8,128)(2,1)}, bf16[1024,1536]{1,0:T(8,128)(2,1)}) custom-call(bf16[256,1536]{1,0:T(8,128)(2,1)} %get-tuple-element.184.p0.refs_4_, bf16[256,1536]{1,0:T(8,128)(2,1)} %collective-permute-done.24.p1.refs_5_, bf16[256,1536]{1,0:T(8,128)(2,1)} %copy-done.54, ...), custom_call_target="tpu_custom_call" | custom-call | flops 28991029248 | bytes 22000000 | tf_op jit(solution)/shard_map/pallas_call | solution.py:21
  339.4 19.1 %shard_map.229 = (bf16[768,1536]{1,0:T(8,128)(2,1)}, bf16[768,1536]{1,0:T(8,128)(2,1)}) custom-call(s32[1]{0:T(128)} %bitcast.19.par, bf16[256,1536]{1,0:T(8,128)(2,1)} %get-tuple-element.362.refs_0_, bf16[256,1536]{1,0:T(8,128)(2,1)} %get-tuple-element.360.refs_1_, bf16[256,1536]{1,0:T(8,128)(2,1)} %get-tuple-element.358.refs_2_, ...), custom_call_target="tpu_custom_call" | custom-call | flops 28991029248 | bytes 17301504 | tf_op jit(solution)/shard_map/pallas_call | solution.py:21
  358.8 23.0 %all-gather.11.cloned.1.call-done.wd.weight = bf16[1536,1536]{1,0:T(8,128)(2,1)} async-done(((bf16[192,1536]{1,0:T(8,128)(2,1)}), bf16[1536,1536]{1,0:T(8,128)(2,1)}) %all-gather.11.cloned.1.call-update) | async-done | bytes 4718608 | tf_op jit(solution)/shard_map/all_gather | solution.py:639
  381.8 24.9 %shard_map.230 = (bf16[1024,1536]{1,0:T(8,128)(2,1)}, bf16[1024,1536]{1,0:T(8,128)(2,1)}, bf16[512,1536]{1,0:T(8,128)(2,1)}, bf16[512,1536]{1,0:T(8,128)(2,1)}) custom-call(bf16[2,256,1536]{2,1,0:T(8,128)(2,1)} %copy-done.3, bf16[2,256,1536]{2,1,0:T(8,128)(2,1)} %copy-done.20, bf16[2,256,1536]{2,1,0:T(8,128)(2,1)} %collective-permute-done.22.p2, ...), custom_call_target="tpu_custom_call" | custom-call | flops 43486543872 | bytes 33000000 | tf_op jit(solution)/shard_map/pallas_call | solution.py:21
  406.7 24.9 %shard_map.231 = (bf16[1024,1536]{1,0:T(8,128)(2,1)}, bf16[1024,1536]{1,0:T(8,128)(2,1)}, bf16[512,1536]{1,0:T(8,128)(2,1)}, bf16[512,1536]{1,0:T(8,128)(2,1)}) custom-call(bf16[2,256,1536]{2,1,0:T(8,128)(2,1)} %copy-done.3, bf16[2,256,1536]{2,1,0:T(8,128)(2,1)} %copy-done.20, bf16[2,256,1536]{2,1,0:T(8,128)(2,1)} %collective-permute-done.22.p2, ...), custom_call_target="tpu_custom_call" | custom-call | flops 43486543872 | bytes 33000000 | tf_op jit(solution)/shard_map/pallas_call | solution.py:21
  434.0 19.4 %shard_map.232 = (bf16[768,1536]{1,0:T(8,128)(2,1)}, bf16[768,1536]{1,0:T(8,128)(2,1)}) custom-call(s32[1]{0:T(128)} %bitcast.19.par, bf16[256,1536]{1,0:T(8,128)(2,1)} %get-tuple-element.178.p0.refs_0_, bf16[256,1536]{1,0:T(8,128)(2,1)} %collective-permute-done.19.p1.refs_1_, bf16[256,1536]{1,0:T(8,128)(2,1)} %collective-permute-done.20.p2.refs_2_, ...), custom_call_target="tpu_custom_call" | custom-call | flops 28991029248 | bytes 17301504 | tf_op jit(solution)/shard_map/pallas_call | solution.py:21
  458.0 19.5 %shard_map.233 = (bf16[768,1536]{1,0:T(8,128)(2,1)}, bf16[768,1536]{1,0:T(8,128)(2,1)}) custom-call(s32[1]{0:T(128)} %bitcast.19.par, bf16[256,1536]{1,0:T(8,128)(2,1)} %get-tuple-element.178.p0.refs_0_, bf16[256,1536]{1,0:T(8,128)(2,1)} %collective-permute-done.19.p1.refs_1_, bf16[256,1536]{1,0:T(8,128)(2,1)} %collective-permute-done.20.p2.refs_2_, ...), custom_call_target="tpu_custom_call" | custom-call | flops 28991029248 | bytes 17301504 | tf_op jit(solution)/shard_map/pallas_call | solution.py:21
  479.8 24.1 %shard_map.234 = (f32[256,1536]{1,0:T(8,128)}, bf16[256,1536]{1,0:T(8,128)(2,1)}, bf16[256,1536]{1,0:T(8,128)(2,1)}, bf16[256,1536]{1,0:T(8,128)(2,1)}, bf16[4,2...) custom-call(bf16[2,256,1536]{2,1,0:T(8,128)(2,1)} %copy-done.3, bf16[512,1536]{1,0:T(8,128)(2,1)} %get-tuple-element.192.a, ...), custom_call_target="tpu_custom_call" | custom-call | flops 10267656192 | bytes 24000000 | tf_op jit(solution)/shard_map/pallas_call | solution.py:21
  506.8 24.2 %shard_map.235 = (f32[256,1536]{1,0:T(8,128)}, bf16[256,1536]{1,0:T(8,128)(2,1)}, bf16[256,1536]{1,0:T(8,128)(2,1)}, bf16[256,1536]{1,0:T(8,128)(2,1)}, bf16[4,2...) custom-call(bf16[2,256,1536]{2,1,0:T(8,128)(2,1)} %copy-done.3, bf16[512,1536]{1,0:T(8,128)(2,1)} %get-tuple-element.195.a, ...), custom_call_target="tpu_custom_call" | custom-call | flops 10267656192 | bytes 24000000 | tf_op jit(solution)/shard_map/pallas_call | solution.py:21
  539.1 11.0 %shard_map.236 = (bf16[2,768,768]{2,1,0:T(8,128)(2,1)}, bf16[2,768,768]{2,1,0:T(8,128)(2,1)}, bf16[2,768,768]{2,1,0:T(8,128)(2,1)}, bf16[2,768,768]{2,1,0:T(8,128)(2,1)}) custom-call(s32[1]{0:T(128)} %bitcast.19.par, bf16[256,1536]{1,0:T(8,128)(2,1)} %get-tuple-element.226.refs_0_, bf16[256,1536]{1,0:T(8,128)(2,1)} %get-tuple-element.228.refs_1_, ...), custom_call_target="tpu_custom_call" | custom-call | flops 14495514624 | bytes 16000000 | tf_op jit(solution)/shard_map/pallas_call | solution.py:21
  550.2 9.9 %shard_map.237 = (bf16[512,1536]{1,0:T(8,128)(2,1)}, bf16[512,1536]{1,0:T(8,128)(2,1)}) custom-call(bf16[1024,1536]{1,0:T(8,128)(2,1)} %get-tuple-element.234.refs_8_.a, bf16[1536,1536]{1,0:T(8,128)(2,1)} %all-gather.11.cloned.1.call-done.wd.weight), custom_call_target="tpu_custom_call" | custom-call | flops 14495514624 | bytes 11010048 | tf_op jit(solution)/shard_map/pallas_call | solution.py:21
  560.6 9.5 %shard_map.238 = (bf16[512,1536]{1,0:T(8,128)(2,1)}, bf16[512,1536]{1,0:T(8,128)(2,1)}) custom-call(bf16[1024,1536]{1,0:T(8,128)(2,1)} %get-tuple-element.245.refs_9_.a, bf16[1536,1536]{1,0:T(8,128)(2,1)} %all-gather.11.cloned.1.call-done.wd.weight), custom_call_target="tpu_custom_call" | custom-call | flops 14495514624 | bytes 11010048 | tf_op jit(solution)/shard_map/pallas_call | solution.py:21
  581.7 10.9 %collective-permute-done.37 = bf16[2,2,256,384]{3,2,1,0:T(8,128)(2,1)S(1)} collective-permute-done((bf16[2,2,256,384]{3,2,1,0:T(8,128)(2,1)}, bf16[2,2,256,384]{3,2,1,0:T(8,128)(2,1)S(1)}, u32[]{:S(2)}, u32[]{:S(2)}) %collective-permute-start.37) | collective-permute-done | bytes 786464 | tf_op jit(solution)/shard_map/ppermute | solution.py:635
  593.7 35.0 %shard_map.239 = (bf16[1024,1152]{1,0:T(8,128)(2,1)}, bf16[512,1536]{1,0:T(8,128)(2,1)}, bf16[512,1536]{1,0:T(8,128)(2,1)}) custom-call(bf16[256,1536]{1,0:T(8,128)(2,1)} %get-tuple-element.225.p0.refs_0_, bf16[256,1536]{1,0:T(8,128)(2,1)} %collective-permute-done.32.p1.refs_1_, bf16[256,1536]{1,0:T(8,128)(2,1)} %collective-permute-done.42.p2.refs_2_, ...), custom_call_target="tpu_custom_call" | custom-call | flops 26575110144 | bytes 24000000 | tf_op jit(solution)/shard_map/pallas_call | solution.py:21
  647.0 7.9 shard_map.240
  665.8 35.2 %shard_map.241 = (bf16[1024,1152]{1,0:T(8,128)(2,1)}, bf16[512,1536]{1,0:T(8,128)(2,1)}, bf16[512,1536]{1,0:T(8,128)(2,1)}) custom-call(bf16[256,1536]{1,0:T(8,128)(2,1)} %get-tuple-element.241.refs_4_.p0, bf16[256,1536]{1,0:T(8,128)(2,1)} %collective-permute-done.36.refs_5_.p1, bf16[256,1536]{1,0:T(8,128)(2,1)} %collective-permute-done.45.refs_6_.p2, ...), custom_call_target="tpu_custom_call" | custom-call | flops 26575110144 | bytes 24000000 | tf_op jit(solution)/shard_map/pallas_call | solution.py:21
  703.5 9.6 %collective-permute-done.59 = bf16[768,1536]{1,0:T(8,128)(2,1)S(1)} collective-permute-done((bf16[768,1536]{1,0:T(8,128)(2,1)}, bf16[768,1536]{1,0:T(8,128)(2,1)S(1)}, u32[]{:S(2)}, u32[]{:S(2)}) %collective-permute-start.59) | collective-permute-done | bytes 2359328 | tf_op jit(solution)/shard_map/ppermute | solution.py:635
  723.6 15.8 %shard_map.242 = (bf16[768,1152]{1,0:T(8,128)(2,1)}, bf16[768,1152]{1,0:T(8,128)(2,1)}) custom-call(s32[1]{0:T(128)} %bitcast.19.par, bf16[1024,1536]{1,0:T(8,128)(2,1)} %get-tuple-element.259.refs_0_, bf16[1024,1536]{1,0:T(8,128)(2,1)} %get-tuple-element.260.refs_1_, bf16[1024,1152]{1,0:T(8,128)(2,1)} %get-tuple-element.268.refs_2_, ...), custom_call_target="tpu_custom_call" | custom-call | flops 21743271936 | bytes 14548992 | tf_op jit(solution)/shard_map/pallas_call | solution.py:21
  752.8 26.7 %collective-permute-done.60 = bf16[768,1152]{1,0:T(8,128)(2,1)} collective-permute-done((bf16[768,1152]{1,0:T(8,128)(2,1)}, bf16[768,1152]{1,0:T(8,128)(2,1)}, u32[]{:S(2)}, u32[]{:S(2)}) %collective-permute-start.60) | collective-permute-done | bytes 1769504 | tf_op jit(solution)/shard_map/ppermute | solution.py:635
  815.8 9.8 %reduce-scatter.14.cloned.1.call-done = bf16[192,1152]{1,0:T(8,128)(2,1)} async-done(((bf16[768,1152]{1,0:T(8,128)(2,1)}), bf16[192,1152]{1,0:T(8,128)(2,1)}) %reduce-scatter.14.cloned.1.call-update) | async-done | bytes 442384 | tf_op jit(solution)/shard_map/reduce_scatter | solution.py:646
  (370 shorter events, 224.4 us)
Async XLA Ops:
  7.2 73.2 %all-gather.5.cloned.1.call-start = ((), (), s32[]{:S(2)}) async-start(), calls=%async_computation.5 | async-start | bytes 3981312 | tf_op jit(solution)/shard_map/all_gather | solution.py:639
  9.1 152.5 %all-gather.7.cloned.1.call-start = ((), (), s32[]{:S(2)}) async-start(), calls=%async_computation.6 | async-start | bytes 5308416 | tf_op jit(solution)/shard_map/all_gather | solution.py:639
  9.1 37.7 %collective-permute-start = (bf16[2,256,1536]{2,1,0:T(8,128)(2,1)}, bf16[2,256,1536]{2,1,0:T(8,128)(2,1)}, u32[]{:S(2)}, u32[]{:S(2)}) collective-permute-start(bf16[2,256,1536]{2,1,0:T(8,128)(2,1)} %t.3), channel_id=1, source_target_pairs={{0,2},{1,3},{2,0},{3,1},{4,6},{5,7},{6,4},{7,5},{8,10},{9,11},{10,... | collective-permute-start | bytes 4718600 | tf_op jit(solution)/shard_map/ppermute | solution.py:635
  80.5 219.6 %all-gather.9.cloned.1.call-start = ((), (), s32[]{:S(2)}) async-start(), calls=%async_computation.7 | async-start | bytes 10616832 | tf_op jit(solution)/shard_map/all_gather | solution.py:724
  82.9 36.4 %collective-permute-start.8 = (bf16[2,256,1536]{2,1,0:T(8,128)(2,1)S(1)}, bf16[2,256,1536]{2,1,0:T(8,128)(2,1)S(1)}, u32[]{:S(2)}, u32[]{:S(2)}) collective-permute-start(bf16[2,256,1536]{2,1,0:T(8,128)(2,1)S(1)} %multiply_convert_fusion.p0.t), channel_id=1, source_target_pairs={{0,2},{1,3},{2,0},{3,1},{4,6},{5,7},{6,4},{7,5},{8,10},{9,11},{10,... | collective-permute-start | bytes 4718600 | tf_op jit(solution)/shard_map/ppermute | solution.py:635
  161.6 220.2 %all-gather.11.cloned.1.call-start = ((), (), s32[]{:S(2)}) async-start(), calls=%async_computation.8 | async-start | bytes 5308416 | tf_op jit(solution)/shard_map/all_gather | solution.py:639
  165.2 52.3 %collective-permute-start.10 = (bf16[1536,768]{1,0:T(8,128)(2,1)}, bf16[1536,768]{1,0:T(8,128)(2,1)}, u32[]{:S(2)}, u32[]{:S(2)}) collective-permute-start(bf16[1536,768]{1,0:T(8,128)(2,1)} %slice.218.w0), channel_id=1, source_target_pairs={{0,2},{1,3},{2,0},{3,1},{4,6},{5,7},{6,4},{7,5},{8,10},{9,11},{10,... | collective-permute-start | bytes 7077896 | tf_op jit(solution)/shard_map/ppermute | solution.py:635
  166.7 50.8 %collective-permute-start.22 = (bf16[2,256,1536]{2,1,0:T(8,128)(2,1)S(1)}, bf16[2,256,1536]{2,1,0:T(8,128)(2,1)}, u32[]{:S(2)}, u32[]{:S(2)}) collective-permute-start(bf16[2,256,1536]{2,1,0:T(8,128)(2,1)S(1)} %multiply_convert_fusion.p0.t), channel_id=1, source_target_pairs={{0,1},{1,0},{2,3},{3,2},{4,5},{5,4},{6,7},{7,6},{8,9},{9,8},{10,11... | collective-permute-start | bytes 4718600 | tf_op jit(solution)/shard_map/ppermute | solution.py:649
  173.5 50.0 %collective-permute-start.9 = (bf16[512,1536]{1,0:T(8,128)(2,1)}, bf16[512,1536]{1,0:T(8,128)(2,1)}, u32[]{:S(2)}, u32[]{:S(2)}) collective-permute-start(bf16[512,1536]{1,0:T(8,128)(2,1)} %get-tuple-element.168), channel_id=1, source_target_pairs={{0,1},{1,0},{2,3},{3,2},{4,5},{5,4},{6,7},{7,6},{8,9},{9,8},{10,11... | collective-permute-start | bytes 4718600 | tf_op jit(solution)/shard_map/ppermute | solution.py:649
  178.9 57.7 %collective-permute-start.17 = (bf16[512,1536]{1,0:T(8,128)(2,1)}, bf16[512,1536]{1,0:T(8,128)(2,1)S(1)}, u32[]{:S(2)}, u32[]{:S(2)}) collective-permute-start(bf16[512,1536]{1,0:T(8,128)(2,1)} %get-tuple-element.176), channel_id=1, source_target_pairs={{0,1},{1,0},{2,3},{3,2},{4,5},{5,4},{6,7},{7,6},{8,9},{9,8},{10,11... | collective-permute-start | bytes 4718600 | tf_op jit(solution)/shard_map/ppermute | solution.py:649
  180.1 75.4 %collective-permute-start.13 = (bf16[1536,768]{1,0:T(8,128)(2,1)}, bf16[1536,768]{1,0:T(8,128)(2,1)}, u32[]{:S(2)}, u32[]{:S(2)}) collective-permute-start(bf16[1536,768]{1,0:T(8,128)(2,1)} %slice.218.w0), channel_id=1, source_target_pairs={{0,1},{1,0},{2,3},{3,2},{4,5},{5,4},{6,7},{7,6},{8,9},{9,8},{10,11... | collective-permute-start | bytes 7077896 | tf_op jit(solution)/shard_map/ppermute | solution.py:649
  217.5 37.9 %collective-permute-start.14 = (bf16[1536,768]{1,0:T(8,128)(2,1)}, bf16[1536,768]{1,0:T(8,128)(2,1)}, u32[]{:S(2)}, u32[]{:S(2)}) collective-permute-start(bf16[1536,768]{1,0:T(8,128)(2,1)} %collective-permute-done.10.w1), channel_id=1, source_target_pairs={{0,1},{1,0},{2,3},{3,2},{4,5},{5,4},{6,7},{7,6},{8,9},{9,8},{10,11... | collective-permute-start | bytes 7077896 | tf_op jit(solution)/shard_map/ppermute | solution.py:649
  237.8 62.3 %collective-permute-start.23 = (bf16[2,256,1536]{2,1,0:T(8,128)(2,1)S(1)}, bf16[2,256,1536]{2,1,0:T(8,128)(2,1)S(1)}, u32[]{:S(2)}, u32[]{:S(2)}) collective-permute-start(bf16[2,256,1536]{2,1,0:T(8,128)(2,1)S(1)} %copy-done.21), channel_id=1, source_target_pairs={{0,1},{1,0},{2,3},{3,2},{4,5},{5,4},{6,7},{7,6},{8,9},{9,8},{10,11... | collective-permute-start | bytes 4718600 | tf_op jit(solution)/shard_map/ppermute | solution.py:649
  270.1 37.8 %collective-permute-start.20 = (bf16[256,1536]{1,0:T(8,128)(2,1)}, bf16[256,1536]{1,0:T(8,128)(2,1)}, u32[]{:S(2)}, u32[]{:S(2)}) collective-permute-start(bf16[256,1536]{1,0:T(8,128)(2,1)} %get-tuple-element.178.p0.refs_0_), channel_id=1, source_target_pairs={{0,1},{1,0},{2,3},{3,2},{4,5},{5,4},{6,7},{7,6},{8,9},{9,8},{10,11... | collective-permute-start | bytes 2359304 | tf_op jit(solution)/shard_map/ppermute | solution.py:649
  300.1 272.3 %reduce-scatter.6.cloned.1.call-start = ((), (), s32[]{:S(2)}) async-start(), calls=%async_computation.9 | async-start | bytes 2949120 | tf_op jit(solution)/shard_map/reduce_scatter | solution.py:646
  358.5 73.2 %collective-permute-start.31 = (bf16[768,1536]{1,0:T(8,128)(2,1)}, bf16[768,1536]{1,0:T(8,128)(2,1)S(1)}, u32[]{:S(2)}, u32[]{:S(2)}) collective-permute-start(bf16[768,1536]{1,0:T(8,128)(2,1)} %get-tuple-element.188), channel_id=1, source_target_pairs={{0,4},{4,0},{8,12},{12,8},{16,20},{20,16},{24,28},{28,24},{1,5},{5... | collective-permute-start | bytes 7077896 | tf_op jit(solution)/shard_map/ppermute | solution.py:635
  433.8 213.1 %reduce-scatter.8.cloned.1.call-start = ((), (), s32[]{:S(2)}) async-start(), calls=%async_computation.10 | async-start | bytes 2949120 | tf_op jit(solution)/shard_map/reduce_scatter | solution.py:646
  453.4 80.3 %collective-permute-start.44 = (bf16[768,1536]{1,0:T(8,128)(2,1)}, bf16[768,1536]{1,0:T(8,128)(2,1)S(1)}, u32[]{:S(2)}, u32[]{:S(2)}) collective-permute-start(bf16[768,1536]{1,0:T(8,128)(2,1)} %get-tuple-element.252), channel_id=1, source_target_pairs={{0,4},{4,0},{8,12},{12,8},{16,20},{20,16},{24,28},{28,24},{1,5},{5... | collective-permute-start | bytes 7077896 | tf_op jit(solution)/shard_map/ppermute | solution.py:635
  503.9 68.6 %collective-permute-start.42 = (bf16[256,1536]{1,0:T(8,128)(2,1)}, bf16[256,1536]{1,0:T(8,128)(2,1)}, u32[]{:S(2)}, u32[]{:S(2)}) collective-permute-start(bf16[256,1536]{1,0:T(8,128)(2,1)} %get-tuple-element.225.p0.refs_0_), channel_id=1, source_target_pairs={{0,1},{1,0},{2,3},{3,2},{4,5},{5,4},{6,7},{7,6},{8,9},{9,8},{10,11... | collective-permute-start | bytes 2359304 | tf_op jit(solution)/shard_map/ppermute | solution.py:649
  531.0 44.8 %collective-permute-start.45 = (bf16[256,1536]{1,0:T(8,128)(2,1)}, bf16[256,1536]{1,0:T(8,128)(2,1)}, u32[]{:S(2)}, u32[]{:S(2)}) collective-permute-start(bf16[256,1536]{1,0:T(8,128)(2,1)} %get-tuple-element.241.refs_4_.p0), channel_id=1, source_target_pairs={{0,1},{1,0},{2,3},{3,2},{4,5},{5,4},{6,7},{7,6},{8,9},{9,8},{10,11... | collective-permute-start | bytes 2359304 | tf_op jit(solution)/shard_map/ppermute | solution.py:649
  572.4 142.7 %reduce-scatter.10.cloned.1.call-start = ((), (), s32[]{:S(2)}) async-start(), calls=%async_computation.11 | async-start | bytes 2949120 | tf_op jit(solution)/shard_map/reduce_scatter | solution.py:646
  575.8 56.8 %collective-permute-start.47 = (bf16[768,1536]{1,0:T(8,128)(2,1)}, bf16[768,1536]{1,0:T(8,128)(2,1)}, u32[]{:S(2)}, u32[]{:S(2)}) collective-permute-start(bf16[768,1536]{1,0:T(8,128)(2,1)} %get-tuple-element.264), channel_id=1, source_target_pairs={{0,4},{4,0},{8,12},{12,8},{16,20},{20,16},{24,28},{28,24},{1,5},{5... | collective-permute-start | bytes 7077896 | tf_op jit(solution)/shard_map/ppermute | solution.py:635
  577.4 51.3 %collective-permute-start.49 = (bf16[2,2,256,384]{3,2,1,0:T(8,128)(2,1)S(1)}, bf16[2,2,256,384]{3,2,1,0:T(8,128)(2,1)S(1)}, u32[]{:S(2)}, u32[]{:S(2)}) collective-permute-start(bf16[2,2,256,384]{3,2,1,0:T(8,128)(2,1)S(1)} %pad_maximum_fusion.6), channel_id=1, source_target_pairs={{0,1},{1,0},{2,3},{3,2},{4,5},{5,4},{6,7},{7,6},{8,9},{9,8},{10,11... | collective-permute-start | bytes 2359304 | tf_op jit(solution)/shard_map/ppermute | solution.py:649
  577.4 61.4 %collective-permute-start.33 = (bf16[512,1536]{1,0:T(8,128)(2,1)}, bf16[512,1536]{1,0:T(8,128)(2,1)}, u32[]{:S(2)}, u32[]{:S(2)}) collective-permute-start(bf16[512,1536]{1,0:T(8,128)(2,1)} %get-tuple-element.236), channel_id=1, source_target_pairs={{0,1},{1,0},{2,3},{3,2},{4,5},{5,4},{6,7},{7,6},{8,9},{9,8},{10,11... | collective-permute-start | bytes 4718600 | tf_op jit(solution)/shard_map/ppermute | solution.py:649
  577.9 63.5 %collective-permute-start.40 = (bf16[512,1536]{1,0:T(8,128)(2,1)}, bf16[512,1536]{1,0:T(8,128)(2,1)}, u32[]{:S(2)}, u32[]{:S(2)}) collective-permute-start(bf16[512,1536]{1,0:T(8,128)(2,1)} %get-tuple-element.247), channel_id=1, source_target_pairs={{0,1},{1,0},{2,3},{3,2},{4,5},{5,4},{6,7},{7,6},{8,9},{9,8},{10,11... | collective-permute-start | bytes 4718600 | tf_op jit(solution)/shard_map/ppermute | solution.py:649
  592.6 53.2 %collective-permute-start.38 = (bf16[2,768,768]{2,1,0:T(8,128)(2,1)}, bf16[2,768,768]{2,1,0:T(8,128)(2,1)}, u32[]{:S(2)}, u32[]{:S(2)}) collective-permute-start(bf16[2,768,768]{2,1,0:T(8,128)(2,1)} %add_convert_fusion.1), channel_id=1, source_target_pairs={{0,2},{1,3},{2,0},{3,1},{4,6},{5,7},{6,4},{7,5},{8,10},{9,11},{10,... | collective-permute-start | bytes 7077896 | tf_op jit(solution)/shard_map/ppermute | solution.py:635
  647.0 136.2 %reduce-scatter.12.cloned.1.call-start = ((), (), s32[]{:S(2)}) async-start(), calls=%async_computation.12 | async-start | bytes 2949120 | tf_op jit(solution)/shard_map/reduce_scatter | solution.py:646
  660.8 52.3 %collective-permute-start.59 = (bf16[768,1536]{1,0:T(8,128)(2,1)}, bf16[768,1536]{1,0:T(8,128)(2,1)S(1)}, u32[]{:S(2)}, u32[]{:S(2)}) collective-permute-start(bf16[768,1536]{1,0:T(8,128)(2,1)} %pad_maximum_fusion.2), channel_id=1, source_target_pairs={{0,4},{4,0},{8,12},{12,8},{16,20},{20,16},{24,28},{28,24},{1,5},{5... | collective-permute-start | bytes 7077896 | tf_op jit(solution)/shard_map/ppermute | solution.py:635
  664.8 37.5 %collective-permute-start.41 = (bf16[256,1536]{1,0:T(8,128)(2,1)}, bf16[256,1536]{1,0:T(8,128)(2,1)}, u32[]{:S(2)}, u32[]{:S(2)}) collective-permute-start(bf16[256,1536]{1,0:T(8,128)(2,1)} %add_convert_fusion.4), channel_id=1, source_target_pairs={{0,2},{1,3},{2,0},{3,1},{4,6},{5,7},{6,4},{7,5},{8,10},{9,11},{10,... | collective-permute-start | bytes 2359304 | tf_op jit(solution)/shard_map/ppermute | solution.py:635
  715.1 110.4 %reduce-scatter.14.cloned.1.call-start = ((), (), s32[]{:S(2)}) async-start(), calls=%async_computation.13 | async-start | bytes 2211840 | tf_op jit(solution)/shard_map/reduce_scatter | solution.py:646
  739.3 40.2 %collective-permute-start.60 = (bf16[768,1152]{1,0:T(8,128)(2,1)}, bf16[768,1152]{1,0:T(8,128)(2,1)}, u32[]{:S(2)}, u32[]{:S(2)}) collective-permute-start(bf16[768,1152]{1,0:T(8,128)(2,1)} %get-tuple-element.301), channel_id=1, source_target_pairs={{0,4},{4,0},{8,12},{12,8},{16,20},{20,16},{24,28},{28,24},{1,5},{5... | collective-permute-start | bytes 5308424 | tf_op jit(solution)/shard_map/ppermute | solution.py:635
  752.8 35.4 %collective-permute-start.54 = (f32[6,1536]{1,0:T(8,128)}, f32[6,1536]{1,0:T(8,128)}, u32[]{:S(2)}, u32[]{:S(2)}) collective-permute-start(f32[6,1536]{1,0:T(8,128)} %stack.98), channel_id=1, source_target_pairs={{0,1},{1,0},{2,3},{3,2},{4,5},{5,4},{6,7},{7,6},{8,9},{9,8},{10,11... | collective-permute-start | bytes 110600 | tf_op jit(solution)/shard_map/ppermute | solution.py:672
  (102 other events, 1287.7 us)
Sparse Core Ops, SparseCore 0:
  10.8 69.6 all-gather.4
  83.2 78.3 all-gather.6
  163.8 136.1 all-gather.8
  302.1 79.6 all-gather.10
  433.9 48.1 reduce-scatter.5
  572.5 47.6 reduce-scatter.7
  647.1 47.4 reduce-scatter.9
  715.2 47.6 reduce-scatter.11
  785.6 39.9 reduce-scatter.13

commit v4 on v3

--- a/solution.py
+++ b/solution.py
@@ -749,7 +749,7 @@
             st = state[s]
             st["gate"], st["up"], st["hidden"] = gate_forward(st["normed3"], gu_full)
         third_lefts = [part[s] for s in range(seqs) for part in third_parts]
-        dn_pair = weight_grad(parity, third_lefts, [st["hidden"] for st in state], 384)
+        dn_pair = weight_grad(parity, third_lefts, [st["hidden"] for st in state], 512)
         last = dn_pair[1]
         for s in range(seqs):
             st = state[s]
@@ -761,8 +761,8 @@
         dn_sum = pair_sum(*dn_pair, last)
         dn_grad = line_sum(dn_sum)
         normed3 = [p for st in state for p in st["normed3"]]
-        gate_pair = weight_grad(parity, normed3, [after(st["dgate"], dn_sum) for st in state], 384)
-        up_pair = weight_grad(parity, normed3, [after(st["dup"], gate_pair[1]) for st in state], 384)
+        gate_pair = weight_grad(parity, normed3, [after(st["dgate"], dn_sum) for st in state], 512)
+        up_pair = weight_grad(parity, normed3, [after(st["dup"], gate_pair[1]) for st in state], 512)
 
         gain_grads, shift_grads = [0.0] * 3, [0.0] * 3
         last = up_pair[1]

time: 842 us -> 840 us (level)
  Pallas kernels: 397 us -> 387 us
    pallas_call x22, Pallas kernels: 397 us -> 387 us  [call(): pl.pallas_call(kernel, out_shape=outs, grid=grid, in_specs=in_specs, out_...]
  transfers between devices with their start and end apart: 70 -> 70, of which waited for: 27 -> 28; matrix products, arithmetic and copies ran while one was open for 12% -> 12% of each run, Pallas kernels for 48% -> 46%
where the time goes in v4:
time: 840 us; the launch traced here: 833 us
  Pallas kernels  387 us (46%)
  waiting for transfers between devices  258 us (31%)
  other arithmetic  76.9 us (9%)
  starting transfers between devices  50.7 us (6%)
  local copies, waits for them, and re-layouts  42.3 us (5%)
  between operations  14.9 us (2%)
    pallas_call x22, Pallas kernels, call(): pl.pallas_call(kernel, out_shape=outs, grid=grid, in_specs=in_specs, out_...  387 us
    ppermute x25, waiting for transfers between devices, in_turn(): turns[axis] = lax.ppermute(v, name, pairs_of)  148 us
    all_gather x3, waiting for transfers between devices, fetch_all(): return lax.all_gather(local, 'dp', axis=0, tiled=True)  76.8 us
    ppermute x25, starting transfers between devices, in_turn(): turns[axis] = lax.ppermute(v, name, pairs_of)  33.5 us
  transfers between devices with their start and end apart: 70, of which 28 were waited for; matrix products, arithmetic and copies ran while one was open for 12% of the time, Pallas kernels for 46%

profile of v4, /device:TPU:0, one launch (start us, length us, event | category | flops | bytes accessed | tf_op | source)
XLA Modules:
  0.0 832.7 jit_solution(4002244062123246737)
XLA Ops:
  33.2 13.6 %collective-permute-done.p1 = bf16[2,256,1536]{2,1,0:T(8,128)(2,1)} collective-permute-done((bf16[2,256,1536]{2,1,0:T(8,128)(2,1)}, bf16[2,256,1536]{2,1,0:T(8,128)(2,1)}, u32[]{:S(2)}, u32[]{:S(2)}) %collective-permute-start) | collective-permute-done | bytes 1572896 | tf_op jit(solution)/shard_map/ppermute | solution.py:635
  51.0 29.5 %all-gather.5.cloned.1.call-done.weight.w_ref = bf16[1536,1152]{1,0:T(8,128)(2,1)} async-done(((bf16[192,1152]{1,0:T(8,128)(2,1)}), bf16[1536,1152]{1,0:T(8,128)(2,1)}) %all-gather.5.cloned.1.call-update) | async-done | bytes 3538960 | tf_op jit(solution)/shard_map/all_gather | solution.py:639
  87.6 24.4 %shard_map.221 = (bf16[1024,1536]{1,0:T(8,128)(2,1)}, bf16[1024,384]{1,0:T(8,128)(2,1)}, bf16[1024,384]{1,0:T(8,128)(2,1)}, bf16[1024,384]{1,0:T(8,128)(2,1)}, b...) custom-call(bf16[2,256,1536]{2,1,0:T(8,128)(2,1)} %t.3, bf16[2,256,1536]{2,1,0:T(8,128)(2,1)} %collective-permute-done.p1, ...), custom_call_target="tpu_custom_call" | custom-call | flops 15703474176 | bytes 16000000 | tf_op jit(solution)/shard_map/pallas_call | solution.py:21
  120.6 23.4 %shard_map.222 = (bf16[1024,1536]{1,0:T(8,128)(2,1)}, bf16[1024,384]{1,0:T(8,128)(2,1)}, bf16[1024,384]{1,0:T(8,128)(2,1)}, bf16[1024,384]{1,0:T(8,128)(2,1)}, b...) custom-call(bf16[2,256,1536]{2,1,0:T(8,128)(2,1)} %t.3, bf16[2,256,1536]{2,1,0:T(8,128)(2,1)} %collective-permute-done.p1, ...), custom_call_target="tpu_custom_call" | custom-call | flops 15703474176 | bytes 16000000 | tf_op jit(solution)/shard_map/pallas_call | solution.py:21
  144.0 17.6 %all-gather.7.cloned.1.call-done.weight.o_ref = bf16[1536,1536]{1,0:T(8,128)(2,1)} async-done(((bf16[192,1536]{1,0:T(8,128)(2,1)}), bf16[1536,1536]{1,0:T(8,128)(2,1)}) %all-gather.7.cloned.1.call-update) | async-done | bytes 4718608 | tf_op jit(solution)/shard_map/all_gather | solution.py:639
  180.6 36.9 %collective-permute-done.10.w1 = bf16[1536,768]{1,0:T(8,128)(2,1)} collective-permute-done((bf16[1536,768]{1,0:T(8,128)(2,1)}, bf16[1536,768]{1,0:T(8,128)(2,1)}, u32[]{:S(2)}, u32[]{:S(2)}) %collective-permute-start.10) | collective-permute-done | bytes 2359328 | tf_op jit(solution)/shard_map/ppermute | solution.py:635
  226.4 8.8 %collective-permute-done.11 = bf16[2,2,130,384]{3,2,1,0:T(8,128)(2,1)S(1)} collective-permute-done((bf16[2,2,130,384]{3,2,1,0:T(8,128)(2,1)S(1)}, bf16[2,2,130,384]{3,2,1,0:T(8,128)(2,1)S(1)}, u32[]{:S(2)}, u32[]{:S(2)}) %collective-permute-start.11) | collective-permute-done | bytes 399392 | tf_op jit(solution)/shard_map/ppermute | solution.py:635
  240.2 13.7 %collective-permute-done.12.c = bf16[256,1536]{1,0:T(8,128)(2,1)S(1)} collective-permute-done((bf16[256,1536]{1,0:T(8,128)(2,1)S(1)}, bf16[256,1536]{1,0:T(8,128)(2,1)S(1)}, u32[]{:S(2)}, u32[]{:S(2)}) %collective-permute-start.12) | collective-permute-done | bytes 786464 | tf_op jit(solution)/shard_map/ppermute | solution.py:635
  255.4 14.6 %shard_map.224 = (f32[256,1536]{1,0:T(8,128)}, f32[256,1536]{1,0:T(8,128)}, bf16[256,1536]{1,0:T(8,128)(2,1)}, bf16[256,1536]{1,0:T(8,128)(2,1)}, bf16[256,1536]...) custom-call(bf16[2,256,1536]{2,1,0:T(8,128)(2,1)} %t.3, bf16[512,1536]{1,0:T(8,128)(2,1)} %get-tuple-element.167.a, ...), custom_call_target="tpu_custom_call" | custom-call | flops 8455716864 | bytes 18000000 | tf_op jit(solution)/shard_map/pallas_call | solution.py:21
  273.4 14.9 %shard_map.227 = (f32[256,1536]{1,0:T(8,128)}, f32[256,1536]{1,0:T(8,128)}, bf16[256,1536]{1,0:T(8,128)(2,1)}, bf16[256,1536]{1,0:T(8,128)(2,1)}, bf16[256,1536]...) custom-call(bf16[2,256,1536]{2,1,0:T(8,128)(2,1)} %t.3, bf16[512,1536]{1,0:T(8,128)(2,1)} %get-tuple-element.182.a, ...), custom_call_target="tpu_custom_call" | custom-call | flops 8455716864 | bytes 18000000 | tf_op jit(solution)/shard_map/pallas_call | solution.py:21
  292.5 7.6 all-gather.9.cloned.1.call-done.wg.wu
  307.8 14.9 %shard_map.226 = (bf16[1024,1536]{1,0:T(8,128)(2,1)}, bf16[1024,1536]{1,0:T(8,128)(2,1)}, bf16[1024,1536]{1,0:T(8,128)(2,1)}) custom-call(bf16[256,1536]{1,0:T(8,128)(2,1)} %get-tuple-element.178.p0.refs_0_, bf16[256,1536]{1,0:T(8,128)(2,1)} %collective-permute-done.19.p1.refs_1_, bf16[256,1536]{1,0:T(8,128)(2,1)} %collective-permute-done.20.p2.refs_2_, ...), custom_call_target="tpu_custom_call" | custom-call | flops 28991029248 | bytes 22000000 | tf_op jit(solution)/shard_map/pallas_call | solution.py:21
  324.6 14.7 %shard_map.228 = (bf16[1024,1536]{1,0:T(8,128)(2,1)}, bf16[1024,1536]{1,0:T(8,128)(2,1)}, bf16[1024,1536]{1,0:T(8,128)(2,1)}) custom-call(bf16[256,1536]{1,0:T(8,128)(2,1)} %get-tuple-element.184.p0.refs_4_, bf16[256,1536]{1,0:T(8,128)(2,1)} %collective-permute-done.24.p1.refs_5_, bf16[256,1536]{1,0:T(8,128)(2,1)} %copy-done.54, ...), custom_call_target="tpu_custom_call" | custom-call | flops 28991029248 | bytes 22000000 | tf_op jit(solution)/shard_map/pallas_call | solution.py:21
  339.4 15.8 %shard_map.229 = (bf16[768,1536]{1,0:T(8,128)(2,1)}, bf16[768,1536]{1,0:T(8,128)(2,1)}) custom-call(s32[1]{0:T(128)} %bitcast.19.par, bf16[256,1536]{1,0:T(8,128)(2,1)} %get-tuple-element.362.refs_0_, bf16[256,1536]{1,0:T(8,128)(2,1)} %get-tuple-element.360.refs_1_, bf16[256,1536]{1,0:T(8,128)(2,1)} %get-tuple-element.358.refs_2_, ...), custom_call_target="tpu_custom_call" | custom-call | flops 28991029248 | bytes 17301504 | tf_op jit(solution)/shard_map/pallas_call | solution.py:21
  355.5 29.7 %all-gather.11.cloned.1.call-done.wd.weight = bf16[1536,1536]{1,0:T(8,128)(2,1)} async-done(((bf16[192,1536]{1,0:T(8,128)(2,1)}), bf16[1536,1536]{1,0:T(8,128)(2,1)}) %all-gather.11.cloned.1.call-update) | async-done | bytes 4718608 | tf_op jit(solution)/shard_map/all_gather | solution.py:639
  385.1 24.9 %shard_map.230 = (bf16[1024,1536]{1,0:T(8,128)(2,1)}, bf16[1024,1536]{1,0:T(8,128)(2,1)}, bf16[512,1536]{1,0:T(8,128)(2,1)}, bf16[512,1536]{1,0:T(8,128)(2,1)}) custom-call(bf16[2,256,1536]{2,1,0:T(8,128)(2,1)} %copy-done.3, bf16[2,256,1536]{2,1,0:T(8,128)(2,1)} %copy-done.20, bf16[2,256,1536]{2,1,0:T(8,128)(2,1)} %collective-permute-done.22.p2, ...), custom_call_target="tpu_custom_call" | custom-call | flops 43486543872 | bytes 33000000 | tf_op jit(solution)/shard_map/pallas_call | solution.py:21
  410.1 25.0 %shard_map.231 = (bf16[1024,1536]{1,0:T(8,128)(2,1)}, bf16[1024,1536]{1,0:T(8,128)(2,1)}, bf16[512,1536]{1,0:T(8,128)(2,1)}, bf16[512,1536]{1,0:T(8,128)(2,1)}) custom-call(bf16[2,256,1536]{2,1,0:T(8,128)(2,1)} %copy-done.3, bf16[2,256,1536]{2,1,0:T(8,128)(2,1)} %copy-done.20, bf16[2,256,1536]{2,1,0:T(8,128)(2,1)} %collective-permute-done.22.p2, ...), custom_call_target="tpu_custom_call" | custom-call | flops 43486543872 | bytes 33000000 | tf_op jit(solution)/shard_map/pallas_call | solution.py:21
  437.3 16.1 %shard_map.232 = (bf16[768,1536]{1,0:T(8,128)(2,1)}, bf16[768,1536]{1,0:T(8,128)(2,1)}) custom-call(s32[1]{0:T(128)} %bitcast.19.par, bf16[256,1536]{1,0:T(8,128)(2,1)} %get-tuple-element.178.p0.refs_0_, bf16[256,1536]{1,0:T(8,128)(2,1)} %collective-permute-done.19.p1.refs_1_, bf16[256,1536]{1,0:T(8,128)(2,1)} %collective-permute-done.20.p2.refs_2_, ...), custom_call_target="tpu_custom_call" | custom-call | flops 28991029248 | bytes 17301504 | tf_op jit(solution)/shard_map/pallas_call | solution.py:21
  458.0 16.3 %shard_map.233 = (bf16[768,1536]{1,0:T(8,128)(2,1)}, bf16[768,1536]{1,0:T(8,128)(2,1)}) custom-call(s32[1]{0:T(128)} %bitcast.19.par, bf16[256,1536]{1,0:T(8,128)(2,1)} %get-tuple-element.178.p0.refs_0_, bf16[256,1536]{1,0:T(8,128)(2,1)} %collective-permute-done.19.p1.refs_1_, bf16[256,1536]{1,0:T(8,128)(2,1)} %collective-permute-done.20.p2.refs_2_, ...), custom_call_target="tpu_custom_call" | custom-call | flops 28991029248 | bytes 17301504 | tf_op jit(solution)/shard_map/pallas_call | solution.py:21
  477.9 24.1 %shard_map.234 = (f32[256,1536]{1,0:T(8,128)}, bf16[256,1536]{1,0:T(8,128)(2,1)}, bf16[256,1536]{1,0:T(8,128)(2,1)}, bf16[256,1536]{1,0:T(8,128)(2,1)}, bf16[4,2...) custom-call(bf16[2,256,1536]{2,1,0:T(8,128)(2,1)} %copy-done.3, bf16[512,1536]{1,0:T(8,128)(2,1)} %get-tuple-element.192.a, ...), custom_call_target="tpu_custom_call" | custom-call | flops 10267656192 | bytes 24000000 | tf_op jit(solution)/shard_map/pallas_call | solution.py:21
  504.6 24.2 %shard_map.235 = (f32[256,1536]{1,0:T(8,128)}, bf16[256,1536]{1,0:T(8,128)(2,1)}, bf16[256,1536]{1,0:T(8,128)(2,1)}, bf16[256,1536]{1,0:T(8,128)(2,1)}, bf16[4,2...) custom-call(bf16[2,256,1536]{2,1,0:T(8,128)(2,1)} %copy-done.3, bf16[512,1536]{1,0:T(8,128)(2,1)} %get-tuple-element.195.a, ...), custom_call_target="tpu_custom_call" | custom-call | flops 10267656192 | bytes 24000000 | tf_op jit(solution)/shard_map/pallas_call | solution.py:21
  537.1 11.0 %shard_map.236 = (bf16[2,768,768]{2,1,0:T(8,128)(2,1)}, bf16[2,768,768]{2,1,0:T(8,128)(2,1)}, bf16[2,768,768]{2,1,0:T(8,128)(2,1)}, bf16[2,768,768]{2,1,0:T(8,128)(2,1)}) custom-call(s32[1]{0:T(128)} %bitcast.19.par, bf16[256,1536]{1,0:T(8,128)(2,1)} %get-tuple-element.226.refs_0_, bf16[256,1536]{1,0:T(8,128)(2,1)} %get-tuple-element.228.refs_1_, ...), custom_call_target="tpu_custom_call" | custom-call | flops 14495514624 | bytes 16000000 | tf_op jit(solution)/shard_map/pallas_call | solution.py:21
  548.1 9.9 %shard_map.237 = (bf16[512,1536]{1,0:T(8,128)(2,1)}, bf16[512,1536]{1,0:T(8,128)(2,1)}) custom-call(bf16[1024,1536]{1,0:T(8,128)(2,1)} %get-tuple-element.234.refs_8_.a, bf16[1536,1536]{1,0:T(8,128)(2,1)} %all-gather.11.cloned.1.call-done.wd.weight), custom_call_target="tpu_custom_call" | custom-call | flops 14495514624 | bytes 11010048 | tf_op jit(solution)/shard_map/pallas_call | solution.py:21
  558.6 9.5 %shard_map.238 = (bf16[512,1536]{1,0:T(8,128)(2,1)}, bf16[512,1536]{1,0:T(8,128)(2,1)}) custom-call(bf16[1024,1536]{1,0:T(8,128)(2,1)} %get-tuple-element.245.refs_9_.a, bf16[1536,1536]{1,0:T(8,128)(2,1)} %all-gather.11.cloned.1.call-done.wd.weight), custom_call_target="tpu_custom_call" | custom-call | flops 14495514624 | bytes 11010048 | tf_op jit(solution)/shard_map/pallas_call | solution.py:21
  579.6 11.1 %collective-permute-done.37 = bf16[2,2,256,384]{3,2,1,0:T(8,128)(2,1)S(1)} collective-permute-done((bf16[2,2,256,384]{3,2,1,0:T(8,128)(2,1)}, bf16[2,2,256,384]{3,2,1,0:T(8,128)(2,1)S(1)}, u32[]{:S(2)}, u32[]{:S(2)}) %collective-permute-start.37) | collective-permute-done | bytes 786464 | tf_op jit(solution)/shard_map/ppermute | solution.py:635
  591.5 35.0 %shard_map.239 = (bf16[1024,1152]{1,0:T(8,128)(2,1)}, bf16[512,1536]{1,0:T(8,128)(2,1)}, bf16[512,1536]{1,0:T(8,128)(2,1)}) custom-call(bf16[256,1536]{1,0:T(8,128)(2,1)} %get-tuple-element.225.p0.refs_0_, bf16[256,1536]{1,0:T(8,128)(2,1)} %collective-permute-done.32.p1.refs_1_, bf16[256,1536]{1,0:T(8,128)(2,1)} %collective-permute-done.42.p2.refs_2_, ...), custom_call_target="tpu_custom_call" | custom-call | flops 26575110144 | bytes 24000000 | tf_op jit(solution)/shard_map/pallas_call | solution.py:21
  644.7 7.9 shard_map.240
  663.7 35.2 %shard_map.241 = (bf16[1024,1152]{1,0:T(8,128)(2,1)}, bf16[512,1536]{1,0:T(8,128)(2,1)}, bf16[512,1536]{1,0:T(8,128)(2,1)}) custom-call(bf16[256,1536]{1,0:T(8,128)(2,1)} %get-tuple-element.241.refs_4_.p0, bf16[256,1536]{1,0:T(8,128)(2,1)} %collective-permute-done.36.refs_5_.p1, bf16[256,1536]{1,0:T(8,128)(2,1)} %collective-permute-done.45.refs_6_.p2, ...), custom_call_target="tpu_custom_call" | custom-call | flops 26575110144 | bytes 24000000 | tf_op jit(solution)/shard_map/pallas_call | solution.py:21
  701.2 9.8 %collective-permute-done.59 = bf16[768,1536]{1,0:T(8,128)(2,1)S(1)} collective-permute-done((bf16[768,1536]{1,0:T(8,128)(2,1)}, bf16[768,1536]{1,0:T(8,128)(2,1)S(1)}, u32[]{:S(2)}, u32[]{:S(2)}) %collective-permute-start.59) | collective-permute-done | bytes 2359328 | tf_op jit(solution)/shard_map/ppermute | solution.py:635
  721.3 15.8 %shard_map.242 = (bf16[768,1152]{1,0:T(8,128)(2,1)}, bf16[768,1152]{1,0:T(8,128)(2,1)}) custom-call(s32[1]{0:T(128)} %bitcast.19.par, bf16[1024,1536]{1,0:T(8,128)(2,1)} %get-tuple-element.259.refs_0_, bf16[1024,1536]{1,0:T(8,128)(2,1)} %get-tuple-element.260.refs_1_, bf16[1024,1152]{1,0:T(8,128)(2,1)} %get-tuple-element.268.refs_2_, ...), custom_call_target="tpu_custom_call" | custom-call | flops 21743271936 | bytes 14548992 | tf_op jit(solution)/shard_map/pallas_call | solution.py:21
  750.5 26.8 %collective-permute-done.60 = bf16[768,1152]{1,0:T(8,128)(2,1)} collective-permute-done((bf16[768,1152]{1,0:T(8,128)(2,1)}, bf16[768,1152]{1,0:T(8,128)(2,1)}, u32[]{:S(2)}, u32[]{:S(2)}) %collective-permute-start.60) | collective-permute-done | bytes 1769504 | tf_op jit(solution)/shard_map/ppermute | solution.py:635
  813.3 10.3 %reduce-scatter.14.cloned.1.call-done = bf16[192,1152]{1,0:T(8,128)(2,1)} async-done(((bf16[768,1152]{1,0:T(8,128)(2,1)}), bf16[192,1152]{1,0:T(8,128)(2,1)}) %reduce-scatter.14.cloned.1.call-update) | async-done | bytes 442384 | tf_op jit(solution)/shard_map/reduce_scatter | solution.py:646
  (370 shorter events, 224.6 us)
Async XLA Ops:
  7.2 73.2 %all-gather.5.cloned.1.call-start = ((), (), s32[]{:S(2)}) async-start(), calls=%async_computation.5 | async-start | bytes 3981312 | tf_op jit(solution)/shard_map/all_gather | solution.py:639
  9.1 152.5 %all-gather.7.cloned.1.call-start = ((), (), s32[]{:S(2)}) async-start(), calls=%async_computation.6 | async-start | bytes 5308416 | tf_op jit(solution)/shard_map/all_gather | solution.py:639
  9.1 37.7 %collective-permute-start = (bf16[2,256,1536]{2,1,0:T(8,128)(2,1)}, bf16[2,256,1536]{2,1,0:T(8,128)(2,1)}, u32[]{:S(2)}, u32[]{:S(2)}) collective-permute-start(bf16[2,256,1536]{2,1,0:T(8,128)(2,1)} %t.3), channel_id=1, source_target_pairs={{0,2},{1,3},{2,0},{3,1},{4,6},{5,7},{6,4},{7,5},{8,10},{9,11},{10,... | collective-permute-start | bytes 4718600 | tf_op jit(solution)/shard_map/ppermute | solution.py:635
  80.5 219.6 %all-gather.9.cloned.1.call-start = ((), (), s32[]{:S(2)}) async-start(), calls=%async_computation.7 | async-start | bytes 10616832 | tf_op jit(solution)/shard_map/all_gather | solution.py:724
  82.9 36.4 %collective-permute-start.8 = (bf16[2,256,1536]{2,1,0:T(8,128)(2,1)S(1)}, bf16[2,256,1536]{2,1,0:T(8,128)(2,1)S(1)}, u32[]{:S(2)}, u32[]{:S(2)}) collective-permute-start(bf16[2,256,1536]{2,1,0:T(8,128)(2,1)S(1)} %multiply_convert_fusion.p0.t), channel_id=1, source_target_pairs={{0,2},{1,3},{2,0},{3,1},{4,6},{5,7},{6,4},{7,5},{8,10},{9,11},{10,... | collective-permute-start | bytes 4718600 | tf_op jit(solution)/shard_map/ppermute | solution.py:635
  161.6 223.5 %all-gather.11.cloned.1.call-start = ((), (), s32[]{:S(2)}) async-start(), calls=%async_computation.8 | async-start | bytes 5308416 | tf_op jit(solution)/shard_map/all_gather | solution.py:639
  165.2 52.3 %collective-permute-start.10 = (bf16[1536,768]{1,0:T(8,128)(2,1)}, bf16[1536,768]{1,0:T(8,128)(2,1)}, u32[]{:S(2)}, u32[]{:S(2)}) collective-permute-start(bf16[1536,768]{1,0:T(8,128)(2,1)} %slice.218.w0), channel_id=1, source_target_pairs={{0,2},{1,3},{2,0},{3,1},{4,6},{5,7},{6,4},{7,5},{8,10},{9,11},{10,... | collective-permute-start | bytes 7077896 | tf_op jit(solution)/shard_map/ppermute | solution.py:635
  166.7 50.8 %collective-permute-start.22 = (bf16[2,256,1536]{2,1,0:T(8,128)(2,1)S(1)}, bf16[2,256,1536]{2,1,0:T(8,128)(2,1)}, u32[]{:S(2)}, u32[]{:S(2)}) collective-permute-start(bf16[2,256,1536]{2,1,0:T(8,128)(2,1)S(1)} %multiply_convert_fusion.p0.t), channel_id=1, source_target_pairs={{0,1},{1,0},{2,3},{3,2},{4,5},{5,4},{6,7},{7,6},{8,9},{9,8},{10,11... | collective-permute-start | bytes 4718600 | tf_op jit(solution)/shard_map/ppermute | solution.py:649
  173.5 50.0 %collective-permute-start.9 = (bf16[512,1536]{1,0:T(8,128)(2,1)}, bf16[512,1536]{1,0:T(8,128)(2,1)}, u32[]{:S(2)}, u32[]{:S(2)}) collective-permute-start(bf16[512,1536]{1,0:T(8,128)(2,1)} %get-tuple-element.168), channel_id=1, source_target_pairs={{0,1},{1,0},{2,3},{3,2},{4,5},{5,4},{6,7},{7,6},{8,9},{9,8},{10,11... | collective-permute-start | bytes 4718600 | tf_op jit(solution)/shard_map/ppermute | solution.py:649
  178.9 57.7 %collective-permute-start.17 = (bf16[512,1536]{1,0:T(8,128)(2,1)}, bf16[512,1536]{1,0:T(8,128)(2,1)S(1)}, u32[]{:S(2)}, u32[]{:S(2)}) collective-permute-start(bf16[512,1536]{1,0:T(8,128)(2,1)} %get-tuple-element.176), channel_id=1, source_target_pairs={{0,1},{1,0},{2,3},{3,2},{4,5},{5,4},{6,7},{7,6},{8,9},{9,8},{10,11... | collective-permute-start | bytes 4718600 | tf_op jit(solution)/shard_map/ppermute | solution.py:649
  180.1 75.4 %collective-permute-start.13 = (bf16[1536,768]{1,0:T(8,128)(2,1)}, bf16[1536,768]{1,0:T(8,128)(2,1)}, u32[]{:S(2)}, u32[]{:S(2)}) collective-permute-start(bf16[1536,768]{1,0:T(8,128)(2,1)} %slice.218.w0), channel_id=1, source_target_pairs={{0,1},{1,0},{2,3},{3,2},{4,5},{5,4},{6,7},{7,6},{8,9},{9,8},{10,11... | collective-permute-start | bytes 7077896 | tf_op jit(solution)/shard_map/ppermute | solution.py:649
  217.5 37.9 %collective-permute-start.14 = (bf16[1536,768]{1,0:T(8,128)(2,1)}, bf16[1536,768]{1,0:T(8,128)(2,1)}, u32[]{:S(2)}, u32[]{:S(2)}) collective-permute-start(bf16[1536,768]{1,0:T(8,128)(2,1)} %collective-permute-done.10.w1), channel_id=1, source_target_pairs={{0,1},{1,0},{2,3},{3,2},{4,5},{5,4},{6,7},{7,6},{8,9},{9,8},{10,11... | collective-permute-start | bytes 7077896 | tf_op jit(solution)/shard_map/ppermute | solution.py:649
  237.8 62.3 %collective-permute-start.23 = (bf16[2,256,1536]{2,1,0:T(8,128)(2,1)S(1)}, bf16[2,256,1536]{2,1,0:T(8,128)(2,1)S(1)}, u32[]{:S(2)}, u32[]{:S(2)}) collective-permute-start(bf16[2,256,1536]{2,1,0:T(8,128)(2,1)S(1)} %copy-done.21), channel_id=1, source_target_pairs={{0,1},{1,0},{2,3},{3,2},{4,5},{5,4},{6,7},{7,6},{8,9},{9,8},{10,11... | collective-permute-start | bytes 4718600 | tf_op jit(solution)/shard_map/ppermute | solution.py:649
  270.1 37.8 %collective-permute-start.20 = (bf16[256,1536]{1,0:T(8,128)(2,1)}, bf16[256,1536]{1,0:T(8,128)(2,1)}, u32[]{:S(2)}, u32[]{:S(2)}) collective-permute-start(bf16[256,1536]{1,0:T(8,128)(2,1)} %get-tuple-element.178.p0.refs_0_), channel_id=1, source_target_pairs={{0,1},{1,0},{2,3},{3,2},{4,5},{5,4},{6,7},{7,6},{8,9},{9,8},{10,11... | collective-permute-start | bytes 2359304 | tf_op jit(solution)/shard_map/ppermute | solution.py:649
  300.1 270.3 %reduce-scatter.6.cloned.1.call-start = ((), (), s32[]{:S(2)}) async-start(), calls=%async_computation.9 | async-start | bytes 2949120 | tf_op jit(solution)/shard_map/reduce_scatter | solution.py:646
  355.1 80.0 %collective-permute-start.31 = (bf16[768,1536]{1,0:T(8,128)(2,1)}, bf16[768,1536]{1,0:T(8,128)(2,1)S(1)}, u32[]{:S(2)}, u32[]{:S(2)}) collective-permute-start(bf16[768,1536]{1,0:T(8,128)(2,1)} %get-tuple-element.188), channel_id=1, source_target_pairs={{0,4},{4,0},{8,12},{12,8},{16,20},{20,16},{24,28},{28,24},{1,5},{5... | collective-permute-start | bytes 7077896 | tf_op jit(solution)/shard_map/ppermute | solution.py:635
  437.2 207.4 %reduce-scatter.8.cloned.1.call-start = ((), (), s32[]{:S(2)}) async-start(), calls=%async_computation.10 | async-start | bytes 2949120 | tf_op jit(solution)/shard_map/reduce_scatter | solution.py:646
  453.4 78.3 %collective-permute-start.44 = (bf16[768,1536]{1,0:T(8,128)(2,1)}, bf16[768,1536]{1,0:T(8,128)(2,1)S(1)}, u32[]{:S(2)}, u32[]{:S(2)}) collective-permute-start(bf16[768,1536]{1,0:T(8,128)(2,1)} %get-tuple-element.252), channel_id=1, source_target_pairs={{0,4},{4,0},{8,12},{12,8},{16,20},{20,16},{24,28},{28,24},{1,5},{5... | collective-permute-start | bytes 7077896 | tf_op jit(solution)/shard_map/ppermute | solution.py:635
  502.0 68.4 %collective-permute-start.42 = (bf16[256,1536]{1,0:T(8,128)(2,1)}, bf16[256,1536]{1,0:T(8,128)(2,1)}, u32[]{:S(2)}, u32[]{:S(2)}) collective-permute-start(bf16[256,1536]{1,0:T(8,128)(2,1)} %get-tuple-element.225.p0.refs_0_), channel_id=1, source_target_pairs={{0,1},{1,0},{2,3},{3,2},{4,5},{5,4},{6,7},{7,6},{8,9},{9,8},{10,11... | collective-permute-start | bytes 2359304 | tf_op jit(solution)/shard_map/ppermute | solution.py:649
  528.8 44.9 %collective-permute-start.45 = (bf16[256,1536]{1,0:T(8,128)(2,1)}, bf16[256,1536]{1,0:T(8,128)(2,1)}, u32[]{:S(2)}, u32[]{:S(2)}) collective-permute-start(bf16[256,1536]{1,0:T(8,128)(2,1)} %get-tuple-element.241.refs_4_.p0), channel_id=1, source_target_pairs={{0,1},{1,0},{2,3},{3,2},{4,5},{5,4},{6,7},{7,6},{8,9},{9,8},{10,11... | collective-permute-start | bytes 2359304 | tf_op jit(solution)/shard_map/ppermute | solution.py:649
  570.4 142.7 %reduce-scatter.10.cloned.1.call-start = ((), (), s32[]{:S(2)}) async-start(), calls=%async_computation.11 | async-start | bytes 2949120 | tf_op jit(solution)/shard_map/reduce_scatter | solution.py:646
  573.7 56.7 %collective-permute-start.47 = (bf16[768,1536]{1,0:T(8,128)(2,1)}, bf16[768,1536]{1,0:T(8,128)(2,1)}, u32[]{:S(2)}, u32[]{:S(2)}) collective-permute-start(bf16[768,1536]{1,0:T(8,128)(2,1)} %get-tuple-element.264), channel_id=1, source_target_pairs={{0,4},{4,0},{8,12},{12,8},{16,20},{20,16},{24,28},{28,24},{1,5},{5... | collective-permute-start | bytes 7077896 | tf_op jit(solution)/shard_map/ppermute | solution.py:635
  575.2 51.3 %collective-permute-start.49 = (bf16[2,2,256,384]{3,2,1,0:T(8,128)(2,1)S(1)}, bf16[2,2,256,384]{3,2,1,0:T(8,128)(2,1)S(1)}, u32[]{:S(2)}, u32[]{:S(2)}) collective-permute-start(bf16[2,2,256,384]{3,2,1,0:T(8,128)(2,1)S(1)} %pad_maximum_fusion.6), channel_id=1, source_target_pairs={{0,1},{1,0},{2,3},{3,2},{4,5},{5,4},{6,7},{7,6},{8,9},{9,8},{10,11... | collective-permute-start | bytes 2359304 | tf_op jit(solution)/shard_map/ppermute | solution.py:649
  575.2 61.4 %collective-permute-start.33 = (bf16[512,1536]{1,0:T(8,128)(2,1)}, bf16[512,1536]{1,0:T(8,128)(2,1)}, u32[]{:S(2)}, u32[]{:S(2)}) collective-permute-start(bf16[512,1536]{1,0:T(8,128)(2,1)} %get-tuple-element.236), channel_id=1, source_target_pairs={{0,1},{1,0},{2,3},{3,2},{4,5},{5,4},{6,7},{7,6},{8,9},{9,8},{10,11... | collective-permute-start | bytes 4718600 | tf_op jit(solution)/shard_map/ppermute | solution.py:649
  575.8 63.5 %collective-permute-start.40 = (bf16[512,1536]{1,0:T(8,128)(2,1)}, bf16[512,1536]{1,0:T(8,128)(2,1)}, u32[]{:S(2)}, u32[]{:S(2)}) collective-permute-start(bf16[512,1536]{1,0:T(8,128)(2,1)} %get-tuple-element.247), channel_id=1, source_target_pairs={{0,1},{1,0},{2,3},{3,2},{4,5},{5,4},{6,7},{7,6},{8,9},{9,8},{10,11... | collective-permute-start | bytes 4718600 | tf_op jit(solution)/shard_map/ppermute | solution.py:649
  590.6 53.2 %collective-permute-start.38 = (bf16[2,768,768]{2,1,0:T(8,128)(2,1)}, bf16[2,768,768]{2,1,0:T(8,128)(2,1)}, u32[]{:S(2)}, u32[]{:S(2)}) collective-permute-start(bf16[2,768,768]{2,1,0:T(8,128)(2,1)} %add_convert_fusion.1), channel_id=1, source_target_pairs={{0,2},{1,3},{2,0},{3,1},{4,6},{5,7},{6,4},{7,5},{8,10},{9,11},{10,... | collective-permute-start | bytes 7077896 | tf_op jit(solution)/shard_map/ppermute | solution.py:635
  644.6 136.3 %reduce-scatter.12.cloned.1.call-start = ((), (), s32[]{:S(2)}) async-start(), calls=%async_computation.12 | async-start | bytes 2949120 | tf_op jit(solution)/shard_map/reduce_scatter | solution.py:646
  658.5 52.6 %collective-permute-start.59 = (bf16[768,1536]{1,0:T(8,128)(2,1)}, bf16[768,1536]{1,0:T(8,128)(2,1)S(1)}, u32[]{:S(2)}, u32[]{:S(2)}) collective-permute-start(bf16[768,1536]{1,0:T(8,128)(2,1)} %pad_maximum_fusion.2), channel_id=1, source_target_pairs={{0,4},{4,0},{8,12},{12,8},{16,20},{20,16},{24,28},{28,24},{1,5},{5... | collective-permute-start | bytes 7077896 | tf_op jit(solution)/shard_map/ppermute | solution.py:635
  662.6 37.7 %collective-permute-start.41 = (bf16[256,1536]{1,0:T(8,128)(2,1)}, bf16[256,1536]{1,0:T(8,128)(2,1)}, u32[]{:S(2)}, u32[]{:S(2)}) collective-permute-start(bf16[256,1536]{1,0:T(8,128)(2,1)} %add_convert_fusion.4), channel_id=1, source_target_pairs={{0,2},{1,3},{2,0},{3,1},{4,6},{5,7},{6,4},{7,5},{8,10},{9,11},{10,... | collective-permute-start | bytes 2359304 | tf_op jit(solution)/shard_map/ppermute | solution.py:635
  713.1 110.5 %reduce-scatter.14.cloned.1.call-start = ((), (), s32[]{:S(2)}) async-start(), calls=%async_computation.13 | async-start | bytes 2211840 | tf_op jit(solution)/shard_map/reduce_scatter | solution.py:646
  737.1 40.2 %collective-permute-start.60 = (bf16[768,1152]{1,0:T(8,128)(2,1)}, bf16[768,1152]{1,0:T(8,128)(2,1)}, u32[]{:S(2)}, u32[]{:S(2)}) collective-permute-start(bf16[768,1152]{1,0:T(8,128)(2,1)} %get-tuple-element.301), channel_id=1, source_target_pairs={{0,4},{4,0},{8,12},{12,8},{16,20},{20,16},{24,28},{28,24},{1,5},{5... | collective-permute-start | bytes 5308424 | tf_op jit(solution)/shard_map/ppermute | solution.py:635
  750.5 35.5 %collective-permute-start.54 = (f32[6,1536]{1,0:T(8,128)}, f32[6,1536]{1,0:T(8,128)}, u32[]{:S(2)}, u32[]{:S(2)}) collective-permute-start(f32[6,1536]{1,0:T(8,128)} %stack.98), channel_id=1, source_target_pairs={{0,1},{1,0},{2,3},{3,2},{4,5},{5,4},{6,7},{7,6},{8,9},{9,8},{10,11... | collective-permute-start | bytes 110600 | tf_op jit(solution)/shard_map/ppermute | solution.py:672
  (102 other events, 1270.9 us)
Sparse Core Ops, SparseCore 0:
  10.8 69.6 all-gather.4
  83.2 78.3 all-gather.6
  163.8 136.1 all-gather.8
  302.1 83.0 all-gather.10
  437.3 48.1 reduce-scatter.5
  570.5 47.5 reduce-scatter.7
  644.7 47.8 reduce-scatter.9
  713.2 47.4 reduce-scatter.11
  783.4 40.1 reduce-scatter.13
